TPU v7x, 128 devices: a whole 4x4x4 slice. The times are simulated.
128 devices in a mesh: row: 8 (over x, y_hi), col: 16 (over z, y_lo, core).
Axes of the slice: x: 4, y: 4 (y_hi: 2, y_lo: 2; y = y_hi * 2 + y_lo), z: 4, core: 2. Of those that a mesh axis runs over, the one named last changes fastest.
Arguments:
- amplitudes: bfloat16 [240, 240, 1024], P('row', None, 'col'), may hold values from -6 to 6
- pp_integrals: bfloat16 [1024, 1024], P('row', 'col'), may hold values from -0.1875 to 0.1875
- cycle_integrals: bfloat16 [240, 32, 7680], P('row', None, 'col'), may hold values from -0.0625 to 0.0625
- occ_map: int32 [8, 8], replicated, may hold values 0 or 1
- vir_map: int32 [16, 16], replicated, may hold values 0 or 1
Outputs:
- ladder: bfloat16 [240, 240, 1024], P('row', None, 'col')
- cycle_out: bfloat16 [240, 32, 7680], P('row', None, 'col')
All inputs are finite; a program needn't handle non-finite values.
Results may differ from a plain program's by a relative error of at most 0.001.
Values may be sent and summed in bfloat16 or wider, within the bound.
No kernel may reach another device: no remote copies, remote signals or barrier semaphores. Data moves between devices by JAX's collectives and lax.ppermute only.
A program may use at most 128 MiB of HBM per device.

v0:
```python
import jax
import jax.numpy as jnp
from jax import lax
from jax.sharding import PartitionSpec as P

VA_DEV = 2
OTILES = 8


def on_device(amplitudes, pp_integrals, cycle_integrals, occ_map, vir_map):
    row_count, occ_count, pair_width = amplitudes.shape
    virt_count = pair_width // VA_DEV
    tile_size = occ_count // OTILES
    occ_full = jnp.repeat(jnp.repeat(occ_map, tile_size, axis=0), tile_size, axis=1)
    occ_rows = lax.dynamic_slice_in_dim(occ_full, lax.axis_index("row") * row_count, row_count, 0)
    vir_full = jnp.repeat(jnp.repeat(vir_map, VA_DEV, axis=0), VA_DEV, axis=1)
    vir_rows = lax.dynamic_slice_in_dim(
        vir_full, lax.axis_index("col") * VA_DEV, VA_DEV, 0
    ).reshape(pair_width)
    mask = (occ_rows[:, :, None] * vir_rows[None, None, :]).astype(jnp.bfloat16)
    masked = amplitudes * mask
    pp_panel = lax.all_gather(pp_integrals, "row", axis=0, tiled=True)
    cycle_panel = lax.all_gather(cycle_integrals, "row", axis=0, tiled=True)
    piece = lax.all_gather(masked, "col", axis=2, tiled=True)
    width = piece.shape[2]
    flat_piece = piece.reshape(row_count * occ_count, width)
    ladder_total = jnp.dot(flat_piece, pp_panel, preferred_element_type=jnp.float32)
    a_count = width // virt_count
    piece_four = piece.reshape(row_count, occ_count, a_count, virt_count)
    contrib = jnp.einsum(
        "ikac,kcm->iam", piece_four, cycle_panel, preferred_element_type=jnp.float32
    )
    ladder = ladder_total.astype(jnp.bfloat16).reshape(row_count, occ_count, pair_width)
    cycle_out = contrib.astype(jnp.bfloat16)
    return (ladder, cycle_out)


def solution(mesh):
    in_specs = (P("row", None, "col"), P("row", "col"), P("row", None, "col"), P(), P())
    out_specs = (P("row", None, "col"), P("row", None, "col"))
    return jax.shard_map(
        on_device, mesh=mesh, in_specs=in_specs, out_specs=out_specs, check_vma=False
    )
```

profile of v0, /device:TPU:0, one launch (start us, length us, event | category | flops | bytes accessed | tf_op | source)
XLA Modules:
  0.0 265.7 jit_solution(12532979941312612831)
XLA Ops:
  7.2 0.0 all-gather.3.cloned.1.call-start
  7.2 0.8 copy.27
  8.0 0.1 broadcast_in_dim.13
  8.0 0.1 reshape.27
  8.2 0.1 constant_dynamic-slice_fusion.1
  8.3 0.1 copy.28
  8.4 0.7 broadcast_in_dim.15
  9.1 0.1 copy.29
  9.2 0.1 constant_dynamic-slice_fusion
  9.3 0.1 copy.30
  9.3 0.1 mul.27
  9.4 2.6 fusion.8
  12.0 0.0 all-gather.3.cloned.1.call-update
  12.0 0.0 all-gather.5.cloned.1.call-start
  12.1 0.7 all-gather.5.cloned.1.call-update
  12.8 30.8 %all_gather.10 = bf16[1024,64]{0,1:T(8,128)(2,1)S(1)} all-gather(bf16[128,64]{0,1:T(8,128)(2,1)} %param.6), channel_id=1, replica_groups=mesh['row'=8,'col'=16] {'row'}, dimensions={0}, use_global_device_ids=true | all-gather | bytes 147456 | tf_op jit(solution)/shard_map/all_gather | solution.py:22
  43.6 59.3 %all-gather.3.cloned.1.call-done = bf16[30,240,1024]{1,2,0:T(8,128)(2,1)} async-done(((bf16[30,240,64]{1,2,0:T(8,128)(2,1)}), bf16[30,240,1024]{1,2,0:T(8,128)(2,1)}) %all-gather.3.cloned.1.call-update) | async-done | bytes 14745616 | tf_op jit(solution)/shard_map/all_gather | solution.py:24
  102.9 19.5 %copy.31 = bf16[30,240,1024]{2,1,0:T(8,128)(2,1)} copy(bf16[30,240,1024]{1,2,0:T(8,128)(2,1)} %all-gather.3.cloned.1.call-done) | data formatting | bytes 29491200 | tf_op jit(solution)/shard_map/all_gather | solution.py:24
  122.4 9.8 %convolution_convert_fusion = bf16[7200,64]{0,1:T(8,128)(2,1)S(1)} fusion(bf16[7200,1024]{1,0:T(8,128)(2,1)} %bitcast.20, bf16[1024,64]{0,1:T(8,128)(2,1)S(1)} %all_gather.10), kind=kOutput, calls=%fused_computation.2 | convolution fusion | flops 944179200 | bytes 15798272 | tf_op jit(solution)/shard_map/dot_general | solution.py:27
  132.2 2.3 reshape.32
  134.5 1.5 copy.34
  136.0 74.0 %all-gather.5.cloned.1.call-done = bf16[240,32,480]{2,1,0:T(8,128)(2,1)} async-done(((bf16[30,32,480]{2,1,0:T(8,128)(2,1)}), bf16[240,32,480]{2,1,0:T(8,128)(2,1)}) %all-gather.5.cloned.1.call-update) | async-done | bytes 7372816 | tf_op jit(solution)/shard_map/all_gather | solution.py:23
  210.0 48.8 %bitcast_convert_fusion = bf16[30,32,480]{2,1,0:T(8,128)(2,1)} fusion(bf16[240,32,480]{2,1,0:T(8,128)(2,1)} %all-gather.5.cloned.1.call-done, bf16[30,240,32,32]{1,3,2,0:T(8,128)(2,1)} %bitcast.21), kind=kOutput, calls=%fused_computation.5 | convolution fusion | flops 7078348800 | bytes 23040000 | tf_op jit(solution)/shard_map/ikac,kcm->iam/dot_general | solution.py:30
  (3 shorter events, 0.1 us)
Async XLA Ops:
  7.2 95.7 %all-gather.3.cloned.1.call-start = ((), (), s32[]{:S(2)}) async-start(), calls=%async_computation | async-start | bytes 16711680 | tf_op jit(solution)/shard_map/all_gather | solution.py:24
  12.0 198.0 %all-gather.5.cloned.1.call-start = ((), (), s32[]{:S(2)}) async-start(), calls=%async_computation.1 | async-start | bytes 8847360 | tf_op jit(solution)/shard_map/all_gather | solution.py:23
Sparse Core Ops, SparseCore 0:
  12.1 90.7 all-gather.2
  105.2 104.7 all-gather.4
where the time goes:
time: 267 us; the launch traced here: 266 us
  waiting for transfers between devices  134 us (50%)
  matrix products  58.7 us (22%)
  blocking collectives  30.8 us (12%)
  local copies, waits for them, and re-layouts  25.5 us (10%)
  between operations  14.1 us (5%)
    all_gather x1, waiting for transfers between devices, on_device(): cycle_panel = lax.all_gather(cycle_integrals, 'row', axis=0, tiled=True)  74 us
    all_gather x1, waiting for transfers between devices, on_device(): piece = lax.all_gather(masked, 'col', axis=2, tiled=True)  59.3 us
    dot_general x1, matrix products, on_device(): jnp.einsum('ikac,kcm->iam', piece_four, cycle_panel, preferred_element_ty...  48.8 us
    all_gather x1, blocking collectives, on_device(): pp_panel = lax.all_gather(pp_integrals, 'row', axis=0, tiled=True)  30.8 us
    all_gather x1, local copies, waits for them, and re-layouts, on_device(): piece = lax.all_gather(masked, 'col', axis=2, tiled=True)  19.5 us
    dot_general x1, matrix products, on_device(): jnp.dot(flat_piece, pp_panel, preferred_element_type=jnp.float32)  9.85 us
  transfers between devices with their start and end apart: 2, of which 2 were waited for; matrix products, arithmetic and copies ran while one was open for 12% of the time, Pallas kernels for 0%

commit v1 on v0

v1 whole, which is shorter than its diff:
```python
import jax
import jax.numpy as jnp
from jax import lax
from jax.experimental import pallas as pl
from jax.experimental.pallas import tpu as pltpu
from jax.sharding import PartitionSpec as P

BF = jnp.bfloat16
F32 = jnp.float32
VMEM_LIMIT = 60 * 1024 * 1024
GROUP = 8


def dot(a, b):
    return jnp.dot(a, b, preferred_element_type=F32)


def iota(shape, dim):
    return lax.broadcasted_iota(jnp.int32, shape, dim)


def slot_rows(row):
    x, yh = row // 2, row % 2
    return [((x + dx) % 4) * 2 + (yh + dy) % 2 for dy in (0, 1) for dx in (0, 3, 1, 2)]


def slot_of(row, other):
    dx = (other // 2 - row // 2 + 4) % 4
    base = jnp.where(dx == 0, 0, jnp.where(dx == 3, 1, jnp.where(dx == 1, 2, 3)))
    return base + 4 * ((other + row) % 2)


def piece_ids(col):
    z, yl, core = col // 4, (col // 2) % 2, col % 2
    e = 2 * core - 1
    ids = []
    for dy in (0, 1):
        y = (yl + dy) % 2
        for dz, dc in ((0, 0), (0, 1), (e, 0), (e, 1), (2, 0), (-e, 1), (-e, 0), (2, 1)):
            ids.append(((z + dz + 4) % 4) * 4 + y * 2 + (core + dc) % 2)
    return ids


def lane_map(row, shape, dim):
    lane = iota(shape, dim)
    block, t = lane // 32, lane % 32
    start = jnp.zeros(shape, jnp.int32)
    for k, r in enumerate(slot_rows(row)):
        start = jnp.where(block == k, r * 30, start)
    return start + t, t < 30, block


def prepare_kernel(occ_ref, vir_ref, amp_ref, cyc_ref, pp_ref, a_out, b_out):
    row, col = lax.axis_index("row"), lax.axis_index("col")
    source, held, block = lane_map(row, (1, 256), 1)
    keep = jnp.zeros((1, 256), jnp.int32)
    for k, r in enumerate(slot_rows(row)):
        keep = jnp.where(block == k, occ_ref[row, r], keep)
    keep = jnp.where(held, keep, 0)
    place = jnp.where(iota((240, 256), 0) == source, keep, 0).astype(F32).astype(BF)
    pair = (iota((64, 256), 0) % 32) // 2
    vir = jnp.zeros((64, 256), jnp.int32)
    for k in range(16):
        vir = jnp.where(pair == k, vir_ref[col, k], vir)
    vir = vir.astype(F32)

    def step(i, _):
        a_out[pl.ds(pl.multiple_of(i * 64, 64), 64), :] = (dot(amp_ref[i], place) * vir).astype(BF)
        return 0

    lax.fori_loop(0, 30, step, 0, unroll=5)
    b_out[:, 0:480] = cyc_ref[...]
    for part in range(4):
        b_out[pl.ds(part * 64, 64), 480:512] = pp_ref[:, part * 32:(part + 1) * 32]
    b_out[256:960, 480:512] = jnp.zeros((704, 32), BF)


def prepare(occ_map, vir_map, amp_t, cyc, pp_t):
    return pl.pallas_call(
        prepare_kernel,
        out_shape=(jax.ShapeDtypeStruct((1920, 256), BF), jax.ShapeDtypeStruct((960, 512), BF)),
        in_specs=[pl.BlockSpec(memory_space=pltpu.SMEM)] * 2 + [pl.BlockSpec(memory_space=pltpu.VMEM)] * 3,
        out_specs=(pl.BlockSpec(memory_space=pltpu.VMEM),) * 2,
        compiler_params=pltpu.CompilerParams(vmem_limit_bytes=VMEM_LIMIT),
        cost_estimate=pl.CostEstimate(flops=2 * 1920 * 256 * 256, bytes_accessed=4000000, transcendentals=0),
        name="prepare",
    )(occ_map, vir_map, amp_t, cyc, pp_t)


def regroup_matrix():
    o, s = iota((256, 256), 0), iota((256, 256), 1)
    return jnp.where((s % 32 == o // 8) & (s // 32 == o % 8), 1.0, 0.0).astype(BF)


def regroup(perm, source, count, width):
    for first in range(0, count, 16):
        halves = []
        for m in (first, first + 8):
            n = min(count - m, 8) * 32
            halves.append(dot(perm[:, 0:n], source[pl.ds(m * 32, n), :]).reshape(32, 8, width))
        yield first, jnp.concatenate(halves, axis=1).astype(BF)


def product_kernel(*refs):
    a_refs, b_refs = refs[:16], refs[16:24]
    lad_ref, cyc_ref = refs[24:26]
    a_nat, b_nat, a_cyc, b_cyc, c_out, lad, a_sem, b_sem = refs[26:]
    row, col = lax.axis_index("row"), lax.axis_index("col")
    core = col % 2
    b_copies = [pltpu.make_async_copy(b_refs[k], b_nat.at[k], b_sem.at[k]) for k in range(8)]
    a_copies = [pltpu.make_async_copy(a_refs[k], a_nat.at[k], a_sem.at[k]) for k in range(16)]
    for copy in b_copies + a_copies:
        copy.start()
    perm = regroup_matrix()
    slots = [0, 1 + core, 2 - core, 3]
    slots = slots + [s + 4 for s in slots]
    for k in range(8):
        b_copies[k].wait()
        base = slots[k] * 32
        for first, part in regroup(perm, b_nat.at[k], 30, 512):
            b_cyc[:, pl.ds(pl.multiple_of(base + first, 16), 16), :] = part
    ids = piece_ids(col)
    for group in range(2):
        pieces = range(group * GROUP, (group + 1) * GROUP)
        for n, k in enumerate(pieces):
            a_copies[k].wait()
            for first, part in regroup(perm, a_nat.at[k], 60, 256):
                a_cyc[:, pl.ds(n * 64 + first, 16), :] = part
        for c in range(0, 32, 8):
            left = jnp.concatenate([a_cyc[c + d] for d in range(8)], axis=1)
            right = b_cyc[pl.ds(c, 8), :, :].reshape(2048, 512)
            if c == 0:
                c_acc = dot(left, right)
            else:
                c_acc = c_acc + dot(left, right)
        c_out[pl.ds(group * 512, 512), :] = c_acc.astype(BF)
        tiles = []
        for pair in range(GROUP // 2):
            tile = jnp.zeros((64, 128), F32)
            for half in range(2):
                p = ids[group * GROUP + pair * 2 + half]
                slot = slot_of(row, p // 2)
                place = jnp.where(slot % 4 == 1, 1 + core, jnp.where(slot % 4 == 2, 2 - core, slot % 4)) + 4 * (slot // 4)
                for a in range(2):
                    at = pl.multiple_of((p % 2) * 128 + a * 64, 64)
                    values = b_nat[place, pl.ds(at, 64), 384:512]
                    s, d = iota((128, 128), 0), iota((128, 128), 1)
                    move = jnp.where((s >= 96) & (d == s - 96 + half * 64 + a * 32), 1.0, 0.0).astype(BF)
                    tile = tile + dot(values, move)
            tiles.append(tile.astype(BF))
        v_left = jnp.concatenate(tiles, axis=1)

        def ladder_step(i, _):
            at = pl.ds(pl.multiple_of(i * 64, 64), 64)
            right = jnp.concatenate([a_nat[k, at, :] for k in pieces], axis=0)
            value = dot(v_left, right)
            if group == 0:
                lad[at, :] = value
            else:
                lad[at, :] = lad[at, :] + value
            return 0

        lax.fori_loop(0, 30, ladder_step, 0, unroll=3)
    source, held, _ = lane_map(row, (256, 1), 0)
    back = jnp.where((iota((256, 240), 1) == source) & held, 1.0, 0.0).astype(BF)
    lad_ref[...] = dot(lad[...].astype(BF), back).astype(BF)
    o, s = iota((256, 256), 0), iota((256, 256), 1)
    target = jnp.zeros((256, 256), jnp.int32)
    for k in range(16):
        target = jnp.where(s // 16 == k, ids[k], target)
    target = ((s % 16) // 2) * 32 + target * 2 + s % 2
    spread = jnp.where(o == target, 1.0, 0.0).astype(BF)
    for g in range(4):
        block = jnp.concatenate([c_out[pl.ds(k * 64 + g * 16, 16), :] for k in range(16)], axis=0)
        n = 256 if g < 3 else 192
        cyc_ref[pl.ds(g * 256, n), :] = dot(spread[0:n], block)[:, 0:480].astype(BF)


def products(a_pieces, b_pieces):
    return pl.pallas_call(
        product_kernel,
        out_shape=(jax.ShapeDtypeStruct((1920, 240), BF), jax.ShapeDtypeStruct((960, 480), BF)),
        in_specs=[pl.BlockSpec(memory_space=pl.ANY)] * 24,
        out_specs=(pl.BlockSpec(memory_space=pltpu.VMEM),) * 2,
        scratch_shapes=[
            pltpu.VMEM((16, 1920, 256), BF),
            pltpu.VMEM((8, 960, 512), BF),
            pltpu.VMEM((32, GROUP * 64, 256), BF),
            pltpu.VMEM((32, 256, 512), BF),
            pltpu.VMEM((1024, 512), BF),
            pltpu.VMEM((1920, 256), F32),
            pltpu.SemaphoreType.DMA((16,)),
            pltpu.SemaphoreType.DMA((8,)),
        ],
        compiler_params=pltpu.CompilerParams(vmem_limit_bytes=VMEM_LIMIT),
        cost_estimate=pl.CostEstimate(flops=20 * 10**9, bytes_accessed=26 * 10**6, transcendentals=0),
        name="products",
    )(*a_pieces, *b_pieces)


def permute(value, move):
    pairs = []
    for row in range(8):
        for col in range(16):
            here = (row // 2, (row % 2) * 2 + (col // 2) % 2, col // 4, col % 2)
            x, y, z, core = move(*here)
            x, y, z = x % 4, y % 4, z % 4
            pairs.append((row * 16 + col, (x * 2 + y // 2) * 16 + z * 4 + (y % 2) * 2 + core))
    return lax.ppermute(value, ("row", "col"), pairs)


def along_z(value):
    return permute(value, lambda x, y, z, c: (x, y, z + 1 - 2 * c, c))


def along_x(value):
    return permute(value, lambda x, y, z, c: (x + 1 - 2 * c, y, z, c))


def swap(value):
    return permute(value, lambda x, y, z, c: (x, y, z, 1 - c))


def near_y(value):
    return permute(value, lambda x, y, z, c: (x, y ^ 1, z, c))


def far_y(value):
    return permute(value, lambda x, y, z, c: (x, y + 2, z, c))


def gather_a(own):
    other = swap(own)
    c1, c2 = along_z(own), along_z(other)
    c5 = along_z(c1)
    return [own, other, c1, c2, c5, swap(c1), swap(c2), swap(c5)]


def gather_b(own):
    other = swap(own)
    d1, d2 = along_x(own), along_x(other)
    d5 = along_x(d1)
    return [own, d1, swap(d2), d5]


def on_device(amplitudes, pp_integrals, cycle_integrals, occ_map, vir_map):
    amp_t = jnp.transpose(amplitudes, (0, 2, 1))
    a, b = prepare(occ_map, vir_map, amp_t, cycle_integrals.reshape(960, 480), pp_integrals.T)
    bq = far_y(b)
    aq = near_y(a)
    a_pieces = gather_a(a) + gather_a(aq)
    b_pieces = gather_b(b) + gather_b(bq)
    ladder, cycle_out = products(a_pieces, b_pieces)
    ladder = jnp.transpose(ladder.reshape(30, 64, 240), (0, 2, 1))
    return ladder, cycle_out.reshape(30, 32, 480)


def solution(mesh):
    in_specs = (P("row", None, "col"), P("row", "col"), P("row", None, "col"), P(), P())
    out_specs = (P("row", None, "col"), P("row", None, "col"))
    return jax.shard_map(
        on_device, mesh=mesh, in_specs=in_specs, out_specs=out_specs, check_vma=False
    )
```

time: 267 us -> 154 us (0.58)
  matrix products: 58.7 us -> 0 us
  waiting for transfers between devices: 134 us -> 88.6 us
  Pallas kernels: 0 us -> 36.1 us
  blocking collectives: 30.8 us -> 0 us
  starting transfers between devices: 0.08 us -> 25.3 us
  local copies, waits for them, and re-layouts: 25.5 us -> 2.56 us
  between operations: 14.1 us -> 1.03 us
    all_gather x2 -> x0, waiting for transfers between devices: 133 us -> none  [the longest x1 74 us: on_device(): cycle_panel = lax.all_gather(cycle_integrals, 'row', axis=0, tiled=True)]
    ppermute x0 -> x26, waiting for transfers between devices: none -> 88.6 us  [permute(): return lax.ppermute(value, ('row', 'col'), pairs)]
    dot_general x2 -> x0, matrix products: 58.7 us -> none  [the longest x1 48.8 us: on_device(): jnp.einsum('ikac,kcm->iam', piece_four, cycle_panel, preferred_element_ty...]
    pallas_call x0 -> x2, Pallas kernels: none -> 36.1 us  [the longest x1 31.7 us: products(): pl.pallas_call(product_kernel, out_shape=(jax.ShapeDtypeStruct((1920, 240...]
    all_gather x1 -> x0, blocking collectives: 30.8 us -> none  [on_device(): pp_panel = lax.all_gather(pp_integrals, 'row', axis=0, tiled=True)]
    ppermute x0 -> x26, starting transfers between devices: none -> 25.3 us  [permute(): return lax.ppermute(value, ('row', 'col'), pairs)]
    all_gather x1 -> x0, local copies, waits for them, and re-layouts: 19.5 us -> none  [on_device(): piece = lax.all_gather(masked, 'col', axis=2, tiled=True)]
  transfers between devices with their start and end apart: 2 -> 26, of which waited for: 2 -> 10; matrix products, arithmetic and copies ran while one was open for 12% -> 0% of each run, Pallas kernels for 0% -> 0%
where the time goes in v1:
time: 154 us
  waiting for transfers between devices  88.6 us (58%)
  Pallas kernels  36.1 us (23%)
  starting transfers between devices  25.3 us (16%)
  local copies, waits for them, and re-layouts  2.56 us (2%)
    ppermute x26, waiting for transfers between devices, permute(): return lax.ppermute(value, ('row', 'col'), pairs)  88.6 us
    pallas_call x1, Pallas kernels, products(): pl.pallas_call(product_kernel, out_shape=(jax.ShapeDtypeStruct((1920, 240...  31.7 us
    ppermute x26, starting transfers between devices, permute(): return lax.ppermute(value, ('row', 'col'), pairs)  25.3 us
    pallas_call x1, Pallas kernels, prepare(): pl.pallas_call(prepare_kernel, out_shape=(jax.ShapeDtypeStruct((1920, 256...  4.37 us
  transfers between devices with their start and end apart: 26, of which 10 were waited for; matrix products, arithmetic and copies ran while one was open for 0% of the time, Pallas kernels for 0%

profile of v1, /device:TPU:0, one launch (start us, length us, event | category | flops | bytes accessed | tf_op | source)
XLA Modules:
  0.0 153.5 jit_solution(10123499998434815933)
XLA Ops:
  0.6 4.4 %prepare.1 = (bf16[1920,256]{1,0:T(8,128)(2,1)}, bf16[960,512]{1,0:T(8,128)(2,1)}) custom-call(s32[8,8]{1,0:T(8,128)} %occ_ref.1, s32[16,16]{1,0:T(8,128)} %vir_ref.1, bf16[30,64,240]{2,1,0:T(8,128)(2,1)} %bitcast.7, bf16[960,480]{1,0:T(8,128)(2,1)} %bitcast.8, bf16[64,128]{1,0:T(8,128)(2,1)} %bitcast.9), custom_call_target="tpu_custom_call" | custom-call | flops 251658240 | bytes 4000000 | tf_op jit(solution)/shard_map/prepare/pallas_call | solution.py:79
  5.0 1.7 %collective-permute-start.7 = (bf16[1920,256]{1,0:T(8,128)(2,1)}, bf16[1920,256]{1,0:T(8,128)(2,1)S(1)}, u32[]{:S(2)}, u32[]{:S(2)}) collective-permute-start(bf16[1920,256]{1,0:T(8,128)(2,1)} %get-tuple-element.6.refs_0_), channel_id=1, source_target_pairs={{0,2},{1,3},{2,0},{3,1},{4,6},{5,7},{6,4},{7,5},{8,10},{9,11},{10,... | collective-permute-start | bytes 2949128 | tf_op jit(solution)/shard_map/ppermute | solution.py:209
  6.7 1.9 %collective-permute-start.1 = (bf16[1920,256]{1,0:T(8,128)(2,1)}, bf16[1920,256]{1,0:T(8,128)(2,1)S(1)}, u32[]{:S(2)}, u32[]{:S(2)}) collective-permute-start(bf16[1920,256]{1,0:T(8,128)(2,1)} %get-tuple-element.6.refs_0_), channel_id=1, source_target_pairs={{0,4},{1,13},{2,6},{3,15},{4,8},{5,1},{6,10},{7,3},{8,12},{9,5},{1... | collective-permute-start | bytes 2949128 | tf_op jit(solution)/shard_map/ppermute | solution.py:209
  8.6 1.4 collective-permute-start
  10.0 2.9 %collective-permute-start.20 = (bf16[960,512]{1,0:T(8,128)(2,1)}, bf16[960,512]{1,0:T(8,128)(2,1)S(1)}, u32[]{:S(2)}, u32[]{:S(2)}) collective-permute-start(bf16[960,512]{1,0:T(8,128)(2,1)} %get-tuple-element.7.refs_16_), channel_id=1, source_target_pairs={{0,16},{1,17},{2,18},{3,19},{4,20},{5,21},{6,22},{7,23},{8,24},{9,... | collective-permute-start | bytes 2949128 | tf_op jit(solution)/shard_map/ppermute | solution.py:209
  12.9 17.0 %collective-permute-done.7.refs_8_ = bf16[1920,256]{1,0:T(8,128)(2,1)S(1)} collective-permute-done((bf16[1920,256]{1,0:T(8,128)(2,1)}, bf16[1920,256]{1,0:T(8,128)(2,1)S(1)}, u32[]{:S(2)}, u32[]{:S(2)}) %collective-permute-start.7) | collective-permute-done | bytes 983072 | tf_op jit(solution)/shard_map/ppermute | solution.py:209
  29.9 1.6 %collective-permute-start.15 = (bf16[960,512]{1,0:T(8,128)(2,1)}, bf16[960,512]{1,0:T(8,128)(2,1)S(1)}, u32[]{:S(2)}, u32[]{:S(2)}) collective-permute-start(bf16[960,512]{1,0:T(8,128)(2,1)} %get-tuple-element.7.refs_16_), channel_id=1, source_target_pairs={{0,32},{1,97},{2,34},{3,99},{4,36},{5,101},{6,38},{7,103},{8,40},{... | collective-permute-start | bytes 2949128 | tf_op jit(solution)/shard_map/ppermute | solution.py:209
  31.4 1.9 %collective-permute-start.9 = (bf16[1920,256]{1,0:T(8,128)(2,1)S(1)}, bf16[1920,256]{1,0:T(8,128)(2,1)S(1)}, u32[]{:S(2)}, u32[]{:S(2)}) collective-permute-start(bf16[1920,256]{1,0:T(8,128)(2,1)S(1)} %collective-permute-done.7.refs_8_), channel_id=1, source_target_pairs={{0,4},{1,13},{2,6},{3,15},{4,8},{5,1},{6,10},{7,3},{8,12},{9,5},{1... | collective-permute-start | bytes 2949128 | tf_op jit(solution)/shard_map/ppermute | solution.py:209
  33.4 0.6 collective-permute-start.8
  34.0 18.3 %collective-permute-done.20.refs_20_ = bf16[960,512]{1,0:T(8,128)(2,1)S(1)} collective-permute-done((bf16[960,512]{1,0:T(8,128)(2,1)}, bf16[960,512]{1,0:T(8,128)(2,1)S(1)}, u32[]{:S(2)}, u32[]{:S(2)}) %collective-permute-start.20) | collective-permute-done | bytes 983072 | tf_op jit(solution)/shard_map/ppermute | solution.py:209
  52.3 2.0 %collective-permute-start.3 = (bf16[1920,256]{1,0:T(8,128)(2,1)S(1)}, bf16[1920,256]{1,0:T(8,128)(2,1)S(1)}, u32[]{:S(2)}, u32[]{:S(2)}) collective-permute-start(bf16[1920,256]{1,0:T(8,128)(2,1)S(1)} %collective-permute-done.1.refs_2_), channel_id=1, source_target_pairs={{0,4},{1,13},{2,6},{3,15},{4,8},{5,1},{6,10},{7,3},{8,12},{9,5},{1... | collective-permute-start | bytes 2949128 | tf_op jit(solution)/shard_map/ppermute | solution.py:209
  54.3 1.9 %collective-permute-start.2 = (bf16[1920,256]{1,0:T(8,128)(2,1)S(1)}, bf16[1920,256]{1,0:T(8,128)(2,1)S(1)}, u32[]{:S(2)}, u32[]{:S(2)}) collective-permute-start(bf16[1920,256]{1,0:T(8,128)(2,1)S(1)} %collective-permute-done.refs_1_), channel_id=1, source_target_pairs={{0,4},{1,13},{2,6},{3,15},{4,8},{5,1},{6,10},{7,3},{8,12},{9,5},{1... | collective-permute-start | bytes 2949128 | tf_op jit(solution)/shard_map/ppermute | solution.py:209
  56.2 0.5 collective-permute-start.22
  56.7 1.5 collective-permute-start.21
  58.2 1.5 collective-permute-start.17
  59.7 8.8 %collective-permute-done.3.refs_4_ = bf16[1920,256]{1,0:T(8,128)(2,1)S(1)} collective-permute-done((bf16[1920,256]{1,0:T(8,128)(2,1)S(1)}, bf16[1920,256]{1,0:T(8,128)(2,1)S(1)}, u32[]{:S(2)}, u32[]{:S(2)}) %collective-permute-start.3) | collective-permute-done | bytes 983072 | tf_op jit(solution)/shard_map/ppermute | solution.py:209
  68.5 1.5 collective-permute-start.19
  70.0 9.0 %collective-permute-done.2.refs_3_ = bf16[1920,256]{1,0:T(8,128)(2,1)S(1)} collective-permute-done((bf16[1920,256]{1,0:T(8,128)(2,1)S(1)}, bf16[1920,256]{1,0:T(8,128)(2,1)S(1)}, u32[]{:S(2)}, u32[]{:S(2)}) %collective-permute-start.2) | collective-permute-done | bytes 983072 | tf_op jit(solution)/shard_map/ppermute | solution.py:209
  79.2 1.8 %collective-permute-start.10 = (bf16[1920,256]{1,0:T(8,128)(2,1)S(1)}, bf16[1920,256]{1,0:T(8,128)(2,1)S(1)}, u32[]{:S(2)}, u32[]{:S(2)}) collective-permute-start(bf16[1920,256]{1,0:T(8,128)(2,1)S(1)} %collective-permute-done.8.refs_9_), channel_id=1, source_target_pairs={{0,4},{1,13},{2,6},{3,15},{4,8},{5,1},{6,10},{7,3},{8,12},{9,5},{1... | collective-permute-start | bytes 2949128 | tf_op jit(solution)/shard_map/ppermute | solution.py:209
  81.0 1.6 %collective-permute-done.17 = bf16[960,512]{1,0:T(8,128)(2,1)S(1)} collective-permute-done((bf16[960,512]{1,0:T(8,128)(2,1)S(1)}, bf16[960,512]{1,0:T(8,128)(2,1)S(1)}, u32[]{:S(2)}, u32[]{:S(2)}) %collective-permute-start.17) | collective-permute-done | bytes 983072 | tf_op jit(solution)/shard_map/ppermute | solution.py:209
  82.6 10.5 %collective-permute-done.19.refs_19_ = bf16[960,512]{1,0:T(8,128)(2,1)S(1)} collective-permute-done((bf16[960,512]{1,0:T(8,128)(2,1)S(1)}, bf16[960,512]{1,0:T(8,128)(2,1)S(1)}, u32[]{:S(2)}, u32[]{:S(2)}) %collective-permute-start.19) | collective-permute-done | bytes 983072 | tf_op jit(solution)/shard_map/ppermute | solution.py:209
  93.1 0.3 collective-permute-start.23
  93.5 0.9 collective-permute-done.11.refs_12_
  94.4 1.5 collective-permute-start.25
  95.9 9.0 %collective-permute-done.10.refs_11_ = bf16[1920,256]{1,0:T(8,128)(2,1)S(1)} collective-permute-done((bf16[1920,256]{1,0:T(8,128)(2,1)S(1)}, bf16[1920,256]{1,0:T(8,128)(2,1)S(1)}, u32[]{:S(2)}, u32[]{:S(2)}) %collective-permute-start.10) | collective-permute-done | bytes 983072 | tf_op jit(solution)/shard_map/ppermute | solution.py:209
  105.0 0.6 collective-permute-start.14
  105.7 2.8 %collective-permute-done.23 = bf16[960,512]{1,0:T(8,128)(2,1)S(1)} collective-permute-done((bf16[960,512]{1,0:T(8,128)(2,1)S(1)}, bf16[960,512]{1,0:T(8,128)(2,1)S(1)}, u32[]{:S(2)}, u32[]{:S(2)}) %collective-permute-start.23) | collective-permute-done | bytes 983072 | tf_op jit(solution)/shard_map/ppermute | solution.py:209
  108.5 10.5 %collective-permute-done.25.refs_23_ = bf16[960,512]{1,0:T(8,128)(2,1)S(1)} collective-permute-done((bf16[960,512]{1,0:T(8,128)(2,1)S(1)}, bf16[960,512]{1,0:T(8,128)(2,1)S(1)}, u32[]{:S(2)}, u32[]{:S(2)}) %collective-permute-start.25) | collective-permute-done | bytes 983072 | tf_op jit(solution)/shard_map/ppermute | solution.py:209
  119.1 0.9 copy-done.17
  120.3 0.3 copy-done.19
  120.7 1.0 copy-done.20
  121.7 31.7 %products.1 = (bf16[1920,240]{1,0:T(8,128)(2,1)}, bf16[960,480]{1,0:T(8,128)(2,1)}) custom-call(bf16[1920,256]{1,0:T(8,128)(2,1)} %get-tuple-element.6.refs_0_, bf16[1920,256]{1,0:T(8,128)(2,1)} %copy-done.2, bf16[1920,256]{1,0:T(8,128)(2,1)} %copy-done.1, bf16[1920,256]{1,0:T(8,128)(2,1)} %copy-done.9, bf16[1920,256]{1,0:T(8,128)(2,1)} %copy-done.8, ...), custom_call_target="tpu_custom_call" | custom-call | flops 20000000000 | bytes 26000000 | tf_op jit(solution)/shard_map/products/pallas_call | solution.py:180
  (64 shorter events, 0.6 us)
Async XLA Ops:
  5.0 24.9 %collective-permute-start.7 = (bf16[1920,256]{1,0:T(8,128)(2,1)}, bf16[1920,256]{1,0:T(8,128)(2,1)S(1)}, u32[]{:S(2)}, u32[]{:S(2)}) collective-permute-start(bf16[1920,256]{1,0:T(8,128)(2,1)} %get-tuple-element.6.refs_0_), channel_id=1, source_target_pairs={{0,2},{1,3},{2,0},{3,1},{4,6},{5,7},{6,4},{7,5},{8,10},{9,11},{10,... | collective-permute-start | bytes 2949128 | tf_op jit(solution)/shard_map/ppermute | solution.py:209
  6.7 24.8 %collective-permute-start.1 = (bf16[1920,256]{1,0:T(8,128)(2,1)}, bf16[1920,256]{1,0:T(8,128)(2,1)S(1)}, u32[]{:S(2)}, u32[]{:S(2)}) collective-permute-start(bf16[1920,256]{1,0:T(8,128)(2,1)} %get-tuple-element.6.refs_0_), channel_id=1, source_target_pairs={{0,4},{1,13},{2,6},{3,15},{4,8},{5,1},{6,10},{7,3},{8,12},{9,5},{1... | collective-permute-start | bytes 2949128 | tf_op jit(solution)/shard_map/ppermute | solution.py:209
  8.6 24.8 %collective-permute-start = (bf16[1920,256]{1,0:T(8,128)(2,1)}, bf16[1920,256]{1,0:T(8,128)(2,1)S(1)}, u32[]{:S(2)}, u32[]{:S(2)}) collective-permute-start(bf16[1920,256]{1,0:T(8,128)(2,1)} %get-tuple-element.6.refs_0_), channel_id=1, source_target_pairs={{0,1},{1,0},{2,3},{3,2},{4,5},{5,4},{6,7},{7,6},{8,9},{9,8},{10,11... | collective-permute-start | bytes 2949128 | tf_op jit(solution)/shard_map/ppermute | solution.py:209
  10.0 42.3 %collective-permute-start.20 = (bf16[960,512]{1,0:T(8,128)(2,1)}, bf16[960,512]{1,0:T(8,128)(2,1)S(1)}, u32[]{:S(2)}, u32[]{:S(2)}) collective-permute-start(bf16[960,512]{1,0:T(8,128)(2,1)} %get-tuple-element.7.refs_16_), channel_id=1, source_target_pairs={{0,16},{1,17},{2,18},{3,19},{4,20},{5,21},{6,22},{7,23},{8,24},{9,... | collective-permute-start | bytes 2949128 | tf_op jit(solution)/shard_map/ppermute | solution.py:209
  12.9 39.4 %collective-permute-start.16 = (bf16[960,512]{1,0:T(8,128)(2,1)}, bf16[960,512]{1,0:T(8,128)(2,1)S(1)}, u32[]{:S(2)}, u32[]{:S(2)}) collective-permute-start(bf16[960,512]{1,0:T(8,128)(2,1)} %get-tuple-element.7.refs_16_), channel_id=1, source_target_pairs={{0,1},{1,0},{2,3},{3,2},{4,5},{5,4},{6,7},{7,6},{8,9},{9,8},{10,11... | collective-permute-start | bytes 2949128 | tf_op jit(solution)/shard_map/ppermute | solution.py:209
  29.9 91.8 %copy-start = (bf16[1920,256]{1,0:T(8,128)(2,1)}, bf16[1920,256]{1,0:T(8,128)(2,1)S(1)}, u32[]{:S(2)}) copy-start(bf16[1920,256]{1,0:T(8,128)(2,1)S(1)} %collective-permute-done.7.refs_8_) | copy-start | bytes 2949124
  29.9 24.4 %collective-permute-start.15 = (bf16[960,512]{1,0:T(8,128)(2,1)}, bf16[960,512]{1,0:T(8,128)(2,1)S(1)}, u32[]{:S(2)}, u32[]{:S(2)}) collective-permute-start(bf16[960,512]{1,0:T(8,128)(2,1)} %get-tuple-element.7.refs_16_), channel_id=1, source_target_pairs={{0,32},{1,97},{2,34},{3,99},{4,36},{5,101},{6,38},{7,103},{8,40},{... | collective-permute-start | bytes 2949128 | tf_op jit(solution)/shard_map/ppermute | solution.py:209
  31.4 90.2 %copy-start.1 = (bf16[1920,256]{1,0:T(8,128)(2,1)}, bf16[1920,256]{1,0:T(8,128)(2,1)S(1)}, u32[]{:S(2)}) copy-start(bf16[1920,256]{1,0:T(8,128)(2,1)S(1)} %collective-permute-done.1.refs_2_) | copy-start | bytes 2949124
  31.4 24.8 %collective-permute-start.9 = (bf16[1920,256]{1,0:T(8,128)(2,1)S(1)}, bf16[1920,256]{1,0:T(8,128)(2,1)S(1)}, u32[]{:S(2)}, u32[]{:S(2)}) collective-permute-start(bf16[1920,256]{1,0:T(8,128)(2,1)S(1)} %collective-permute-done.7.refs_8_), channel_id=1, source_target_pairs={{0,4},{1,13},{2,6},{3,15},{4,8},{5,1},{6,10},{7,3},{8,12},{9,5},{1... | collective-permute-start | bytes 2949128 | tf_op jit(solution)/shard_map/ppermute | solution.py:209
  33.4 88.3 %copy-start.2 = (bf16[1920,256]{1,0:T(8,128)(2,1)}, bf16[1920,256]{1,0:T(8,128)(2,1)S(1)}, u32[]{:S(2)}) copy-start(bf16[1920,256]{1,0:T(8,128)(2,1)S(1)} %collective-permute-done.refs_1_) | copy-start | bytes 2949124
  33.4 23.4 %collective-permute-start.8 = (bf16[1920,256]{1,0:T(8,128)(2,1)S(1)}, bf16[1920,256]{1,0:T(8,128)(2,1)S(1)}, u32[]{:S(2)}, u32[]{:S(2)}) collective-permute-start(bf16[1920,256]{1,0:T(8,128)(2,1)S(1)} %collective-permute-done.7.refs_8_), channel_id=1, source_target_pairs={{0,1},{1,0},{2,3},{3,2},{4,5},{5,4},{6,7},{7,6},{8,9},{9,8},{10,11... | collective-permute-start | bytes 2949128 | tf_op jit(solution)/shard_map/ppermute | solution.py:209
  52.3 69.3 %copy-start.3 = (bf16[960,512]{1,0:T(8,128)(2,1)}, bf16[960,512]{1,0:T(8,128)(2,1)S(1)}, u32[]{:S(2)}) copy-start(bf16[960,512]{1,0:T(8,128)(2,1)S(1)} %collective-permute-done.20.refs_20_) | copy-start | bytes 2949124
  52.3 5.9 %collective-permute-start.4 = (bf16[1920,256]{1,0:T(8,128)(2,1)S(1)}, bf16[1920,256]{1,0:T(8,128)(2,1)S(1)}, u32[]{:S(2)}, u32[]{:S(2)}) collective-permute-start(bf16[1920,256]{1,0:T(8,128)(2,1)S(1)} %collective-permute-done.1.refs_2_), channel_id=1, source_target_pairs={{0,1},{1,0},{2,3},{3,2},{4,5},{5,4},{6,7},{7,6},{8,9},{9,8},{10,11... | collective-permute-start | bytes 2949128 | tf_op jit(solution)/shard_map/ppermute | solution.py:209
  52.3 16.2 %collective-permute-start.3 = (bf16[1920,256]{1,0:T(8,128)(2,1)S(1)}, bf16[1920,256]{1,0:T(8,128)(2,1)S(1)}, u32[]{:S(2)}, u32[]{:S(2)}) collective-permute-start(bf16[1920,256]{1,0:T(8,128)(2,1)S(1)} %collective-permute-done.1.refs_2_), channel_id=1, source_target_pairs={{0,4},{1,13},{2,6},{3,15},{4,8},{5,1},{6,10},{7,3},{8,12},{9,5},{1... | collective-permute-start | bytes 2949128 | tf_op jit(solution)/shard_map/ppermute | solution.py:209
  54.3 24.7 %collective-permute-start.2 = (bf16[1920,256]{1,0:T(8,128)(2,1)S(1)}, bf16[1920,256]{1,0:T(8,128)(2,1)S(1)}, u32[]{:S(2)}, u32[]{:S(2)}) collective-permute-start(bf16[1920,256]{1,0:T(8,128)(2,1)S(1)} %collective-permute-done.refs_1_), channel_id=1, source_target_pairs={{0,4},{1,13},{2,6},{3,15},{4,8},{5,1},{6,10},{7,3},{8,12},{9,5},{1... | collective-permute-start | bytes 2949128 | tf_op jit(solution)/shard_map/ppermute | solution.py:209
  56.2 22.8 %collective-permute-start.22 = (bf16[960,512]{1,0:T(8,128)(2,1)S(1)}, bf16[960,512]{1,0:T(8,128)(2,1)S(1)}, u32[]{:S(2)}, u32[]{:S(2)}) collective-permute-start(bf16[960,512]{1,0:T(8,128)(2,1)S(1)} %collective-permute-done.20.refs_20_), channel_id=1, source_target_pairs={{0,1},{1,0},{2,3},{3,2},{4,5},{5,4},{6,7},{7,6},{8,9},{9,8},{10,11... | collective-permute-start | bytes 2949128 | tf_op jit(solution)/shard_map/ppermute | solution.py:209
  56.7 37.7 %copy-start.6 = (bf16[1920,256]{1,0:T(8,128)(2,1)}, bf16[1920,256]{1,0:T(8,128)(2,1)S(1)}, u32[]{:S(2)}) copy-start(bf16[1920,256]{1,0:T(8,128)(2,1)S(1)} %collective-permute-done.8.refs_9_) | copy-start | bytes 2949124
  56.7 22.4 %collective-permute-start.21 = (bf16[960,512]{1,0:T(8,128)(2,1)S(1)}, bf16[960,512]{1,0:T(8,128)(2,1)S(1)}, u32[]{:S(2)}, u32[]{:S(2)}) collective-permute-start(bf16[960,512]{1,0:T(8,128)(2,1)S(1)} %collective-permute-done.20.refs_20_), channel_id=1, source_target_pairs={{0,32},{1,97},{2,34},{3,99},{4,36},{5,101},{6,38},{7,103},{8,40},{... | collective-permute-start | bytes 2949128 | tf_op jit(solution)/shard_map/ppermute | solution.py:209
  58.2 46.7 %copy-start.7 = (bf16[1920,256]{1,0:T(8,128)(2,1)}, bf16[1920,256]{1,0:T(8,128)(2,1)S(1)}, u32[]{:S(2)}) copy-start(bf16[1920,256]{1,0:T(8,128)(2,1)S(1)} %collective-permute-done.4.refs_5_) | copy-start | bytes 2949124
  58.2 24.3 %collective-permute-start.17 = (bf16[960,512]{1,0:T(8,128)(2,1)S(1)}, bf16[960,512]{1,0:T(8,128)(2,1)S(1)}, u32[]{:S(2)}, u32[]{:S(2)}) collective-permute-start(bf16[960,512]{1,0:T(8,128)(2,1)S(1)} %collective-permute-done.16), channel_id=1, source_target_pairs={{0,32},{1,97},{2,34},{3,99},{4,36},{5,101},{6,38},{7,103},{8,40},{... | collective-permute-start | bytes 2949128 | tf_op jit(solution)/shard_map/ppermute | solution.py:209
  68.5 24.6 %collective-permute-start.19 = (bf16[960,512]{1,0:T(8,128)(2,1)S(1)}, bf16[960,512]{1,0:T(8,128)(2,1)S(1)}, u32[]{:S(2)}, u32[]{:S(2)}) collective-permute-start(bf16[960,512]{1,0:T(8,128)(2,1)S(1)} %collective-permute-done.15.refs_17_), channel_id=1, source_target_pairs={{0,32},{1,97},{2,34},{3,99},{4,36},{5,101},{6,38},{7,103},{8,40},{... | collective-permute-start | bytes 2949128 | tf_op jit(solution)/shard_map/ppermute | solution.py:209
  79.0 14.1 %collective-permute-start.12 = (bf16[1920,256]{1,0:T(8,128)(2,1)S(1)}, bf16[1920,256]{1,0:T(8,128)(2,1)S(1)}, u32[]{:S(2)}, u32[]{:S(2)}) collective-permute-start(bf16[1920,256]{1,0:T(8,128)(2,1)S(1)} %collective-permute-done.9.refs_10_), channel_id=1, source_target_pairs={{0,1},{1,0},{2,3},{3,2},{4,5},{5,4},{6,7},{7,6},{8,9},{9,8},{10,11... | collective-permute-start | bytes 2949128 | tf_op jit(solution)/shard_map/ppermute | solution.py:209
  79.0 15.4 %collective-permute-start.11 = (bf16[1920,256]{1,0:T(8,128)(2,1)S(1)}, bf16[1920,256]{1,0:T(8,128)(2,1)S(1)}, u32[]{:S(2)}, u32[]{:S(2)}) collective-permute-start(bf16[1920,256]{1,0:T(8,128)(2,1)S(1)} %collective-permute-done.9.refs_10_), channel_id=1, source_target_pairs={{0,4},{1,13},{2,6},{3,15},{4,8},{5,1},{6,10},{7,3},{8,12},{9,5},{1... | collective-permute-start | bytes 2949128 | tf_op jit(solution)/shard_map/ppermute | solution.py:209
  79.2 25.8 %collective-permute-start.10 = (bf16[1920,256]{1,0:T(8,128)(2,1)S(1)}, bf16[1920,256]{1,0:T(8,128)(2,1)S(1)}, u32[]{:S(2)}, u32[]{:S(2)}) collective-permute-start(bf16[1920,256]{1,0:T(8,128)(2,1)S(1)} %collective-permute-done.8.refs_9_), channel_id=1, source_target_pairs={{0,4},{1,13},{2,6},{3,15},{4,8},{5,1},{6,10},{7,3},{8,12},{9,5},{1... | collective-permute-start | bytes 2949128 | tf_op jit(solution)/shard_map/ppermute | solution.py:209
  82.6 22.4 %collective-permute-start.6 = (bf16[1920,256]{1,0:T(8,128)(2,1)S(1)}, bf16[1920,256]{1,0:T(8,128)(2,1)S(1)}, u32[]{:S(2)}, u32[]{:S(2)}) collective-permute-start(bf16[1920,256]{1,0:T(8,128)(2,1)S(1)} %collective-permute-done.3.refs_4_), channel_id=1, source_target_pairs={{0,1},{1,0},{2,3},{3,2},{4,5},{5,4},{6,7},{7,6},{8,9},{9,8},{10,11... | collective-permute-start | bytes 2949128 | tf_op jit(solution)/shard_map/ppermute | solution.py:209
  93.1 12.5 %collective-permute-start.5 = (bf16[1920,256]{1,0:T(8,128)(2,1)S(1)}, bf16[1920,256]{1,0:T(8,128)(2,1)S(1)}, u32[]{:S(2)}, u32[]{:S(2)}) collective-permute-start(bf16[1920,256]{1,0:T(8,128)(2,1)S(1)} %collective-permute-done.2.refs_3_), channel_id=1, source_target_pairs={{0,1},{1,0},{2,3},{3,2},{4,5},{5,4},{6,7},{7,6},{8,9},{9,8},{10,11... | collective-permute-start | bytes 2949128 | tf_op jit(solution)/shard_map/ppermute | solution.py:209
  93.1 15.4 %collective-permute-start.23 = (bf16[960,512]{1,0:T(8,128)(2,1)S(1)}, bf16[960,512]{1,0:T(8,128)(2,1)S(1)}, u32[]{:S(2)}, u32[]{:S(2)}) collective-permute-start(bf16[960,512]{1,0:T(8,128)(2,1)S(1)} %collective-permute-done.22), channel_id=1, source_target_pairs={{0,32},{1,97},{2,34},{3,99},{4,36},{5,101},{6,38},{7,103},{8,40},{... | collective-permute-start | bytes 2949128 | tf_op jit(solution)/shard_map/ppermute | solution.py:209
  94.4 24.6 %collective-permute-start.25 = (bf16[960,512]{1,0:T(8,128)(2,1)S(1)}, bf16[960,512]{1,0:T(8,128)(2,1)S(1)}, u32[]{:S(2)}, u32[]{:S(2)}) collective-permute-start(bf16[960,512]{1,0:T(8,128)(2,1)S(1)} %collective-permute-done.21.refs_21_), channel_id=1, source_target_pairs={{0,32},{1,97},{2,34},{3,99},{4,36},{5,101},{6,38},{7,103},{8,40},{... | collective-permute-start | bytes 2949128 | tf_op jit(solution)/shard_map/ppermute | solution.py:209
  105.0 14.1 %collective-permute-start.18 = (bf16[960,512]{1,0:T(8,128)(2,1)S(1)}, bf16[960,512]{1,0:T(8,128)(2,1)S(1)}, u32[]{:S(2)}, u32[]{:S(2)}) collective-permute-start(bf16[960,512]{1,0:T(8,128)(2,1)S(1)} %collective-permute-done.17), channel_id=1, source_target_pairs={{0,1},{1,0},{2,3},{3,2},{4,5},{5,4},{6,7},{7,6},{8,9},{9,8},{10,11... | collective-permute-start | bytes 2949128 | tf_op jit(solution)/shard_map/ppermute | solution.py:209
  105.0 14.1 %collective-permute-start.14 = (bf16[1920,256]{1,0:T(8,128)(2,1)S(1)}, bf16[1920,256]{1,0:T(8,128)(2,1)S(1)}, u32[]{:S(2)}, u32[]{:S(2)}) collective-permute-start(bf16[1920,256]{1,0:T(8,128)(2,1)S(1)} %collective-permute-done.11.refs_12_), channel_id=1, source_target_pairs={{0,1},{1,0},{2,3},{3,2},{4,5},{5,4},{6,7},{7,6},{8,9},{9,8},{10,11... | collective-permute-start | bytes 2949128 | tf_op jit(solution)/shard_map/ppermute | solution.py:209
  105.6 13.5 %collective-permute-start.13 = (bf16[1920,256]{1,0:T(8,128)(2,1)S(1)}, bf16[1920,256]{1,0:T(8,128)(2,1)S(1)}, u32[]{:S(2)}, u32[]{:S(2)}) collective-permute-start(bf16[1920,256]{1,0:T(8,128)(2,1)S(1)} %collective-permute-done.10.refs_11_), channel_id=1, source_target_pairs={{0,1},{1,0},{2,3},{3,2},{4,5},{5,4},{6,7},{7,6},{8,9},{9,8},{10,11... | collective-permute-start | bytes 2949128 | tf_op jit(solution)/shard_map/ppermute | solution.py:209
  108.5 13.1 %collective-permute-start.24 = (bf16[960,512]{1,0:T(8,128)(2,1)S(1)}, bf16[960,512]{1,0:T(8,128)(2,1)}, u32[]{:S(2)}, u32[]{:S(2)}) collective-permute-start(bf16[960,512]{1,0:T(8,128)(2,1)S(1)} %collective-permute-done.23), channel_id=1, source_target_pairs={{0,1},{1,0},{2,3},{3,2},{4,5},{5,4},{6,7},{7,6},{8,9},{9,8},{10,11... | collective-permute-start | bytes 2949128 | tf_op jit(solution)/shard_map/ppermute | solution.py:209
  (15 other events, 273.7 us)

commit v2 on v0

v2 whole, which is shorter than its diff:
```python
import functools

import jax
import jax.numpy as jnp
from jax import lax
from jax.experimental import pallas as pl
from jax.experimental.pallas import tpu as pltpu
from jax.sharding import PartitionSpec as P

BF = jnp.bfloat16
F32 = jnp.float32
PARAMS = pltpu.CompilerParams(vmem_limit_bytes=56 * 1024 * 1024)
VMEM = pl.BlockSpec(memory_space=pltpu.VMEM)
SMEM = pl.BlockSpec(memory_space=pltpu.SMEM)
ANY = pl.BlockSpec(memory_space=pl.ANY)


def cost(flops, size):
    return pl.CostEstimate(flops=flops, bytes_accessed=size, transcendentals=0)


def dot(a, b):
    return jnp.dot(a, b, preferred_element_type=F32)


def iota(shape, dim):
    return lax.broadcasted_iota(jnp.int32, shape, dim)


def here():
    return lax.axis_index("row"), lax.axis_index("col")


def slot_rows(row):
    x, yh = row // 2, row % 2
    return [((x + dx) % 4) * 2 + (yh + dy) % 2 for dy in (0, 1) for dx in (0, 3, 1, 2)]


def piece_ids(col):
    z, yl, core = col // 4, (col // 2) % 2, col % 2
    e = 2 * core - 1
    near = dict(a=(0, 0), s_a=(0, 1), c1=(e, 0), c2=(e, 1), c5=(2, 0), s_c1=(-e, 1), s_c2=(-e, 0), s_c5=(2, 1))
    far = dict(aq="a", s_aq="s_a", cq1="c1", cq2="c2", cq5="c5", s_cq1="s_c1", s_cq2="s_c2", s_cq5="s_c5")
    ids = {}
    for dy in (0, 1):
        for name in far if dy else near:
            dz, dc = near[far[name] if dy else name]
            ids[name] = ((z + dz + 4) % 4) * 4 + ((yl + dy) % 2) * 2 + (core + dc) % 2
    return ids


def lane_map(row, shape, dim):
    lane = iota(shape, dim)
    block, t = lane // 32, lane % 32
    start = jnp.zeros(shape, jnp.int32)
    for k, r in enumerate(slot_rows(row)):
        start = jnp.where(block == k, r * 30, start)
    return start + t, t < 30, block


def prepare_kernel(occ_ref, vir_ref, amp_ref, out_ref, place_ref, vir_rows_ref):
    row, col = here()

    @pl.when(pl.program_id(0) == 0)
    def _():
        source, held, block = lane_map(row, (1, 256), 1)
        keep = jnp.zeros((1, 256), jnp.int32)
        for k, r in enumerate(slot_rows(row)):
            keep = jnp.where(block == k, occ_ref[row, r], keep)
        keep = jnp.where(held, keep, 0)
        place_ref[...] = jnp.where(iota((240, 256), 0) == source, keep, 0).astype(F32).astype(BF)
        pair = (iota((64, 256), 0) % 32) // 2
        vir = jnp.zeros((64, 256), jnp.int32)
        for k in range(16):
            vir = jnp.where(pair == k, vir_ref[col, k], vir)
        vir_rows_ref[...] = vir.astype(F32)

    value = dot(amp_ref[...], place_ref[...])
    value = value.reshape(6, 64, 256) * vir_rows_ref[...][None]
    out_ref[...] = value.reshape(384, 256).astype(BF)


def prepare(occ_map, vir_map, amp):
    return pl.pallas_call(
        prepare_kernel,
        grid=(5,),
        out_shape=jax.ShapeDtypeStruct((1920, 256), BF),
        in_specs=[SMEM, SMEM, pl.BlockSpec((384, 240), lambda i: (i, 0))],
        out_specs=pl.BlockSpec((384, 256), lambda i: (i, 0)),
        scratch_shapes=[pltpu.VMEM((240, 256), BF), pltpu.VMEM((64, 256), F32)],
        compiler_params=PARAMS,
        cost_estimate=cost(2 * 1920 * 256 * 256, 2000000),
        name="prepare",
    )(occ_map, vir_map, amp)


def regroup_matrix():
    o, s = iota((256, 256), 0), iota((256, 256), 1)
    return jnp.where((s % 32 == o // 8) & (s // 32 == o % 8), 1.0, 0.0).astype(BF)


def regroup(perm, source, count, width):
    for first in range(0, count, 16):
        halves = []
        for m in (first, first + 8):
            n = min(count - m, 8) * 32
            halves.append(dot(perm[:, 0:n], source[pl.ds(m * 32, n), :]).reshape(32, 8, width))
        yield first, jnp.concatenate(halves, axis=1).astype(BF)


def prepare_b_kernel(cyc_ref, pp_ref, out_ref):
    for first, part in regroup(regroup_matrix(), cyc_ref, 30, 480):
        out_ref[:, pl.ds(first, 16), 0:480] = part
    for q in range(4):
        out_ref[pl.ds(2 * q, 2), :, 480:512] = pp_ref[:, q * 32:(q + 1) * 32].reshape(2, 32, 32)
    out_ref[8:32, :, 480:512] = jnp.zeros((24, 32, 32), BF)


def prepare_b(cyc, pp_t):
    return pl.pallas_call(
        prepare_b_kernel,
        out_shape=jax.ShapeDtypeStruct((32, 32, 512), BF),
        in_specs=[VMEM] * 2,
        out_specs=VMEM,
        compiler_params=PARAMS,
        cost_estimate=cost(2 * 10**8, 2 * 10**6),
        name="prepare_b",
    )(cyc, pp_t)


def slot_of(row, other):
    dx = (other // 2 - row // 2 + 4) % 4
    base = jnp.where(dx == 0, 0, jnp.where(dx == 3, 1, jnp.where(dx == 1, 2, 3)))
    return base + 4 * ((other + row) % 2)


def fetch_b(pieces, vmem, sems, col):
    core = col % 2
    copies = []
    for k, place in enumerate((0, 1 + core, 2 - core, 3)):
        at = pl.ds(pl.multiple_of(place * 32, 32), 32)
        copies.append(pltpu.make_async_copy(pieces[k], vmem.at[:, at, :], sems.at[k]))
        copies[-1].start()
    return copies


def cycle_product(left, right, lanes, start=None):
    total = start
    step = 2048 // (lanes[1] - lanes[0])
    for c in range(0, 32, step):
        l = jnp.concatenate([left(c + d)[:, lanes[0]:lanes[1]] for d in range(step)], axis=1)
        r = right[pl.ds(c, step), :, :].reshape(2048, 512)
        value = dot(l, r)
        total = value if total is None else total + value
    return total


def ladder_weights(v_ref, row, ids):
    s, d = iota((128, 128), 0), iota((128, 128), 1)
    tiles = []
    for pair in range(0, len(ids), 2):
        tile = jnp.zeros((64, 128), F32)
        for half in range(2):
            p = ids[pair + half]
            slot = slot_of(row, p // 2)
            for a in range(2):
                values = v_ref[slot, pl.ds((p % 2) * 4 + a * 2, 2), :, :].reshape(64, 128)
                move = jnp.where((s >= 96) & (d == s - 96 + half * 64 + a * 32), 1.0, 0.0).astype(BF)
                tile = tile + dot(values, move)
        tiles.append(tile.astype(BF))
    return jnp.concatenate(tiles, axis=1)


def ladder_product(weights, pieces, start, out):
    def step(i, _):
        at = pl.ds(pl.multiple_of(i * 64, 64), 64)
        right = jnp.concatenate([p[at, :] for p in pieces], axis=0)
        value = dot(weights, right)
        out[at, :] = value if start is None else value + start[at, :]
        return 0

    lax.fori_loop(0, 30, step, 0, unroll=5)


def partial_kernel(*refs):
    pieces, b_refs, (late_ref, acc_ref, a_ref, b_vmem, sems) = refs[:4], refs[4:8], refs[8:]
    _, col = here()
    copies = fetch_b(b_refs, b_vmem, sems, col)
    perm = regroup_matrix()
    for n, piece in enumerate(pieces):
        for m, part in regroup(perm, piece, 60, 256):
            a_ref[:, pl.ds(n * 64 + m, 16), :] = part[:, :, 0:128]
            late_ref[:, pl.ds(n * 64 + m, 16), :] = part[:, :, 128:256]
    for copy in copies:
        copy.wait()
    acc_ref[...] = cycle_product(lambda c: a_ref[c], b_vmem, (0, 128))


def partial_products(name, pieces, b_early):
    return pl.pallas_call(
        partial_kernel,
        out_shape=(jax.ShapeDtypeStruct((32, 256, 128), BF), jax.ShapeDtypeStruct((256, 512), F32)),
        in_specs=[VMEM] * 4 + [ANY] * 4,
        out_specs=(VMEM,) * 2,
        scratch_shapes=[
            pltpu.VMEM((32, 256, 128), BF),
            pltpu.VMEM((32, 128, 512), BF),
            pltpu.SemaphoreType.DMA((4,)),
        ],
        compiler_params=PARAMS,
        cost_estimate=cost(3 * 10**9, 12 * 10**6),
        name="partial_" + name,
    )(*pieces, *b_early)


def ladder_kernel(names, *refs):
    count = len(names)
    pieces, b_refs, (out_ref, a_vmem, v_vmem, a_sems, v_sems) = refs[:count], refs[count:count + 8], refs[count + 8:]
    row, col = here()
    core = col % 2
    slots = [0, 1 + core, 2 - core, 3, 4, 5 + core, 6 - core, 7]
    v_copies = [
        pltpu.make_async_copy(b_refs[k].at[0:8, :, 384:512], v_vmem.at[slots[k]], v_sems.at[k]) for k in range(8)
    ]
    a_copies = [pltpu.make_async_copy(pieces[k], a_vmem.at[k], a_sems.at[k]) for k in range(count)]
    for copy in v_copies + a_copies:
        copy.start()
    for copy in v_copies:
        copy.wait()
    ids = piece_ids(col)
    for first in range(0, count, 4):
        for k in range(first, first + 4):
            a_copies[k].wait()
        weights = ladder_weights(v_vmem, row, [ids[n] for n in names[first:first + 4]])
        parts = [a_vmem.at[k] for k in range(first, first + 4)]
        ladder_product(weights, parts, None if first == 0 else out_ref, out_ref)


def ladder_part(names, pieces, b_all):
    count = len(names)
    return pl.pallas_call(
        functools.partial(ladder_kernel, names),
        out_shape=jax.ShapeDtypeStruct((1920, 256), F32),
        in_specs=[ANY] * (count + 8),
        out_specs=VMEM,
        scratch_shapes=[
            pltpu.VMEM((count, 1920, 256), BF),
            pltpu.VMEM((8, 8, 32, 128), BF),
            pltpu.SemaphoreType.DMA((count,)),
            pltpu.SemaphoreType.DMA((8,)),
        ],
        compiler_params=PARAMS,
        cost_estimate=cost(3 * 10**9, 14 * 10**6),
        name="ladder_part",
    )(*pieces, *b_all)


def last_kernel(names, *refs):
    refs = list(refs)

    def take(n):
        out = refs[:n]
        del refs[:n]
        return out

    pieces, b_refs, lates, accs, (lad_in,) = take(4), take(8), take(3), take(3), take(1)
    lad_out, cyc_out = take(2)
    a_ref, b_early, b_late, v_vmem, late_vmem, c_ref, lad_ref, sems, b_sems, v_sems = refs
    row, col = here()
    core = col % 2
    late_copies = fetch_b(b_refs[4:8], b_late, b_sems.at[1], col)
    copies = [pltpu.make_async_copy(lates[k], late_vmem.at[k], sems.at[k]) for k in range(3)]
    for copy in copies:
        copy.start()
    early_copies = fetch_b(b_refs[0:4], b_early, b_sems.at[0], col)
    slots = [0, 1 + core, 2 - core, 3, 4, 5 + core, 6 - core, 7]
    v_copies = [
        pltpu.make_async_copy(b_refs[k].at[0:8, :, 384:512], v_vmem.at[slots[k]], v_sems.at[k]) for k in range(8)
    ]
    for copy in v_copies:
        copy.start()
    ids = piece_ids(col)
    perm = regroup_matrix()
    for n, piece in enumerate(pieces):
        for m, part in regroup(perm, piece, 60, 256):
            a_ref[:, pl.ds(n * 64 + m, 16), :] = part
    for copy in late_copies:
        copy.wait()
    for k in range(3):
        copies[k].wait()
        total = cycle_product(lambda c: late_vmem[k, c], b_late, (0, 128), accs[k][...])
        c_ref[pl.ds(k * 256, 256), :] = total.astype(BF)
    total = cycle_product(lambda c: a_ref[c], b_late, (128, 256))
    for copy in early_copies:
        copy.wait()
    total = cycle_product(lambda c: a_ref[c], b_early, (0, 128), total)
    c_ref[pl.ds(768, 256), :] = total.astype(BF)
    for copy in v_copies:
        copy.wait()
    ladder_product(ladder_weights(v_vmem, row, [ids[n] for n in names[12:]]), pieces, lad_in, lad_ref)
    source, held, _ = lane_map(row, (256, 1), 0)
    back = jnp.where((iota((256, 240), 1) == source) & held, 1.0, 0.0).astype(BF)
    lad_out[...] = dot(lad_ref[...].astype(BF), back).astype(BF)
    o, s = iota((256, 256), 0), iota((256, 256), 1)
    target = jnp.zeros((256, 256), jnp.int32)
    for k, name in enumerate(names):
        target = jnp.where(s // 16 == k, ids[name], target)
    target = ((s % 16) // 2) * 32 + target * 2 + s % 2
    spread = jnp.where(o == target, 1.0, 0.0).astype(BF)
    for g in range(4):
        block = jnp.concatenate([c_ref[pl.ds(k * 64 + g * 16, 16), :] for k in range(16)], axis=0)
        n = 256 if g < 3 else 192
        cyc_out[pl.ds(g * 256, n), :] = dot(spread[0:n], block)[:, 0:480].astype(BF)


def last_products(names, pieces, b_all, lates, accs, lad):
    return pl.pallas_call(
        functools.partial(last_kernel, names),
        out_shape=(jax.ShapeDtypeStruct((1920, 240), BF), jax.ShapeDtypeStruct((960, 480), BF)),
        in_specs=[VMEM] * 4 + [ANY] * 11 + [VMEM] * 4,
        out_specs=(VMEM,) * 2,
        scratch_shapes=[
            pltpu.VMEM((32, 256, 256), BF),
            pltpu.VMEM((32, 128, 512), BF),
            pltpu.VMEM((32, 128, 512), BF),
            pltpu.VMEM((8, 8, 32, 128), BF),
            pltpu.VMEM((3, 32, 256, 128), BF),
            pltpu.VMEM((1024, 512), BF),
            pltpu.VMEM((1920, 256), F32),
            pltpu.SemaphoreType.DMA((3,)),
            pltpu.SemaphoreType.DMA((2, 4)),
            pltpu.SemaphoreType.DMA((8,)),
        ],
        compiler_params=PARAMS,
        cost_estimate=cost(9 * 10**9, 26 * 10**6),
        name="last",
    )(*pieces, *b_all, *lates, *accs, lad)


def permute(value, move):
    pairs = []
    for row in range(8):
        for col in range(16):
            x, y, z, core = move(row // 2, (row % 2) * 2 + (col // 2) % 2, col // 4, col % 2)
            x, y, z = x % 4, y % 4, z % 4
            pairs.append((row * 16 + col, (x * 2 + y // 2) * 16 + z * 4 + (y % 2) * 2 + core))
    return lax.ppermute(value, ("row", "col"), pairs)


KINDS = {
    "z": lambda x, y, z, c: (x, y, z + 1 - 2 * c, c),
    "x": lambda x, y, z, c: (x + 1 - 2 * c, y, z, c),
    "near": lambda x, y, z, c: (x, y ^ 1, z, c),
    "far": lambda x, y, z, c: (x, y + 2, z, c),
    "swap": lambda x, y, z, c: (x, y, z, 1 - c),
}

AHEAD = 5

MOVES = (
    ("s_b", "swap", "b"),
    ("bq", "far", "b"),
    ("d1", "x", "b"),
    ("s_a", "swap", "a"),
    ("d2", "x", "s_b"),
    ("c1", "z", "a"),
    ("s_bq", "swap", "bq"),
    ("aq", "near", "a"),
    ("c2", "z", "s_a"),
    ("d5", "x", "d1"),
    ("dq1", "x", "bq"),
    ("c5", "z", "c1"),
    ("cq1", "z", "aq"),
    ("s_d2", "swap", "d2"),
    ("s_aq", "swap", "aq"),
    ("s_c1", "swap", "c1"),
    ("dq2", "x", "s_bq"),
    ("cq5", "z", "cq1"),
    ("s_c5", "swap", "c5"),
    ("dq5", "x", "dq1"),
    ("P1", "kernel", 1),
    ("s_cq1", "swap", "cq1"),
    ("cq2", "z", "s_aq"),
    ("P0", "kernel", 0),
    ("s_dq2", "swap", "dq2"),
    ("P2", "kernel", 2),
    ("s_cq2", "swap", "cq2"),
    ("s_cq5", "swap", "cq5"),
    ("s_c2", "swap", "c2"),
)

SETS = (
    ("a", "s_a", "c1", "aq"),
    ("c2", "c5", "cq1", "s_aq"),
    ("s_c1", "cq5", "s_c5", "s_cq1"),
    ("cq2", "s_cq2", "s_cq5", "s_c2"),
)

B_NAMES = ("b", "d1", "s_d2", "d5", "bq", "dq1", "s_dq2", "dq5")

GATES = {"s_cq1": ("P1",), "s_dq2": ("P0",), "s_cq2": ("P2",)}


def on_device(amplitudes, pp_integrals, cycle_integrals, occ_map, vir_map):
    amp = jnp.transpose(amplitudes, (0, 2, 1)).reshape(1920, 240)
    have = {
        "b": prepare_b(cycle_integrals.reshape(960, 480), pp_integrals.T),
        "a": prepare(occ_map, vir_map, amp),
    }
    parts = {}

    def partial(k):
        parts[k] = partial_products(SETS[k][0], [have[n] for n in SETS[k]], [have[n] for n in B_NAMES[:4]])

    order = []
    for name, kind, source in MOVES:
        if kind == "kernel":
            partial(source)
            have[name] = parts[source][1]
            continue
        value = have[source]
        gates = [have[order[-AHEAD]]] if len(order) >= AHEAD else []
        gates += [have[g] for g in GATES.get(name, ())]
        if gates:
            value = lax.optimization_barrier((value, *gates))[0]
        with jax.named_scope(name):
            have[name] = permute(value, KINDS[kind])
        order.append(name)
    for k in range(3):
        if k not in parts:
            partial(k)
    b_all = [have[n] for n in B_NAMES]
    names = sum(SETS, ())
    lad = ladder_part(names[:12], [have[n] for n in names[:12]], b_all)
    lates, accs = [parts[k][0] for k in range(3)], [parts[k][1] for k in range(3)]
    ladder, cycle_out = last_products(names, [have[n] for n in SETS[3]], b_all, lates, accs, lad)
    ladder = jnp.transpose(ladder.reshape(30, 64, 240), (0, 2, 1))
    return ladder, cycle_out.reshape(30, 32, 480)


def solution(mesh):
    in_specs = (P("row", None, "col"), P("row", "col"), P("row", None, "col"), P(), P())
    out_specs = (P("row", None, "col"), P("row", None, "col"))
    return jax.shard_map(
        on_device, mesh=mesh, in_specs=in_specs, out_specs=out_specs, check_vma=False
    )
```

time: 267 us -> 136 us (0.51)
  waiting for transfers between devices: 134 us -> 45.2 us
  matrix products: 58.7 us -> 0 us
  Pallas kernels: 0 us -> 53.5 us
  blocking collectives: 30.8 us -> 0 us
  starting transfers between devices: 0.08 us -> 28.5 us
  local copies, waits for them, and re-layouts: 25.5 us -> 5.89 us
  between operations: 14.1 us -> 1.06 us
    all_gather x2 -> x0, waiting for transfers between devices: 133 us -> none  [the longest x1 74 us: on_device(): cycle_panel = lax.all_gather(cycle_integrals, 'row', axis=0, tiled=True)]
    dot_general x2 -> x0, matrix products: 58.7 us -> none  [the longest x1 48.8 us: on_device(): jnp.einsum('ikac,kcm->iam', piece_four, cycle_panel, preferred_element_ty...]
    pallas_call x0 -> x7, Pallas kernels: none -> 53.5 us  [the longest x3 19.1 us: partial_products(): pl.pallas_call(partial_kernel, out_shape=(jax.ShapeDtypeStruct((32, 256,...]
    ppermute x0 -> x26, waiting for transfers between devices: none -> 45.2 us  [permute(): return lax.ppermute(value, ('row', 'col'), pairs)]
    all_gather x1 -> x0, blocking collectives: 30.8 us -> none  [on_device(): pp_panel = lax.all_gather(pp_integrals, 'row', axis=0, tiled=True)]
    ppermute x0 -> x26, starting transfers between devices: none -> 28.5 us  [permute(): return lax.ppermute(value, ('row', 'col'), pairs)]
    all_gather x1 -> x0, local copies, waits for them, and re-layouts: 19.5 us -> none  [on_device(): piece = lax.all_gather(masked, 'col', axis=2, tiled=True)]
    unnamed x2 -> x40, local copies, waits for them, and re-layouts: 2.25 us -> 5.89 us
  transfers between devices with their start and end apart: 2 -> 26, of which waited for: 2 -> 5; matrix products, arithmetic and copies ran while one was open for 12% -> 0% of each run, Pallas kernels for 0% -> 26%
where the time goes in v2:
time: 136 us; the launch traced here: 134 us
  Pallas kernels  53.5 us (39%)
  waiting for transfers between devices  45.2 us (33%)
  starting transfers between devices  28.5 us (21%)
  local copies, waits for them, and re-layouts  5.89 us (4%)
    ppermute x26, waiting for transfers between devices, permute(): return lax.ppermute(value, ('row', 'col'), pairs)  45.2 us
    ppermute x26, starting transfers between devices, permute(): return lax.ppermute(value, ('row', 'col'), pairs)  28.5 us
    pallas_call x3, Pallas kernels, partial_products(): pl.pallas_call(partial_kernel, out_shape=(jax.ShapeDtypeStruct((32, 256,...  19.1 us
    pallas_call x1, Pallas kernels, last_products(): pl.pallas_call(functools.partial(last_kernel, names), out_shape=(jax.Shap...  16.3 us
    pallas_call x1, Pallas kernels, ladder_part(): pl.pallas_call(functools.partial(ladder_kernel, names), out_shape=jax.Sha...  10.9 us
    unnamed x40, local copies, waits for them, and re-layouts  5.89 us
    pallas_call x1, Pallas kernels, prepare(): pl.pallas_call(prepare_kernel, grid=(5,), out_shape=jax.ShapeDtypeStruct(...  4.48 us
  transfers between devices with their start and end apart: 26, of which 5 were waited for; matrix products, arithmetic and copies ran while one was open for 0% of the time, Pallas kernels for 26%

profile of v2, /device:TPU:0, one launch (start us, length us, event | category | flops | bytes accessed | tf_op | source)
XLA Modules:
  0.0 134.2 jit_solution(7014876148215980364)
XLA Ops:
  0.6 2.6 %prepare_b.1.refs_4_.refs_12_ = bf16[32,32,512]{2,1,0:T(8,128)(2,1)} custom-call(bf16[960,480]{1,0:T(8,128)(2,1)} %bitcast.9, bf16[64,128]{1,0:T(8,128)(2,1)} %bitcast.11), custom_call_target="tpu_custom_call" | custom-call | flops 200000000 | bytes 2000000 | tf_op jit(solution)/shard_map/prepare_b/pallas_call | solution.py:120
  3.3 3.3 %collective-permute-start.6 = (bf16[32,32,512]{2,1,0:T(8,128)(2,1)}, bf16[32,32,512]{2,1,0:T(8,128)(2,1)S(1)}, u32[]{:S(2)}, u32[]{:S(2)}) collective-permute-start(bf16[32,32,512]{2,1,0:T(8,128)(2,1)} %prepare_b.1.refs_4_.refs_12_), channel_id=1, source_target_pairs={{0,16},{1,17},{2,18},{3,19},{4,20},{5,21},{6,22},{7,23},{8,24},{9,... | collective-permute-start | bytes 3145736 | tf_op jit(solution)/shard_map/bq/ppermute | solution.py:347
  6.5 1.5 %collective-permute-start = (bf16[32,32,512]{2,1,0:T(8,128)(2,1)}, bf16[32,32,512]{2,1,0:T(8,128)(2,1)S(1)}, u32[]{:S(2)}, u32[]{:S(2)}) collective-permute-start(bf16[32,32,512]{2,1,0:T(8,128)(2,1)} %prepare_b.1.refs_4_.refs_12_), channel_id=1, source_target_pairs={{0,32},{1,97},{2,34},{3,99},{4,36},{5,101},{6,38},{7,103},{8,40},{... | collective-permute-start | bytes 3145736 | tf_op jit(solution)/shard_map/d1/ppermute | solution.py:347
  8.0 1.5 %collective-permute-start.3 = (bf16[32,32,512]{2,1,0:T(8,128)(2,1)S(1)}, bf16[32,32,512]{2,1,0:T(8,128)(2,1)S(1)}, u32[]{:S(2)}, u32[]{:S(2)}) collective-permute-start(bf16[32,32,512]{2,1,0:T(8,128)(2,1)S(1)} %collective-permute-done.2), channel_id=1, source_target_pairs={{0,32},{1,97},{2,34},{3,99},{4,36},{5,101},{6,38},{7,103},{8,40},{... | collective-permute-start | bytes 3145736 | tf_op jit(solution)/shard_map/d2/ppermute | solution.py:347
  9.5 4.5 %prepare.1.refs_0_ = bf16[1920,256]{1,0:T(8,128)(2,1)} custom-call(s32[8,8]{1,0:T(8,128)} %occ_ref.1, s32[16,16]{1,0:T(8,128)} %vir_ref.1, bf16[1920,240]{1,0:T(8,128)(2,1)} %bitcast.10), custom_call_target="tpu_custom_call" | custom-call | flops 251658240 | bytes 2000000 | tf_op jit(solution)/shard_map/prepare/pallas_call | solution.py:84
  14.3 1.9 %collective-permute-start.8 = (bf16[1920,256]{1,0:T(8,128)(2,1)}, bf16[1920,256]{1,0:T(8,128)(2,1)S(1)}, u32[]{:S(2)}, u32[]{:S(2)}) collective-permute-start(bf16[1920,256]{1,0:T(8,128)(2,1)} %prepare.1.refs_0_), channel_id=1, source_target_pairs={{0,4},{1,13},{2,6},{3,15},{4,8},{5,1},{6,10},{7,3},{8,12},{9,5},{1... | collective-permute-start | bytes 2949128 | tf_op jit(solution)/shard_map/c1/ppermute | solution.py:347
  16.2 14.4 %collective-permute-done.6.refs_16_.refs_8_ = bf16[32,32,512]{2,1,0:T(8,128)(2,1)S(1)} collective-permute-done((bf16[32,32,512]{2,1,0:T(8,128)(2,1)}, bf16[32,32,512]{2,1,0:T(8,128)(2,1)S(1)}, u32[]{:S(2)}, u32[]{:S(2)}) %collective-permute-start.6) | collective-permute-done | bytes 1048608 | tf_op jit(solution)/shard_map/bq/ppermute | solution.py:347
  30.6 2.0 %collective-permute-start.13 = (bf16[1920,256]{1,0:T(8,128)(2,1)S(1)}, bf16[1920,256]{1,0:T(8,128)(2,1)S(1)}, u32[]{:S(2)}, u32[]{:S(2)}) collective-permute-start(bf16[1920,256]{1,0:T(8,128)(2,1)S(1)} %collective-permute-done.12.refs_1_), channel_id=1, source_target_pairs={{0,4},{1,13},{2,6},{3,15},{4,8},{5,1},{6,10},{7,3},{8,12},{9,5},{1... | collective-permute-start | bytes 2949128 | tf_op jit(solution)/shard_map/c2/ppermute | solution.py:347
  32.6 1.4 %collective-permute-done.3 = bf16[32,32,512]{2,1,0:T(8,128)(2,1)S(1)} collective-permute-done((bf16[32,32,512]{2,1,0:T(8,128)(2,1)S(1)}, bf16[32,32,512]{2,1,0:T(8,128)(2,1)S(1)}, u32[]{:S(2)}, u32[]{:S(2)}) %collective-permute-start.3) | collective-permute-done | bytes 1048608 | tf_op jit(solution)/shard_map/d2/ppermute | solution.py:347
  34.3 1.5 %collective-permute-start.1 = (bf16[1920,256]{1,0:T(8,128)(2,1)}, bf16[1920,256]{1,0:T(8,128)(2,1)S(1)}, u32[]{:S(2)}, u32[]{:S(2)}) collective-permute-start(bf16[1920,256]{1,0:T(8,128)(2,1)} %prepare.1.refs_0_), channel_id=1, source_target_pairs={{0,2},{1,3},{2,0},{3,1},{4,6},{5,7},{6,4},{7,5},{8,10},{9,11},{10,... | collective-permute-start | bytes 2949128 | tf_op jit(solution)/shard_map/aq/ppermute | solution.py:347
  35.8 1.6 %collective-permute-start.16 = (bf16[32,32,512]{2,1,0:T(8,128)(2,1)S(1)}, bf16[32,32,512]{2,1,0:T(8,128)(2,1)S(1)}, u32[]{:S(2)}, u32[]{:S(2)}) collective-permute-start(bf16[32,32,512]{2,1,0:T(8,128)(2,1)S(1)} %collective-permute-done.6.refs_16_.refs_8_), channel_id=1, source_target_pairs={{0,32},{1,97},{2,34},{3,99},{4,36},{5,101},{6,38},{7,103},{8,40},{... | collective-permute-start | bytes 3145736 | tf_op jit(solution)/shard_map/dq1/ppermute | solution.py:347
  37.4 1.9 %collective-permute-start.9 = (bf16[1920,256]{1,0:T(8,128)(2,1)S(1)}, bf16[1920,256]{1,0:T(8,128)(2,1)S(1)}, u32[]{:S(2)}, u32[]{:S(2)}) collective-permute-start(bf16[1920,256]{1,0:T(8,128)(2,1)S(1)} %collective-permute-done.8.refs_2_), channel_id=1, source_target_pairs={{0,4},{1,13},{2,6},{3,15},{4,8},{5,1},{6,10},{7,3},{8,12},{9,5},{1... | collective-permute-start | bytes 2949128 | tf_op jit(solution)/shard_map/c5/ppermute | solution.py:347
  39.3 7.5 %collective-permute-done.13.refs_0_.refs_4_ = bf16[1920,256]{1,0:T(8,128)(2,1)S(1)} collective-permute-done((bf16[1920,256]{1,0:T(8,128)(2,1)S(1)}, bf16[1920,256]{1,0:T(8,128)(2,1)S(1)}, u32[]{:S(2)}, u32[]{:S(2)}) %collective-permute-start.13) | collective-permute-done | bytes 983072 | tf_op jit(solution)/shard_map/c2/ppermute | solution.py:347
  46.8 10.0 %collective-permute-done.1.refs_3_ = bf16[1920,256]{1,0:T(8,128)(2,1)S(1)} collective-permute-done((bf16[1920,256]{1,0:T(8,128)(2,1)}, bf16[1920,256]{1,0:T(8,128)(2,1)S(1)}, u32[]{:S(2)}, u32[]{:S(2)}) %collective-permute-start.1) | collective-permute-done | bytes 983072 | tf_op jit(solution)/shard_map/aq/ppermute | solution.py:347
  56.8 3.9 %collective-permute-start.18 = (bf16[1920,256]{1,0:T(8,128)(2,1)S(1)}, bf16[1920,256]{1,0:T(8,128)(2,1)}, u32[]{:S(2)}, u32[]{:S(2)}) collective-permute-start(bf16[1920,256]{1,0:T(8,128)(2,1)S(1)} %collective-permute-done.1.refs_3_), channel_id=1, source_target_pairs={{0,4},{1,13},{2,6},{3,15},{4,8},{5,1},{6,10},{7,3},{8,12},{9,5},{1... | collective-permute-start | bytes 2949128 | tf_op jit(solution)/shard_map/cq1/ppermute | solution.py:347
  60.7 2.3 %collective-permute-start.5 = (bf16[1920,256]{1,0:T(8,128)(2,1)S(1)}, bf16[1920,256]{1,0:T(8,128)(2,1)}, u32[]{:S(2)}, u32[]{:S(2)}) collective-permute-start(bf16[1920,256]{1,0:T(8,128)(2,1)S(1)} %collective-permute-done.1.refs_3_), channel_id=1, source_target_pairs={{0,1},{1,0},{2,3},{3,2},{4,5},{5,4},{6,7},{7,6},{8,9},{9,8},{10,11... | collective-permute-start | bytes 2949128 | tf_op jit(solution)/shard_map/s_aq/ppermute | solution.py:347
  63.1 11.9 %collective-permute-done.18.refs_2_.refs_6_ = bf16[1920,256]{1,0:T(8,128)(2,1)} collective-permute-done((bf16[1920,256]{1,0:T(8,128)(2,1)S(1)}, bf16[1920,256]{1,0:T(8,128)(2,1)}, u32[]{:S(2)}, u32[]{:S(2)}) %collective-permute-start.18) | collective-permute-done | bytes 983072 | tf_op jit(solution)/shard_map/cq1/ppermute | solution.py:347
  75.1 0.9 copy-done.4
  76.0 6.4 %partial_c2.1 = (bf16[32,256,128]{2,1,0:T(8,128)(2,1)}, f32[256,512]{1,0:T(8,128)}) custom-call(bf16[1920,256]{1,0:T(8,128)(2,1)} %copy-done.9, bf16[1920,256]{1,0:T(8,128)(2,1)} %copy-done.12, bf16[1920,256]{1,0:T(8,128)(2,1)} %collective-permute-done.18.refs_2_.refs_6_, bf16[1920,256]{1,0:T(8,128)(2,1)} %collective-permute-done.5.refs_3_.refs_7_, ...), custom_call_target="tpu_custom_call" | custom-call | flops 3000000000 | bytes 12000000 | tf_op jit(solution)/shard_map/partial_c2/pallas_call | solution.py:200
  82.4 2.6 %collective-permute-start.20 = (bf16[1920,256]{1,0:T(8,128)(2,1)}, bf16[1920,256]{1,0:T(8,128)(2,1)S(1)}, u32[]{:S(2)}, u32[]{:S(2)}) collective-permute-start(bf16[1920,256]{1,0:T(8,128)(2,1)} %collective-permute-done.18.refs_2_.refs_6_), channel_id=1, source_target_pairs={{0,1},{1,0},{2,3},{3,2},{4,5},{5,4},{6,7},{7,6},{8,9},{9,8},{10,11... | collective-permute-start | bytes 2949128 | tf_op jit(solution)/shard_map/s_cq1/ppermute | solution.py:347
  85.4 6.4 %partial_a.1 = (bf16[32,256,128]{2,1,0:T(8,128)(2,1)}, f32[256,512]{1,0:T(8,128)}) custom-call(bf16[1920,256]{1,0:T(8,128)(2,1)} %prepare.1.refs_0_, bf16[1920,256]{1,0:T(8,128)(2,1)} %copy-done.7, bf16[1920,256]{1,0:T(8,128)(2,1)} %copy-done.8, bf16[1920,256]{1,0:T(8,128)(2,1)} %copy-done.11, bf16[32,32,512]{2,1,0:T(8,128)(2,1)} %prepare_b.1.refs_4_.refs_12_, ...), custom_call_target="tpu_custom_call" | custom-call | flops 3000000000 | bytes 12000000 | tf_op jit(solution)/shard_map/partial_a/pallas_call | solution.py:200
  91.8 2.8 %collective-permute-start.25 = (bf16[32,32,512]{2,1,0:T(8,128)(2,1)}, bf16[32,32,512]{2,1,0:T(8,128)(2,1)S(1)}, u32[]{:S(2)}, u32[]{:S(2)}) collective-permute-start(bf16[32,32,512]{2,1,0:T(8,128)(2,1)} %collective-permute-done.10), channel_id=1, source_target_pairs={{0,1},{1,0},{2,3},{3,2},{4,5},{5,4},{6,7},{7,6},{8,9},{9,8},{10,11... | collective-permute-start | bytes 3145736 | tf_op jit(solution)/shard_map/s_dq2/ppermute | solution.py:347
  94.7 0.8 copy-done.13
  95.6 0.9 copy-done.14
  96.5 6.4 %partial_s_c1.1 = (bf16[32,256,128]{2,1,0:T(8,128)(2,1)}, f32[256,512]{1,0:T(8,128)}) custom-call(bf16[1920,256]{1,0:T(8,128)(2,1)} %collective-permute-done.17.refs_0_.refs_8_, bf16[1920,256]{1,0:T(8,128)(2,1)} %collective-permute-done.19.refs_1_.refs_9_, bf16[1920,256]{1,0:T(8,128)(2,1)} %copy-done.14, bf16[1920,256]{1,0:T(8,128)(2,1)} %copy-done.13, ...), custom_call_target="tpu_custom_call" | custom-call | flops 3000000000 | bytes 12000000 | tf_op jit(solution)/shard_map/partial_s_c1/pallas_call | solution.py:200
  103.1 0.5 collective-permute-start.23
  103.5 0.6 copy-done.5
  104.2 1.0 copy-done.6
  105.1 10.9 %ladder_part.1.refs_18_ = f32[1920,256]{1,0:T(8,128)} custom-call(bf16[1920,256]{1,0:T(8,128)(2,1)} %prepare.1.refs_0_, bf16[1920,256]{1,0:T(8,128)(2,1)} %copy-done.7, bf16[1920,256]{1,0:T(8,128)(2,1)} %copy-done.8, bf16[1920,256]{1,0:T(8,128)(2,1)} %copy-done.11, bf16[1920,256]{1,0:T(8,128)(2,1)} %copy-done.9, bf16[1920,256]{1,0:T(8,128)(2,1)} %copy-done.12, ...), custom_call_target="tpu_custom_call" | custom-call | flops 3000000000 | bytes 14000000 | tf_op jit(solution)/shard_map/ladder_part/pallas_call | solution.py:241
  116.1 0.9 copy-done.17
  117.0 0.3 copy-done.18
  117.7 16.3 %last.1 = (bf16[1920,240]{1,0:T(8,128)(2,1)}, bf16[960,480]{1,0:T(8,128)(2,1)}) custom-call(bf16[1920,256]{1,0:T(8,128)(2,1)} %copy-done.16, bf16[1920,256]{1,0:T(8,128)(2,1)} %copy-done.18, bf16[1920,256]{1,0:T(8,128)(2,1)} %copy-done.19, bf16[1920,256]{1,0:T(8,128)(2,1)} %copy-done.17, bf16[32,32,512]{2,1,0:T(8,128)(2,1)} %prepare_b.1.refs_4_.refs_12_, ...), custom_call_target="tpu_custom_call" | custom-call | flops 8999999488 | bytes 26000000 | tf_op jit(solution)/shard_map/last/pallas_call | solution.py:317
  (67 shorter events, 1.6 us)
Async XLA Ops:
  3.3 4.8 %collective-permute-start.2 = (bf16[32,32,512]{2,1,0:T(8,128)(2,1)}, bf16[32,32,512]{2,1,0:T(8,128)(2,1)S(1)}, u32[]{:S(2)}, u32[]{:S(2)}) collective-permute-start(bf16[32,32,512]{2,1,0:T(8,128)(2,1)} %prepare_b.1.refs_4_.refs_12_), channel_id=1, source_target_pairs={{0,1},{1,0},{2,3},{3,2},{4,5},{5,4},{6,7},{7,6},{8,9},{9,8},{10,11... | collective-permute-start | bytes 3145736 | tf_op jit(solution)/shard_map/s_b/ppermute | solution.py:347
  3.3 27.3 %collective-permute-start.6 = (bf16[32,32,512]{2,1,0:T(8,128)(2,1)}, bf16[32,32,512]{2,1,0:T(8,128)(2,1)S(1)}, u32[]{:S(2)}, u32[]{:S(2)}) collective-permute-start(bf16[32,32,512]{2,1,0:T(8,128)(2,1)} %prepare_b.1.refs_4_.refs_12_), channel_id=1, source_target_pairs={{0,16},{1,17},{2,18},{3,19},{4,20},{5,21},{6,22},{7,23},{8,24},{9,... | collective-permute-start | bytes 3145736 | tf_op jit(solution)/shard_map/bq/ppermute | solution.py:347
  6.5 26.1 %collective-permute-start = (bf16[32,32,512]{2,1,0:T(8,128)(2,1)}, bf16[32,32,512]{2,1,0:T(8,128)(2,1)S(1)}, u32[]{:S(2)}, u32[]{:S(2)}) collective-permute-start(bf16[32,32,512]{2,1,0:T(8,128)(2,1)} %prepare_b.1.refs_4_.refs_12_), channel_id=1, source_target_pairs={{0,32},{1,97},{2,34},{3,99},{4,36},{5,101},{6,38},{7,103},{8,40},{... | collective-permute-start | bytes 3145736 | tf_op jit(solution)/shard_map/d1/ppermute | solution.py:347
  8.0 26.0 %collective-permute-start.3 = (bf16[32,32,512]{2,1,0:T(8,128)(2,1)S(1)}, bf16[32,32,512]{2,1,0:T(8,128)(2,1)S(1)}, u32[]{:S(2)}, u32[]{:S(2)}) collective-permute-start(bf16[32,32,512]{2,1,0:T(8,128)(2,1)S(1)} %collective-permute-done.2), channel_id=1, source_target_pairs={{0,32},{1,97},{2,34},{3,99},{4,36},{5,101},{6,38},{7,103},{8,40},{... | collective-permute-start | bytes 3145736 | tf_op jit(solution)/shard_map/d2/ppermute | solution.py:347
  14.0 16.6 %collective-permute-start.12 = (bf16[1920,256]{1,0:T(8,128)(2,1)}, bf16[1920,256]{1,0:T(8,128)(2,1)S(1)}, u32[]{:S(2)}, u32[]{:S(2)}) collective-permute-start(bf16[1920,256]{1,0:T(8,128)(2,1)} %prepare.1.refs_0_), channel_id=1, source_target_pairs={{0,1},{1,0},{2,3},{3,2},{4,5},{5,4},{6,7},{7,6},{8,9},{9,8},{10,11... | collective-permute-start | bytes 2949128 | tf_op jit(solution)/shard_map/s_a/ppermute | solution.py:347
  14.3 21.5 %collective-permute-start.8 = (bf16[1920,256]{1,0:T(8,128)(2,1)}, bf16[1920,256]{1,0:T(8,128)(2,1)S(1)}, u32[]{:S(2)}, u32[]{:S(2)}) collective-permute-start(bf16[1920,256]{1,0:T(8,128)(2,1)} %prepare.1.refs_0_), channel_id=1, source_target_pairs={{0,4},{1,13},{2,6},{3,15},{4,8},{5,1},{6,10},{7,3},{8,12},{9,5},{1... | collective-permute-start | bytes 2949128 | tf_op jit(solution)/shard_map/c1/ppermute | solution.py:347
  30.6 51.8 %copy-start = (bf16[32,32,512]{2,1,0:T(8,128)(2,1)}, bf16[32,32,512]{2,1,0:T(8,128)(2,1)S(1)}, u32[]{:S(2)}) copy-start(bf16[32,32,512]{2,1,0:T(8,128)(2,1)S(1)} %collective-permute-done.6.refs_16_.refs_8_) | copy-start | bytes 3145732
  30.6 6.8 %collective-permute-start.7 = (bf16[32,32,512]{2,1,0:T(8,128)(2,1)S(1)}, bf16[32,32,512]{2,1,0:T(8,128)(2,1)}, u32[]{:S(2)}, u32[]{:S(2)}) collective-permute-start(bf16[32,32,512]{2,1,0:T(8,128)(2,1)S(1)} %collective-permute-done.6.refs_16_.refs_8_), channel_id=1, source_target_pairs={{0,1},{1,0},{2,3},{3,2},{4,5},{5,4},{6,7},{7,6},{8,9},{9,8},{10,11... | collective-permute-start | bytes 3145736 | tf_op jit(solution)/shard_map/s_bq/ppermute | solution.py:347
  30.6 54.8 %copy-start.7 = (bf16[1920,256]{1,0:T(8,128)(2,1)}, bf16[1920,256]{1,0:T(8,128)(2,1)S(1)}, u32[]{:S(2)}) copy-start(bf16[1920,256]{1,0:T(8,128)(2,1)S(1)} %collective-permute-done.12.refs_1_) | copy-start | bytes 2949124
  30.6 16.2 %collective-permute-start.13 = (bf16[1920,256]{1,0:T(8,128)(2,1)S(1)}, bf16[1920,256]{1,0:T(8,128)(2,1)S(1)}, u32[]{:S(2)}, u32[]{:S(2)}) collective-permute-start(bf16[1920,256]{1,0:T(8,128)(2,1)S(1)} %collective-permute-done.12.refs_1_), channel_id=1, source_target_pairs={{0,4},{1,13},{2,6},{3,15},{4,8},{5,1},{6,10},{7,3},{8,12},{9,5},{1... | collective-permute-start | bytes 2949128 | tf_op jit(solution)/shard_map/c2/ppermute | solution.py:347
  32.6 42.4 %copy-start.1 = (bf16[32,32,512]{2,1,0:T(8,128)(2,1)}, bf16[32,32,512]{2,1,0:T(8,128)(2,1)S(1)}, u32[]{:S(2)}) copy-start(bf16[32,32,512]{2,1,0:T(8,128)(2,1)S(1)} %collective-permute-done.refs_5_.refs_13_) | copy-start | bytes 3145732
  34.0 26.7 %collective-permute-start.4 = (bf16[32,32,512]{2,1,0:T(8,128)(2,1)S(1)}, bf16[32,32,512]{2,1,0:T(8,128)(2,1)S(1)}, u32[]{:S(2)}, u32[]{:S(2)}) collective-permute-start(bf16[32,32,512]{2,1,0:T(8,128)(2,1)S(1)} %collective-permute-done.refs_5_.refs_13_), channel_id=1, source_target_pairs={{0,32},{1,97},{2,34},{3,99},{4,36},{5,101},{6,38},{7,103},{8,40},{... | collective-permute-start | bytes 3145736 | tf_op jit(solution)/shard_map/d5/ppermute | solution.py:347
  34.3 22.5 %collective-permute-start.1 = (bf16[1920,256]{1,0:T(8,128)(2,1)}, bf16[1920,256]{1,0:T(8,128)(2,1)S(1)}, u32[]{:S(2)}, u32[]{:S(2)}) collective-permute-start(bf16[1920,256]{1,0:T(8,128)(2,1)} %prepare.1.refs_0_), channel_id=1, source_target_pairs={{0,2},{1,3},{2,0},{3,1},{4,6},{5,7},{6,4},{7,5},{8,10},{9,11},{10,... | collective-permute-start | bytes 2949128 | tf_op jit(solution)/shard_map/aq/ppermute | solution.py:347
  35.8 49.6 %copy-start.8 = (bf16[1920,256]{1,0:T(8,128)(2,1)}, bf16[1920,256]{1,0:T(8,128)(2,1)S(1)}, u32[]{:S(2)}) copy-start(bf16[1920,256]{1,0:T(8,128)(2,1)S(1)} %collective-permute-done.8.refs_2_) | copy-start | bytes 2949124
  35.8 27.2 %collective-permute-start.16 = (bf16[32,32,512]{2,1,0:T(8,128)(2,1)S(1)}, bf16[32,32,512]{2,1,0:T(8,128)(2,1)S(1)}, u32[]{:S(2)}, u32[]{:S(2)}) collective-permute-start(bf16[32,32,512]{2,1,0:T(8,128)(2,1)S(1)} %collective-permute-done.6.refs_16_.refs_8_), channel_id=1, source_target_pairs={{0,32},{1,97},{2,34},{3,99},{4,36},{5,101},{6,38},{7,103},{8,40},{... | collective-permute-start | bytes 3145736 | tf_op jit(solution)/shard_map/dq1/ppermute | solution.py:347
  37.4 25.7 %collective-permute-start.9 = (bf16[1920,256]{1,0:T(8,128)(2,1)S(1)}, bf16[1920,256]{1,0:T(8,128)(2,1)S(1)}, u32[]{:S(2)}, u32[]{:S(2)}) collective-permute-start(bf16[1920,256]{1,0:T(8,128)(2,1)S(1)} %collective-permute-done.8.refs_2_), channel_id=1, source_target_pairs={{0,4},{1,13},{2,6},{3,15},{4,8},{5,1},{6,10},{7,3},{8,12},{9,5},{1... | collective-permute-start | bytes 2949128 | tf_op jit(solution)/shard_map/c5/ppermute | solution.py:347
  46.8 28.3 %copy-start.9 = (bf16[1920,256]{1,0:T(8,128)(2,1)}, bf16[1920,256]{1,0:T(8,128)(2,1)S(1)}, u32[]{:S(2)}) copy-start(bf16[1920,256]{1,0:T(8,128)(2,1)S(1)} %collective-permute-done.13.refs_0_.refs_4_) | copy-start | bytes 2949124
  46.8 28.2 %collective-permute-start.14 = (bf16[32,32,512]{2,1,0:T(8,128)(2,1)}, bf16[32,32,512]{2,1,0:T(8,128)(2,1)S(1)}, u32[]{:S(2)}, u32[]{:S(2)}) collective-permute-start(bf16[32,32,512]{2,1,0:T(8,128)(2,1)} %copy-done.15), channel_id=1, source_target_pairs={{0,1},{1,0},{2,3},{3,2},{4,5},{5,4},{6,7},{7,6},{8,9},{9,8},{10,11... | collective-permute-start | bytes 3145736 | tf_op jit(solution)/shard_map/s_d2/ppermute | solution.py:347
  56.8 18.2 %collective-permute-start.18 = (bf16[1920,256]{1,0:T(8,128)(2,1)S(1)}, bf16[1920,256]{1,0:T(8,128)(2,1)}, u32[]{:S(2)}, u32[]{:S(2)}) collective-permute-start(bf16[1920,256]{1,0:T(8,128)(2,1)S(1)} %collective-permute-done.1.refs_3_), channel_id=1, source_target_pairs={{0,4},{1,13},{2,6},{3,15},{4,8},{5,1},{6,10},{7,3},{8,12},{9,5},{1... | collective-permute-start | bytes 2949128 | tf_op jit(solution)/shard_map/cq1/ppermute | solution.py:347
  60.7 14.3 %collective-permute-start.5 = (bf16[1920,256]{1,0:T(8,128)(2,1)S(1)}, bf16[1920,256]{1,0:T(8,128)(2,1)}, u32[]{:S(2)}, u32[]{:S(2)}) collective-permute-start(bf16[1920,256]{1,0:T(8,128)(2,1)S(1)} %collective-permute-done.1.refs_3_), channel_id=1, source_target_pairs={{0,1},{1,0},{2,3},{3,2},{4,5},{5,4},{6,7},{7,6},{8,9},{9,8},{10,11... | collective-permute-start | bytes 2949128 | tf_op jit(solution)/shard_map/s_aq/ppermute | solution.py:347
  63.0 22.1 %copy-start.3 = (bf16[32,32,512]{2,1,0:T(8,128)(2,1)}, bf16[32,32,512]{2,1,0:T(8,128)(2,1)S(1)}, u32[]{:S(2)}) copy-start(bf16[32,32,512]{2,1,0:T(8,128)(2,1)S(1)} %collective-permute-done.16.refs_17_.refs_9_) | copy-start | bytes 3145732
  63.0 19.4 %collective-permute-start.17 = (bf16[1920,256]{1,0:T(8,128)(2,1)S(1)}, bf16[1920,256]{1,0:T(8,128)(2,1)}, u32[]{:S(2)}, u32[]{:S(2)}) collective-permute-start(bf16[1920,256]{1,0:T(8,128)(2,1)S(1)} %collective-permute-done.8.refs_2_), channel_id=1, source_target_pairs={{0,1},{1,0},{2,3},{3,2},{4,5},{5,4},{6,7},{7,6},{8,9},{9,8},{10,11... | collective-permute-start | bytes 2949128 | tf_op jit(solution)/shard_map/s_c1/ppermute | solution.py:347
  63.1 22.0 %collective-permute-start.10 = (bf16[32,32,512]{2,1,0:T(8,128)(2,1)}, bf16[32,32,512]{2,1,0:T(8,128)(2,1)}, u32[]{:S(2)}, u32[]{:S(2)}) collective-permute-start(bf16[32,32,512]{2,1,0:T(8,128)(2,1)} %collective-permute-done.7), channel_id=1, source_target_pairs={{0,32},{1,97},{2,34},{3,99},{4,36},{5,101},{6,38},{7,103},{8,40},{... | collective-permute-start | bytes 3145736 | tf_op jit(solution)/shard_map/dq2/ppermute | solution.py:347
  75.0 16.8 %collective-permute-start.19 = (bf16[1920,256]{1,0:T(8,128)(2,1)}, bf16[1920,256]{1,0:T(8,128)(2,1)}, u32[]{:S(2)}, u32[]{:S(2)}) collective-permute-start(bf16[1920,256]{1,0:T(8,128)(2,1)} %collective-permute-done.18.refs_2_.refs_6_), channel_id=1, source_target_pairs={{0,4},{1,13},{2,6},{3,15},{4,8},{5,1},{6,10},{7,3},{8,12},{9,5},{1... | collective-permute-start | bytes 2949128 | tf_op jit(solution)/shard_map/cq5/ppermute | solution.py:347
  82.4 12.2 %collective-permute-start.20 = (bf16[1920,256]{1,0:T(8,128)(2,1)}, bf16[1920,256]{1,0:T(8,128)(2,1)S(1)}, u32[]{:S(2)}, u32[]{:S(2)}) collective-permute-start(bf16[1920,256]{1,0:T(8,128)(2,1)} %collective-permute-done.18.refs_2_.refs_6_), channel_id=1, source_target_pairs={{0,1},{1,0},{2,3},{3,2},{4,5},{5,4},{6,7},{7,6},{8,9},{9,8},{10,11... | collective-permute-start | bytes 2949128 | tf_op jit(solution)/shard_map/s_cq1/ppermute | solution.py:347
  85.0 9.7 %collective-permute-start.15 = (bf16[1920,256]{1,0:T(8,128)(2,1)}, bf16[1920,256]{1,0:T(8,128)(2,1)S(1)}, u32[]{:S(2)}, u32[]{:S(2)}) collective-permute-start(bf16[1920,256]{1,0:T(8,128)(2,1)} %copy-done.12), channel_id=1, source_target_pairs={{0,1},{1,0},{2,3},{3,2},{4,5},{5,4},{6,7},{7,6},{8,9},{9,8},{10,11... | collective-permute-start | bytes 2949128 | tf_op jit(solution)/shard_map/s_c5/ppermute | solution.py:347
  85.1 17.9 %collective-permute-start.22 = (bf16[32,32,512]{2,1,0:T(8,128)(2,1)S(1)}, bf16[32,32,512]{2,1,0:T(8,128)(2,1)S(1)}, u32[]{:S(2)}, u32[]{:S(2)}) collective-permute-start(bf16[32,32,512]{2,1,0:T(8,128)(2,1)S(1)} %collective-permute-done.16.refs_17_.refs_9_), channel_id=1, source_target_pairs={{0,32},{1,97},{2,34},{3,99},{4,36},{5,101},{6,38},{7,103},{8,40},{... | collective-permute-start | bytes 3145736 | tf_op jit(solution)/shard_map/dq5/ppermute | solution.py:347
  85.1 17.8 %collective-permute-start.11 = (bf16[1920,256]{1,0:T(8,128)(2,1)}, bf16[1920,256]{1,0:T(8,128)(2,1)S(1)}, u32[]{:S(2)}, u32[]{:S(2)}) collective-permute-start(bf16[1920,256]{1,0:T(8,128)(2,1)} %collective-permute-done.5.refs_3_.refs_7_), channel_id=1, source_target_pairs={{0,4},{1,13},{2,6},{3,15},{4,8},{5,1},{6,10},{7,3},{8,12},{9,5},{1... | collective-permute-start | bytes 2949128 | tf_op jit(solution)/shard_map/cq2/ppermute | solution.py:347
  91.8 11.7 %collective-permute-start.25 = (bf16[32,32,512]{2,1,0:T(8,128)(2,1)}, bf16[32,32,512]{2,1,0:T(8,128)(2,1)S(1)}, u32[]{:S(2)}, u32[]{:S(2)}) collective-permute-start(bf16[32,32,512]{2,1,0:T(8,128)(2,1)} %collective-permute-done.10), channel_id=1, source_target_pairs={{0,1},{1,0},{2,3},{3,2},{4,5},{5,4},{6,7},{7,6},{8,9},{9,8},{10,11... | collective-permute-start | bytes 3145736 | tf_op jit(solution)/shard_map/s_dq2/ppermute | solution.py:347
  94.6 21.5 %collective-permute-start.24 = (bf16[1920,256]{1,0:T(8,128)(2,1)S(1)}, bf16[1920,256]{1,0:T(8,128)(2,1)S(1)}, u32[]{:S(2)}, u32[]{:S(2)}) collective-permute-start(bf16[1920,256]{1,0:T(8,128)(2,1)S(1)} %copy-done.10), channel_id=1, source_target_pairs={{0,1},{1,0},{2,3},{3,2},{4,5},{5,4},{6,7},{7,6},{8,9},{9,8},{10,11... | collective-permute-start | bytes 2949128 | tf_op jit(solution)/shard_map/s_c2/ppermute | solution.py:347
  103.0 13.2 %collective-permute-start.21 = (bf16[1920,256]{1,0:T(8,128)(2,1)S(1)}, bf16[1920,256]{1,0:T(8,128)(2,1)S(1)}, u32[]{:S(2)}, u32[]{:S(2)}) collective-permute-start(bf16[1920,256]{1,0:T(8,128)(2,1)S(1)} %collective-permute-done.11.refs_0_), channel_id=1, source_target_pairs={{0,1},{1,0},{2,3},{3,2},{4,5},{5,4},{6,7},{7,6},{8,9},{9,8},{10,11... | collective-permute-start | bytes 2949128 | tf_op jit(solution)/shard_map/s_cq2/ppermute | solution.py:347
  103.1 13.1 %collective-permute-start.23 = (bf16[1920,256]{1,0:T(8,128)(2,1)}, bf16[1920,256]{1,0:T(8,128)(2,1)S(1)}, u32[]{:S(2)}, u32[]{:S(2)}) collective-permute-start(bf16[1920,256]{1,0:T(8,128)(2,1)} %collective-permute-done.19.refs_1_.refs_9_), channel_id=1, source_target_pairs={{0,1},{1,0},{2,3},{3,2},{4,5},{5,4},{6,7},{7,6},{8,9},{9,8},{10,11... | collective-permute-start | bytes 2949128 | tf_op jit(solution)/shard_map/s_cq5/ppermute | solution.py:347
  (14 other events, 80.4 us)

commit v3 on v0

v3 whole, which is shorter than its diff:
```python
import functools

import jax
import jax.numpy as jnp
from jax import lax
from jax.experimental import pallas as pl
from jax.experimental.pallas import tpu as pltpu
from jax.sharding import PartitionSpec as P

BF = jnp.bfloat16
F32 = jnp.float32
PARAMS = pltpu.CompilerParams(vmem_limit_bytes=16 * 1024 * 1024)
LAST_PARAMS = pltpu.CompilerParams(vmem_limit_bytes=16 * 1024 * 1024)
VMEM = pl.BlockSpec(memory_space=pltpu.VMEM)
SMEM = pl.BlockSpec(memory_space=pltpu.SMEM)


def cost(flops, size):
    return pl.CostEstimate(flops=flops, bytes_accessed=size, transcendentals=0)


def dot(a, b):
    return jnp.dot(a, b, preferred_element_type=F32)


def iota(shape, dim):
    return lax.broadcasted_iota(jnp.int32, shape, dim)


def here():
    return lax.axis_index("row"), lax.axis_index("col")


def slot_rows(row, col):
    x, yh, e = row // 2, row % 2, 2 * (col % 2) - 1
    return [((x + dx + 4) % 4) * 2 + (yh + dy) % 2 for dy in (0, 1) for dx in (0, e, -e, 2)]


def piece_ids(col):
    z, yl, core = col // 4, (col // 2) % 2, col % 2
    e = 2 * core - 1
    near = dict(a=(0, 0), s_a=(0, 1), c1=(e, 0), c2=(e, 1), c5=(2, 0), s_c1=(-e, 1), s_c2=(-e, 0), s_c5=(2, 1))
    far = dict(aq="a", s_aq="s_a", cq1="c1", cq2="c2", cq5="c5", s_cq1="s_c1", s_cq2="s_c2", s_cq5="s_c5")
    ids = {}
    for dy in (0, 1):
        for name in far if dy else near:
            dz, dc = near[far[name] if dy else name]
            ids[name] = ((z + dz + 4) % 4) * 4 + ((yl + dy) % 2) * 2 + (core + dc) % 2
    return ids


def lane_map(row, col, shape, dim):
    lane = iota(shape, dim)
    block, t = lane // 32, lane % 32
    start = jnp.zeros(shape, jnp.int32)
    for k, r in enumerate(slot_rows(row, col)):
        start = jnp.where(block == k, r * 30, start)
    return start + t, t < 30, block


def regroup_matrix():
    o, s = iota((256, 256), 0), iota((256, 256), 1)
    return jnp.where((s % 32 == o // 8) & (s // 32 == o % 8), 1.0, 0.0)


def place_matrix(occ_ref, row, col):
    source, held, block = lane_map(row, col, (1, 256), 1)
    keep = jnp.zeros((1, 256), jnp.int32)
    for k, r in enumerate(slot_rows(row, col)):
        keep = jnp.where(block == k, occ_ref[row, r], keep)
    keep = jnp.where(held, keep, 0)
    return jnp.where(iota((240, 256), 0) == source, keep, 0).astype(F32).astype(BF)


def screened(perm, vir_ref, piece):
    k = iota((16, 256), 0)
    value = jnp.zeros((16, 256), jnp.int32)
    for n in range(16):
        value = jnp.where(k == n, vir_ref[piece, n], value)
    spread = jnp.where(iota((256, 16), 0) // 16 == iota((256, 16), 1), 1.0, 0.0).astype(BF)
    return (perm * dot(spread, value.astype(F32).astype(BF))).astype(BF)


def regroup(perm, source, count, width, place=None):
    for first in range(0, count, 16):
        halves = []
        for m in (first, first + 8):
            n = min(count - m, 8) * 32
            if place is None:
                value = source[pl.ds(m * 32, n), :]
            else:
                value = dot(source[pl.ds(m // 2, n // 64)].reshape(n, 240), place).astype(BF)
            halves.append(dot(perm[:, 0:n], value).reshape(32, 8, width))
        yield first, jnp.concatenate(halves, axis=1).astype(BF)


def regroup_pieces(occ_ref, vir_ref, names, pieces, out):
    row, col = here()
    ids = piece_ids(col)
    perm, place = regroup_matrix(), place_matrix(occ_ref, row, col)
    for n, piece in enumerate(pieces):
        own = screened(perm, vir_ref, ids[names[n]])
        for m, part in regroup(own, piece, 60, 256, place):
            out[:, pl.ds(n * 64 + m, 16), :] = part


def regroup_kernel(names, occ_ref, vir_ref, p0, p1, p2, p3, out_ref):
    regroup_pieces(occ_ref, vir_ref, names, (p0, p1, p2, p3), out_ref)


def regroup_set(names, maps, pieces):
    return pl.pallas_call(
        functools.partial(regroup_kernel, names),
        out_shape=jax.ShapeDtypeStruct((32, 256, 256), BF),
        in_specs=[SMEM] * 2 + [VMEM] * 4,
        out_specs=VMEM,
        compiler_params=PARAMS,
        cost_estimate=cost(2 * 10**9, 8 * 10**6),
        name="regroup_" + names[0],
    )(*maps, *pieces)


def prepare_b_kernel(cyc_ref, pp_ref, out_ref):
    for first, part in regroup(regroup_matrix().astype(BF), cyc_ref, 30, 480):
        out_ref[:, pl.ds(first, 16), 0:480] = part
    for q in range(4):
        out_ref[pl.ds(2 * q, 2), :, 480:512] = pp_ref[:, q * 32:(q + 1) * 32].reshape(2, 32, 32)
    out_ref[8:32, :, 480:512] = jnp.zeros((24, 32, 32), BF)


def prepare_b(cyc, pp_t):
    return pl.pallas_call(
        prepare_b_kernel,
        out_shape=jax.ShapeDtypeStruct((32, 32, 512), BF),
        in_specs=[VMEM] * 2,
        out_specs=VMEM,
        compiler_params=PARAMS,
        cost_estimate=cost(2 * 10**8, 2 * 10**6),
        name="prepare_b",
    )(cyc, pp_t)


def slot_of(row, col, other):
    dx = (other // 2 - row // 2 + 4) % 4
    core = col % 2
    base = jnp.where(dx == 0, 0, jnp.where(dx == 3, 1 + core, jnp.where(dx == 1, 2 - core, 3)))
    return base + 4 * ((other + row) % 2)


def cycle_product(left, right, start=None):
    total = start
    for c in range(0, 32, 16):
        l = jnp.concatenate([left(c + d) for d in range(16)], axis=1)
        r = jnp.concatenate([piece[c + d] for d in range(16) for piece in right], axis=0)
        value = dot(l, r)
        total = value if total is None else total + value
    return total


def ladder_weights(v_ref, vir_ref, row, col, ids):
    s, d = iota((128, 128), 0), iota((128, 128), 1)
    lane = iota((1, 128), 1)
    tiles = []
    for pair in range(0, len(ids), 2):
        tile = jnp.zeros((64, 128), F32)
        keep = jnp.zeros((1, 128), jnp.int32)
        for half in range(2):
            p = ids[pair + half]
            slot = slot_of(row, col, p // 2)
            for a in range(2):
                values = v_ref[slot, pl.ds((p % 2) * 4 + a * 2, 2), :, :].reshape(64, 128)
                move = jnp.where((s >= 96) & (d == s - 96 + half * 64 + a * 32), 1.0, 0.0).astype(BF)
                tile = tile + dot(values, move)
            for k in range(16):
                keep = jnp.where((lane // 64 == half) & ((lane % 32) // 2 == k), vir_ref[p, k], keep)
        tiles.append((tile * keep.astype(F32)).astype(BF))
    return jnp.concatenate(tiles, axis=1)


def last_kernel(names, occ_ref, vir_ref, *refs):
    refs = list(refs)

    def take(n):
        out = refs[:n]
        del refs[:n]
        return out

    pieces, b_refs, sets, (lad_out, cyc_out, v_ref, set_ref, c_ref) = take(16), take(8), take(3), refs
    row, col = here()
    ids = piece_ids(col)
    regroup_pieces(occ_ref, vir_ref, names[12:], pieces[12:], set_ref)
    for k, part in enumerate(sets + [set_ref]):
        total = cycle_product(lambda c: part[c, :, 0:128], b_refs[0:4])
        total = cycle_product(lambda c: part[c, :, 128:256], b_refs[4:8], total)
        c_ref[pl.ds(k * 256, 256), :] = total.astype(BF)
    for k in range(8):
        v_ref[k] = b_refs[k][0:8, :, 384:512]
    weights = ladder_weights(v_ref, vir_ref, row, col, [ids[n] for n in names])
    tile = iota((1, 240), 1) // 30
    keep = jnp.zeros((1, 240), jnp.int32)
    for r in range(8):
        keep = jnp.where(tile == r, occ_ref[row, r], keep)
    keep = keep.astype(F32)

    def step(i, _):
        right = jnp.concatenate([p[i] for p in pieces], axis=0)
        lad_out[i] = (dot(weights, right) * keep).astype(BF)
        return 0

    lax.fori_loop(0, 30, step, 0, unroll=3)
    o, s = iota((256, 256), 0), iota((256, 256), 1)
    target = jnp.zeros((256, 256), jnp.int32)
    for k, name in enumerate(names):
        target = jnp.where(s // 16 == k, ids[name], target)
    target = ((s % 16) // 2) * 32 + target * 2 + s % 2
    spread = jnp.where(o == target, 1.0, 0.0).astype(BF)
    for g in range(4):
        block = jnp.concatenate([c_ref[pl.ds(k * 64 + g * 16, 16), :] for k in range(16)], axis=0)
        n = 256 if g < 3 else 192
        cyc_out[pl.ds(g * 256, n), :] = dot(spread[0:n], block)[:, 0:480].astype(BF)


def last_products(names, maps, pieces, b_all, sets):
    return pl.pallas_call(
        functools.partial(last_kernel, names),
        out_shape=(jax.ShapeDtypeStruct((30, 64, 240), BF), jax.ShapeDtypeStruct((960, 480), BF)),
        in_specs=[SMEM] * 2 + [VMEM] * 27,
        out_specs=(VMEM,) * 2,
        scratch_shapes=[
            pltpu.VMEM((8, 8, 32, 128), BF),
            pltpu.VMEM((32, 256, 256), BF),
            pltpu.VMEM((1024, 512), BF),
        ],
        compiler_params=LAST_PARAMS,
        cost_estimate=cost(12 * 10**9, 38 * 10**6),
        name="last",
    )(*maps, *pieces, *b_all, *sets)


def permute(value, move):
    pairs = []
    for row in range(8):
        for col in range(16):
            x, y, z, core = move(row // 2, (row % 2) * 2 + (col // 2) % 2, col // 4, col % 2)
            x, y, z = x % 4, y % 4, z % 4
            pairs.append((row * 16 + col, (x * 2 + y // 2) * 16 + z * 4 + (y % 2) * 2 + core))
    return lax.ppermute(value, ("row", "col"), pairs)


KINDS = {
    "z": lambda x, y, z, c: (x, y, z + 1 - 2 * c, c),
    "x": lambda x, y, z, c: (x + 1 - 2 * c, y, z, c),
    "near": lambda x, y, z, c: (x, y ^ 1, z, c),
    "far": lambda x, y, z, c: (x, y + 2, z, c),
    "swap": lambda x, y, z, c: (x, y, z, 1 - c),
}

AHEAD = 5

MOVES = (
    ("s_b", "swap", "b"),
    ("s_a", "swap", "a"),
    ("c1", "z", "a"),
    ("aq", "near", "a"),
    ("c2", "z", "s_a"),
    ("d1", "x", "b"),
    ("c5", "z", "c1"),
    ("bq", "far", "b"),
    ("d2", "x", "s_b"),
    ("P0", "kernel", 0),
    ("s_aq", "swap", "aq"),
    ("cq1", "z", "aq"),
    ("d5", "x", "d1"),
    ("s_bq", "swap", "bq"),
    ("s_c5", "swap", "c5"),
    ("dq1", "x", "bq"),
    ("s_cq1", "swap", "cq1"),
    ("cq2", "z", "s_aq"),
    ("s_c1", "swap", "c1"),
    ("P1", "kernel", 1),
    ("dq2", "x", "s_bq"),
    ("s_cq2", "swap", "cq2"),
    ("cq5", "z", "cq1"),
    ("s_d2", "swap", "d2"),
    ("dq5", "x", "dq1"),
    ("P2", "kernel", 2),
    ("s_dq2", "swap", "dq2"),
    ("s_cq5", "swap", "cq5"),
    ("s_c2", "swap", "c2"),
)

SETS = (
    ("a", "s_a", "c1", "aq"),
    ("c2", "c5", "s_aq", "cq1"),
    ("s_c5", "s_cq1", "cq2", "s_c1"),
    ("s_cq2", "cq5", "s_cq5", "s_c2"),
)

B_NAMES = ("b", "d1", "s_d2", "d5", "bq", "dq1", "s_dq2", "dq5")

GATES = {"s_aq": ("P0",), "dq2": ("P1",), "s_dq2": ("P2",)}


def on_device(amplitudes, pp_integrals, cycle_integrals, occ_map, vir_map):
    maps = (occ_map, vir_map)
    have = {
        "a": jnp.transpose(amplitudes, (0, 2, 1)),
        "b": prepare_b(cycle_integrals.reshape(960, 480), pp_integrals.T),
    }
    names = sum(SETS, ())
    sets = {}
    order = []
    for name, kind, source in MOVES:
        if kind == "kernel":
            have[name] = sets[source] = regroup_set(SETS[source], maps, [have[n] for n in SETS[source]])
            continue
        value = have[source]
        gates = [have[order[-AHEAD]]] if len(order) >= AHEAD else []
        gates += [have[g] for g in GATES.get(name, ())]
        if gates:
            value = lax.optimization_barrier((value, *gates))[0]
        with jax.named_scope(name):
            have[name] = permute(value, KINDS[kind])
        order.append(name)
    ladder, cycle_out = last_products(
        names, maps, [have[n] for n in names], [have[n] for n in B_NAMES], [sets[k] for k in range(3)]
    )
    ladder = jnp.transpose(ladder, (0, 2, 1))
    return ladder, cycle_out.reshape(30, 32, 480)


def solution(mesh):
    in_specs = (P("row", None, "col"), P("row", "col"), P("row", None, "col"), P(), P())
    out_specs = (P("row", None, "col"), P("row", None, "col"))
    return jax.shard_map(
        on_device, mesh=mesh, in_specs=in_specs, out_specs=out_specs, check_vma=False
    )
```

time: 267 us -> 112 us (0.42)
  waiting for transfers between devices: 134 us -> 51.3 us
  matrix products: 58.7 us -> 0 us
  blocking collectives: 30.8 us -> 0 us
  Pallas kernels: 0 us -> 30.2 us
  starting transfers between devices: 0.08 us -> 25.2 us
  local copies, waits for them, and re-layouts: 25.5 us -> 4.5 us
  between operations: 14.1 us -> 0.75 us
    all_gather x2 -> x0, waiting for transfers between devices: 133 us -> none  [the longest x1 74 us: on_device(): cycle_panel = lax.all_gather(cycle_integrals, 'row', axis=0, tiled=True)]
    dot_general x2 -> x0, matrix products: 58.7 us -> none  [the longest x1 48.8 us: on_device(): jnp.einsum('ikac,kcm->iam', piece_four, cycle_panel, preferred_element_ty...]
    ppermute x0 -> x26, waiting for transfers between devices: none -> 51.3 us  [permute(): return lax.ppermute(value, ('row', 'col'), pairs)]
    all_gather x1 -> x0, blocking collectives: 30.8 us -> none  [on_device(): pp_panel = lax.all_gather(pp_integrals, 'row', axis=0, tiled=True)]
    pallas_call x0 -> x5, Pallas kernels: none -> 30.2 us  [the longest x1 18.2 us: last_products(): pl.pallas_call(functools.partial(last_kernel, names), out_shape=(jax.Shap...]
    ppermute x0 -> x26, starting transfers between devices: none -> 25.2 us  [permute(): return lax.ppermute(value, ('row', 'col'), pairs)]
    all_gather x1 -> x0, local copies, waits for them, and re-layouts: 19.5 us -> none  [on_device(): piece = lax.all_gather(masked, 'col', axis=2, tiled=True)]
  transfers between devices with their start and end apart: 2 -> 26, of which waited for: 2 -> 10; matrix products, arithmetic and copies ran while one was open for 12% -> 0% of each run, Pallas kernels for 0% -> 10%
where the time goes in v3:
time: 112 us
  waiting for transfers between devices  51.3 us (46%)
  Pallas kernels  30.2 us (27%)
  starting transfers between devices  25.2 us (22%)
  local copies, waits for them, and re-layouts  4.5 us (4%)
    ppermute x26, waiting for transfers between devices, permute(): return lax.ppermute(value, ('row', 'col'), pairs)  51.3 us
    ppermute x26, starting transfers between devices, permute(): return lax.ppermute(value, ('row', 'col'), pairs)  25.2 us
    pallas_call x1, Pallas kernels, last_products(): pl.pallas_call(functools.partial(last_kernel, names), out_shape=(jax.Shap...  18.2 us
    pallas_call x3, Pallas kernels, regroup_set(): pl.pallas_call(functools.partial(regroup_kernel, names), out_shape=jax.Sh...  11.6 us
    unnamed x12, local copies, waits for them, and re-layouts  4.5 us
  transfers between devices with their start and end apart: 26, of which 10 were waited for; matrix products, arithmetic and copies ran while one was open for 0% of the time, Pallas kernels for 10%

profile of v3, /device:TPU:0, one launch (start us, length us, event | category | flops | bytes accessed | tf_op | source)
XLA Modules:
  0.0 112.0 jit_solution(7858217012510741688)
XLA Ops:
  0.6 1.2 %copy-done = bf16[30,32,480]{2,1,0:T(8,128)(2,1)S(1)} copy-done((bf16[30,32,480]{2,1,0:T(8,128)(2,1)S(1)}, bf16[30,32,480]{2,1,0:T(8,128)(2,1)}, u32[]{:S(2)}) %copy-start) | copy-done | bytes 921624
  1.8 0.7 copy-done.5
  3.6 2.0 %collective-permute-start.1 = (bf16[30,64,240]{2,1,0:T(8,128)(2,1)}, bf16[30,64,240]{2,1,0:T(8,128)(2,1)S(1)}, u32[]{:S(2)}, u32[]{:S(2)}) collective-permute-start(bf16[30,64,240]{2,1,0:T(8,128)(2,1)} %bitcast.7), channel_id=1, source_target_pairs={{0,4},{1,13},{2,6},{3,15},{4,8},{5,1},{6,10},{7,3},{8,12},{9,5},{1... | collective-permute-start | bytes 2764808 | tf_op jit(solution)/shard_map/c1/ppermute | solution.py:247
  5.6 1.6 %collective-permute-start.2 = (bf16[30,64,240]{2,1,0:T(8,128)(2,1)}, bf16[30,64,240]{2,1,0:T(8,128)(2,1)S(1)}, u32[]{:S(2)}, u32[]{:S(2)}) collective-permute-start(bf16[30,64,240]{2,1,0:T(8,128)(2,1)} %bitcast.8), channel_id=1, source_target_pairs={{0,2},{1,3},{2,0},{3,1},{4,6},{5,7},{6,4},{7,5},{8,10},{9,11},{10,... | collective-permute-start | bytes 2764808 | tf_op jit(solution)/shard_map/aq/ppermute | solution.py:247
  7.2 1.5 %collective-permute-start.7 = (bf16[32,32,512]{2,1,0:T(8,128)(2,1)S(1)}, bf16[32,32,512]{2,1,0:T(8,128)(2,1)S(1)}, u32[]{:S(2)}, u32[]{:S(2)}) collective-permute-start(bf16[32,32,512]{2,1,0:T(8,128)(2,1)S(1)} %prepare_b.1.refs_16_), channel_id=1, source_target_pairs={{0,32},{1,97},{2,34},{3,99},{4,36},{5,101},{6,38},{7,103},{8,40},{... | collective-permute-start | bytes 3145736 | tf_op jit(solution)/shard_map/d1/ppermute | solution.py:247
  8.7 1.9 %collective-permute-start.3 = (bf16[30,64,240]{2,1,0:T(8,128)(2,1)S(1)}, bf16[30,64,240]{2,1,0:T(8,128)(2,1)S(1)}, u32[]{:S(2)}, u32[]{:S(2)}) collective-permute-start(bf16[30,64,240]{2,1,0:T(8,128)(2,1)S(1)} %collective-permute-done.p1.refs_1_), channel_id=1, source_target_pairs={{0,4},{1,13},{2,6},{3,15},{4,8},{5,1},{6,10},{7,3},{8,12},{9,5},{1... | collective-permute-start | bytes 2764808 | tf_op jit(solution)/shard_map/c2/ppermute | solution.py:247
  10.6 9.4 %collective-permute-done.1.p2.refs_2_ = bf16[30,64,240]{2,1,0:T(8,128)(2,1)S(1)} collective-permute-done((bf16[30,64,240]{2,1,0:T(8,128)(2,1)}, bf16[30,64,240]{2,1,0:T(8,128)(2,1)S(1)}, u32[]{:S(2)}, u32[]{:S(2)}) %collective-permute-start.1) | collective-permute-done | bytes 921632 | tf_op jit(solution)/shard_map/c1/ppermute | solution.py:247
  20.0 3.2 %collective-permute-start.14 = (bf16[32,32,512]{2,1,0:T(8,128)(2,1)S(1)}, bf16[32,32,512]{2,1,0:T(8,128)(2,1)S(1)}, u32[]{:S(2)}, u32[]{:S(2)}) collective-permute-start(bf16[32,32,512]{2,1,0:T(8,128)(2,1)S(1)} %prepare_b.1.refs_16_), channel_id=1, source_target_pairs={{0,16},{1,17},{2,18},{3,19},{4,20},{5,21},{6,22},{7,23},{8,24},{9,... | collective-permute-start | bytes 3145736 | tf_op jit(solution)/shard_map/bq/ppermute | solution.py:247
  23.2 6.3 %collective-permute-done.2.p3.refs_3_ = bf16[30,64,240]{2,1,0:T(8,128)(2,1)S(1)} collective-permute-done((bf16[30,64,240]{2,1,0:T(8,128)(2,1)}, bf16[30,64,240]{2,1,0:T(8,128)(2,1)S(1)}, u32[]{:S(2)}, u32[]{:S(2)}) %collective-permute-start.2) | collective-permute-done | bytes 921632 | tf_op jit(solution)/shard_map/aq/ppermute | solution.py:247
  29.5 1.5 %collective-permute-start.9 = (bf16[32,32,512]{2,1,0:T(8,128)(2,1)S(1)}, bf16[32,32,512]{2,1,0:T(8,128)(2,1)S(1)}, u32[]{:S(2)}, u32[]{:S(2)}) collective-permute-start(bf16[32,32,512]{2,1,0:T(8,128)(2,1)S(1)} %collective-permute-done.6), channel_id=1, source_target_pairs={{0,32},{1,97},{2,34},{3,99},{4,36},{5,101},{6,38},{7,103},{8,40},{... | collective-permute-start | bytes 3145736 | tf_op jit(solution)/shard_map/d2/ppermute | solution.py:247
  31.0 1.2 %copy-done.1 = bf16[30,240,64]{1,2,0:T(8,128)(2,1)S(1)} copy-done((bf16[30,240,64]{1,2,0:T(8,128)(2,1)S(1)}, bf16[30,240,64]{1,2,0:T(8,128)(2,1)}, u32[]{:S(2)}) %copy-start.1) | copy-done | bytes 921624
  32.2 0.7 copy-done.3
  32.9 0.7 copy-done.4
  33.6 3.9 %regroup_a.1.refs_24_ = bf16[32,256,256]{2,1,0:T(8,128)(2,1)S(1)} custom-call(s32[8,8]{1,0:T(8,128)S(1)} %copy-done.4, s32[16,16]{1,0:T(8,128)S(1)} %copy-done.3, bf16[30,64,240]{2,1,0:T(8,128)(2,1)S(1)} %bitcast.9, bf16[30,64,240]{2,1,0:T(8,128)(2,1)S(1)} %collective-permute-done.p1.refs_1_, bf16[30,64,240]{2,1,0:T(8,128)(2,1)S(1)} %collective-permute-done.1.p2.refs_2_, ...), custom_call_target="tpu_custom_call" | custom-call | flops 2000000000 | bytes 8000000 | tf_op jit(solution)/shard_map/regroup_a/pallas_call | solution.py:112
  37.4 3.1 %collective-permute-start.5 = (bf16[30,64,240]{2,1,0:T(8,128)(2,1)S(1)}, bf16[30,64,240]{2,1,0:T(8,128)(2,1)S(1)}, u32[]{:S(2)}, u32[]{:S(2)}) collective-permute-start(bf16[30,64,240]{2,1,0:T(8,128)(2,1)S(1)} %collective-permute-done.2.p3.refs_3_), channel_id=1, source_target_pairs={{0,1},{1,0},{2,3},{3,2},{4,5},{5,4},{6,7},{7,6},{8,9},{9,8},{10,11... | collective-permute-start | bytes 2764808 | tf_op jit(solution)/shard_map/s_aq/ppermute | solution.py:247
  41.1 1.5 %collective-permute-start.12 = (bf16[32,32,512]{2,1,0:T(8,128)(2,1)S(1)}, bf16[32,32,512]{2,1,0:T(8,128)(2,1)S(1)}, u32[]{:S(2)}, u32[]{:S(2)}) collective-permute-start(bf16[32,32,512]{2,1,0:T(8,128)(2,1)S(1)} %collective-permute-done.7.refs_17_), channel_id=1, source_target_pairs={{0,32},{1,97},{2,34},{3,99},{4,36},{5,101},{6,38},{7,103},{8,40},{... | collective-permute-start | bytes 3145736 | tf_op jit(solution)/shard_map/d5/ppermute | solution.py:247
  42.6 11.8 %collective-permute-done.14.refs_20_ = bf16[32,32,512]{2,1,0:T(8,128)(2,1)S(1)} collective-permute-done((bf16[32,32,512]{2,1,0:T(8,128)(2,1)S(1)}, bf16[32,32,512]{2,1,0:T(8,128)(2,1)S(1)}, u32[]{:S(2)}, u32[]{:S(2)}) %collective-permute-start.14) | collective-permute-done | bytes 1048608 | tf_op jit(solution)/shard_map/bq/ppermute | solution.py:247
  54.4 0.8 collective-permute-start.15
  55.2 1.6 %collective-permute-start.17 = (bf16[32,32,512]{2,1,0:T(8,128)(2,1)S(1)}, bf16[32,32,512]{2,1,0:T(8,128)(2,1)S(1)}, u32[]{:S(2)}, u32[]{:S(2)}) collective-permute-start(bf16[32,32,512]{2,1,0:T(8,128)(2,1)S(1)} %collective-permute-done.14.refs_20_), channel_id=1, source_target_pairs={{0,32},{1,97},{2,34},{3,99},{4,36},{5,101},{6,38},{7,103},{8,40},{... | collective-permute-start | bytes 3145736 | tf_op jit(solution)/shard_map/dq1/ppermute | solution.py:247
  56.7 1.1 %collective-permute-done.8.p3.refs_7_ = bf16[30,64,240]{2,1,0:T(8,128)(2,1)S(1)} collective-permute-done((bf16[30,64,240]{2,1,0:T(8,128)(2,1)S(1)}, bf16[30,64,240]{2,1,0:T(8,128)(2,1)S(1)}, u32[]{:S(2)}, u32[]{:S(2)}) %collective-permute-start.8) | collective-permute-done | bytes 921632 | tf_op jit(solution)/shard_map/cq1/ppermute | solution.py:247
  58.2 1.5 %collective-permute-start.13 = (bf16[30,64,240]{2,1,0:T(8,128)(2,1)S(1)}, bf16[30,64,240]{2,1,0:T(8,128)(2,1)S(1)}, u32[]{:S(2)}, u32[]{:S(2)}) collective-permute-start(bf16[30,64,240]{2,1,0:T(8,128)(2,1)S(1)} %collective-permute-done.5.p2.refs_6_), channel_id=1, source_target_pairs={{0,4},{1,13},{2,6},{3,15},{4,8},{5,1},{6,10},{7,3},{8,12},{9,5},{1... | collective-permute-start | bytes 2764808 | tf_op jit(solution)/shard_map/cq2/ppermute | solution.py:247
  59.9 3.9 %regroup_c2.1.refs_25_ = bf16[32,256,256]{2,1,0:T(8,128)(2,1)S(1)} custom-call(s32[8,8]{1,0:T(8,128)S(1)} %copy-done.4, s32[16,16]{1,0:T(8,128)S(1)} %copy-done.3, bf16[30,64,240]{2,1,0:T(8,128)(2,1)S(1)} %collective-permute-done.3.p0.refs_4_, bf16[30,64,240]{2,1,0:T(8,128)(2,1)S(1)} %collective-permute-done.4.p1.refs_5_, ...), custom_call_target="tpu_custom_call" | custom-call | flops 2000000000 | bytes 8000000 | tf_op jit(solution)/shard_map/regroup_c2/pallas_call | solution.py:112
  63.8 0.6 collective-permute-start.23
  64.4 1.2 %collective-permute-start.19 = (bf16[30,64,240]{2,1,0:T(8,128)(2,1)S(1)}, bf16[30,64,240]{2,1,0:T(8,128)(2,1)S(1)}, u32[]{:S(2)}, u32[]{:S(2)}) collective-permute-start(bf16[30,64,240]{2,1,0:T(8,128)(2,1)S(1)} %collective-permute-done.8.p3.refs_7_), channel_id=1, source_target_pairs={{0,4},{1,13},{2,6},{3,15},{4,8},{5,1},{6,10},{7,3},{8,12},{9,5},{1... | collective-permute-start | bytes 2764808 | tf_op jit(solution)/shard_map/cq5/ppermute | solution.py:247
  65.6 5.7 %collective-permute-done.17.refs_21_ = bf16[32,32,512]{2,1,0:T(8,128)(2,1)S(1)} collective-permute-done((bf16[32,32,512]{2,1,0:T(8,128)(2,1)S(1)}, bf16[32,32,512]{2,1,0:T(8,128)(2,1)S(1)}, u32[]{:S(2)}, u32[]{:S(2)}) %collective-permute-start.17) | collective-permute-done | bytes 1048608 | tf_op jit(solution)/shard_map/dq1/ppermute | solution.py:247
  71.3 2.2 %collective-permute-done.13.p2.refs_10_ = bf16[30,64,240]{2,1,0:T(8,128)(2,1)S(1)} collective-permute-done((bf16[30,64,240]{2,1,0:T(8,128)(2,1)S(1)}, bf16[30,64,240]{2,1,0:T(8,128)(2,1)S(1)}, u32[]{:S(2)}, u32[]{:S(2)}) %collective-permute-start.13) | collective-permute-done | bytes 921632 | tf_op jit(solution)/shard_map/cq2/ppermute | solution.py:247
  73.5 1.2 %collective-permute-start.25 = (bf16[32,32,512]{2,1,0:T(8,128)(2,1)S(1)}, bf16[32,32,512]{2,1,0:T(8,128)(2,1)S(1)}, u32[]{:S(2)}, u32[]{:S(2)}) collective-permute-start(bf16[32,32,512]{2,1,0:T(8,128)(2,1)S(1)} %collective-permute-done.17.refs_21_), channel_id=1, source_target_pairs={{0,32},{1,97},{2,34},{3,99},{4,36},{5,101},{6,38},{7,103},{8,40},{... | collective-permute-start | bytes 3145736 | tf_op jit(solution)/shard_map/dq5/ppermute | solution.py:247
  75.2 3.9 %regroup_s_c5.1.refs_26_ = bf16[32,256,256]{2,1,0:T(8,128)(2,1)S(1)} custom-call(s32[8,8]{1,0:T(8,128)S(1)} %copy-done.4, s32[16,16]{1,0:T(8,128)S(1)} %copy-done.3, bf16[30,64,240]{2,1,0:T(8,128)(2,1)S(1)} %collective-permute-done.10.p0.refs_8_, bf16[30,64,240]{2,1,0:T(8,128)(2,1)S(1)} %collective-permute-done.11.p1.refs_9_, ...), custom_call_target="tpu_custom_call" | custom-call | flops 2000000000 | bytes 8000000 | tf_op jit(solution)/shard_map/regroup_s_c5/pallas_call | solution.py:112
  79.0 3.5 %collective-permute-done.23 = bf16[32,32,512]{2,1,0:T(8,128)(2,1)S(1)} collective-permute-done((bf16[32,32,512]{2,1,0:T(8,128)(2,1)S(1)}, bf16[32,32,512]{2,1,0:T(8,128)(2,1)S(1)}, u32[]{:S(2)}, u32[]{:S(2)}) %collective-permute-start.23) | collective-permute-done | bytes 1048608 | tf_op jit(solution)/shard_map/dq2/ppermute | solution.py:247
  82.5 1.5 %collective-permute-done.19.refs_13_ = bf16[30,64,240]{2,1,0:T(8,128)(2,1)S(1)} collective-permute-done((bf16[30,64,240]{2,1,0:T(8,128)(2,1)S(1)}, bf16[30,64,240]{2,1,0:T(8,128)(2,1)S(1)}, u32[]{:S(2)}, u32[]{:S(2)}) %collective-permute-start.19) | collective-permute-done | bytes 921632 | tf_op jit(solution)/shard_map/cq5/ppermute | solution.py:247
  84.5 9.2 %collective-permute-done.25.refs_23_ = bf16[32,32,512]{2,1,0:T(8,128)(2,1)S(1)} collective-permute-done((bf16[32,32,512]{2,1,0:T(8,128)(2,1)S(1)}, bf16[32,32,512]{2,1,0:T(8,128)(2,1)S(1)}, u32[]{:S(2)}, u32[]{:S(2)}) %collective-permute-start.25) | collective-permute-done | bytes 1048608 | tf_op jit(solution)/shard_map/dq5/ppermute | solution.py:247
  93.8 18.2 %last.1 = (bf16[30,64,240]{2,1,0:T(8,128)(2,1)}, bf16[960,480]{1,0:T(8,128)(2,1)}) custom-call(s32[8,8]{1,0:T(8,128)S(1)} %copy-done.4, s32[16,16]{1,0:T(8,128)S(1)} %copy-done.3, bf16[30,64,240]{2,1,0:T(8,128)(2,1)S(1)} %bitcast.10, bf16[30,64,240]{2,1,0:T(8,128)(2,1)S(1)} %collective-permute-done.p1.refs_1_, ...), custom_call_target="tpu_custom_call" | custom-call | flops 12000000000 | bytes 38000000 | tf_op jit(solution)/shard_map/last/pallas_call | solution.py:224
  (37 shorter events, 3.2 us)
Async XLA Ops:
  0.6 1.2 %copy-start = (bf16[30,32,480]{2,1,0:T(8,128)(2,1)S(1)}, bf16[30,32,480]{2,1,0:T(8,128)(2,1)}, u32[]{:S(2)}) copy-start(bf16[30,32,480]{2,1,0:T(8,128)(2,1)} %param.7) | copy-start | bytes 2764804
  1.8 0.7 copy-start.5
  3.0 4.2 %collective-permute-start.6 = (bf16[32,32,512]{2,1,0:T(8,128)(2,1)S(1)}, bf16[32,32,512]{2,1,0:T(8,128)(2,1)S(1)}, u32[]{:S(2)}, u32[]{:S(2)}) collective-permute-start(bf16[32,32,512]{2,1,0:T(8,128)(2,1)S(1)} %prepare_b.1.refs_16_), channel_id=1, source_target_pairs={{0,1},{1,0},{2,3},{3,2},{4,5},{5,4},{6,7},{7,6},{8,9},{9,8},{10,11... | collective-permute-start | bytes 3145736 | tf_op jit(solution)/shard_map/s_b/ppermute | solution.py:247
  3.1 5.6 %collective-permute-start = (bf16[30,64,240]{2,1,0:T(8,128)(2,1)}, bf16[30,64,240]{2,1,0:T(8,128)(2,1)S(1)}, u32[]{:S(2)}, u32[]{:S(2)}) collective-permute-start(bf16[30,64,240]{2,1,0:T(8,128)(2,1)} %bitcast.6), channel_id=1, source_target_pairs={{0,1},{1,0},{2,3},{3,2},{4,5},{5,4},{6,7},{7,6},{8,9},{9,8},{10,11... | collective-permute-start | bytes 2764808 | tf_op jit(solution)/shard_map/s_a/ppermute | solution.py:247
  3.6 16.4 %collective-permute-start.1 = (bf16[30,64,240]{2,1,0:T(8,128)(2,1)}, bf16[30,64,240]{2,1,0:T(8,128)(2,1)S(1)}, u32[]{:S(2)}, u32[]{:S(2)}) collective-permute-start(bf16[30,64,240]{2,1,0:T(8,128)(2,1)} %bitcast.7), channel_id=1, source_target_pairs={{0,4},{1,13},{2,6},{3,15},{4,8},{5,1},{6,10},{7,3},{8,12},{9,5},{1... | collective-permute-start | bytes 2764808 | tf_op jit(solution)/shard_map/c1/ppermute | solution.py:247
  5.6 23.9 %collective-permute-start.2 = (bf16[30,64,240]{2,1,0:T(8,128)(2,1)}, bf16[30,64,240]{2,1,0:T(8,128)(2,1)S(1)}, u32[]{:S(2)}, u32[]{:S(2)}) collective-permute-start(bf16[30,64,240]{2,1,0:T(8,128)(2,1)} %bitcast.8), channel_id=1, source_target_pairs={{0,2},{1,3},{2,0},{3,1},{4,6},{5,7},{6,4},{7,5},{8,10},{9,11},{10,... | collective-permute-start | bytes 2764808 | tf_op jit(solution)/shard_map/aq/ppermute | solution.py:247
  7.2 33.9 %collective-permute-start.7 = (bf16[32,32,512]{2,1,0:T(8,128)(2,1)S(1)}, bf16[32,32,512]{2,1,0:T(8,128)(2,1)S(1)}, u32[]{:S(2)}, u32[]{:S(2)}) collective-permute-start(bf16[32,32,512]{2,1,0:T(8,128)(2,1)S(1)} %prepare_b.1.refs_16_), channel_id=1, source_target_pairs={{0,32},{1,97},{2,34},{3,99},{4,36},{5,101},{6,38},{7,103},{8,40},{... | collective-permute-start | bytes 3145736 | tf_op jit(solution)/shard_map/d1/ppermute | solution.py:247
  8.7 28.8 %collective-permute-start.3 = (bf16[30,64,240]{2,1,0:T(8,128)(2,1)S(1)}, bf16[30,64,240]{2,1,0:T(8,128)(2,1)S(1)}, u32[]{:S(2)}, u32[]{:S(2)}) collective-permute-start(bf16[30,64,240]{2,1,0:T(8,128)(2,1)S(1)} %collective-permute-done.p1.refs_1_), channel_id=1, source_target_pairs={{0,4},{1,13},{2,6},{3,15},{4,8},{5,1},{6,10},{7,3},{8,12},{9,5},{1... | collective-permute-start | bytes 2764808 | tf_op jit(solution)/shard_map/c2/ppermute | solution.py:247
  20.0 21.1 %collective-permute-start.4 = (bf16[30,64,240]{2,1,0:T(8,128)(2,1)S(1)}, bf16[30,64,240]{2,1,0:T(8,128)(2,1)S(1)}, u32[]{:S(2)}, u32[]{:S(2)}) collective-permute-start(bf16[30,64,240]{2,1,0:T(8,128)(2,1)S(1)} %collective-permute-done.1.p2.refs_2_), channel_id=1, source_target_pairs={{0,4},{1,13},{2,6},{3,15},{4,8},{5,1},{6,10},{7,3},{8,12},{9,5},{1... | collective-permute-start | bytes 2764808 | tf_op jit(solution)/shard_map/c5/ppermute | solution.py:247
  20.0 34.4 %collective-permute-start.14 = (bf16[32,32,512]{2,1,0:T(8,128)(2,1)S(1)}, bf16[32,32,512]{2,1,0:T(8,128)(2,1)S(1)}, u32[]{:S(2)}, u32[]{:S(2)}) collective-permute-start(bf16[32,32,512]{2,1,0:T(8,128)(2,1)S(1)} %prepare_b.1.refs_16_), channel_id=1, source_target_pairs={{0,16},{1,17},{2,18},{3,19},{4,20},{5,21},{6,22},{7,23},{8,24},{9,... | collective-permute-start | bytes 3145736 | tf_op jit(solution)/shard_map/bq/ppermute | solution.py:247
  29.5 25.7 %collective-permute-start.9 = (bf16[32,32,512]{2,1,0:T(8,128)(2,1)S(1)}, bf16[32,32,512]{2,1,0:T(8,128)(2,1)S(1)}, u32[]{:S(2)}, u32[]{:S(2)}) collective-permute-start(bf16[32,32,512]{2,1,0:T(8,128)(2,1)S(1)} %collective-permute-done.6), channel_id=1, source_target_pairs={{0,32},{1,97},{2,34},{3,99},{4,36},{5,101},{6,38},{7,103},{8,40},{... | collective-permute-start | bytes 3145736 | tf_op jit(solution)/shard_map/d2/ppermute | solution.py:247
  31.0 1.2 %copy-start.1 = (bf16[30,240,64]{1,2,0:T(8,128)(2,1)S(1)}, bf16[30,240,64]{1,2,0:T(8,128)(2,1)}, u32[]{:S(2)}) copy-start(bf16[30,240,64]{1,2,0:T(8,128)(2,1)} %param.5) | copy-start | bytes 2764804
  32.2 0.7 copy-start.3
  32.9 0.7 copy-start.4
  37.4 17.7 %collective-permute-start.5 = (bf16[30,64,240]{2,1,0:T(8,128)(2,1)S(1)}, bf16[30,64,240]{2,1,0:T(8,128)(2,1)S(1)}, u32[]{:S(2)}, u32[]{:S(2)}) collective-permute-start(bf16[30,64,240]{2,1,0:T(8,128)(2,1)S(1)} %collective-permute-done.2.p3.refs_3_), channel_id=1, source_target_pairs={{0,1},{1,0},{2,3},{3,2},{4,5},{5,4},{6,7},{7,6},{8,9},{9,8},{10,11... | collective-permute-start | bytes 2764808 | tf_op jit(solution)/shard_map/s_aq/ppermute | solution.py:247
  41.1 17.1 %collective-permute-start.12 = (bf16[32,32,512]{2,1,0:T(8,128)(2,1)S(1)}, bf16[32,32,512]{2,1,0:T(8,128)(2,1)S(1)}, u32[]{:S(2)}, u32[]{:S(2)}) collective-permute-start(bf16[32,32,512]{2,1,0:T(8,128)(2,1)S(1)} %collective-permute-done.7.refs_17_), channel_id=1, source_target_pairs={{0,32},{1,97},{2,34},{3,99},{4,36},{5,101},{6,38},{7,103},{8,40},{... | collective-permute-start | bytes 3145736 | tf_op jit(solution)/shard_map/d5/ppermute | solution.py:247
  42.6 15.3 %collective-permute-start.8 = (bf16[30,64,240]{2,1,0:T(8,128)(2,1)S(1)}, bf16[30,64,240]{2,1,0:T(8,128)(2,1)S(1)}, u32[]{:S(2)}, u32[]{:S(2)}) collective-permute-start(bf16[30,64,240]{2,1,0:T(8,128)(2,1)S(1)} %collective-permute-done.2.p3.refs_3_), channel_id=1, source_target_pairs={{0,4},{1,13},{2,6},{3,15},{4,8},{5,1},{6,10},{7,3},{8,12},{9,5},{1... | collective-permute-start | bytes 2764808 | tf_op jit(solution)/shard_map/cq1/ppermute | solution.py:247
  54.4 5.3 %collective-permute-start.15 = (bf16[32,32,512]{2,1,0:T(8,128)(2,1)S(1)}, bf16[32,32,512]{2,1,0:T(8,128)(2,1)S(1)}, u32[]{:S(2)}, u32[]{:S(2)}) collective-permute-start(bf16[32,32,512]{2,1,0:T(8,128)(2,1)S(1)} %collective-permute-done.14.refs_20_), channel_id=1, source_target_pairs={{0,1},{1,0},{2,3},{3,2},{4,5},{5,4},{6,7},{7,6},{8,9},{9,8},{10,11... | collective-permute-start | bytes 3145736 | tf_op jit(solution)/shard_map/s_bq/ppermute | solution.py:247
  55.2 8.6 %collective-permute-start.10 = (bf16[30,64,240]{2,1,0:T(8,128)(2,1)S(1)}, bf16[30,64,240]{2,1,0:T(8,128)(2,1)S(1)}, u32[]{:S(2)}, u32[]{:S(2)}) collective-permute-start(bf16[30,64,240]{2,1,0:T(8,128)(2,1)S(1)} %collective-permute-done.4.p1.refs_5_), channel_id=1, source_target_pairs={{0,1},{1,0},{2,3},{3,2},{4,5},{5,4},{6,7},{7,6},{8,9},{9,8},{10,11... | collective-permute-start | bytes 2764808 | tf_op jit(solution)/shard_map/s_c5/ppermute | solution.py:247
  55.2 16.1 %collective-permute-start.17 = (bf16[32,32,512]{2,1,0:T(8,128)(2,1)S(1)}, bf16[32,32,512]{2,1,0:T(8,128)(2,1)S(1)}, u32[]{:S(2)}, u32[]{:S(2)}) collective-permute-start(bf16[32,32,512]{2,1,0:T(8,128)(2,1)S(1)} %collective-permute-done.14.refs_20_), channel_id=1, source_target_pairs={{0,32},{1,97},{2,34},{3,99},{4,36},{5,101},{6,38},{7,103},{8,40},{... | collective-permute-start | bytes 3145736 | tf_op jit(solution)/shard_map/dq1/ppermute | solution.py:247
  57.9 6.6 %collective-permute-start.11 = (bf16[30,64,240]{2,1,0:T(8,128)(2,1)S(1)}, bf16[30,64,240]{2,1,0:T(8,128)(2,1)S(1)}, u32[]{:S(2)}, u32[]{:S(2)}) collective-permute-start(bf16[30,64,240]{2,1,0:T(8,128)(2,1)S(1)} %collective-permute-done.8.p3.refs_7_), channel_id=1, source_target_pairs={{0,1},{1,0},{2,3},{3,2},{4,5},{5,4},{6,7},{7,6},{8,9},{9,8},{10,11... | collective-permute-start | bytes 2764808 | tf_op jit(solution)/shard_map/s_cq1/ppermute | solution.py:247
  58.2 15.3 %collective-permute-start.13 = (bf16[30,64,240]{2,1,0:T(8,128)(2,1)S(1)}, bf16[30,64,240]{2,1,0:T(8,128)(2,1)S(1)}, u32[]{:S(2)}, u32[]{:S(2)}) collective-permute-start(bf16[30,64,240]{2,1,0:T(8,128)(2,1)S(1)} %collective-permute-done.5.p2.refs_6_), channel_id=1, source_target_pairs={{0,4},{1,13},{2,6},{3,15},{4,8},{5,1},{6,10},{7,3},{8,12},{9,5},{1... | collective-permute-start | bytes 2764808 | tf_op jit(solution)/shard_map/cq2/ppermute | solution.py:247
  59.7 13.8 %collective-permute-start.16 = (bf16[30,64,240]{2,1,0:T(8,128)(2,1)S(1)}, bf16[30,64,240]{2,1,0:T(8,128)(2,1)S(1)}, u32[]{:S(2)}, u32[]{:S(2)}) collective-permute-start(bf16[30,64,240]{2,1,0:T(8,128)(2,1)S(1)} %collective-permute-done.1.p2.refs_2_), channel_id=1, source_target_pairs={{0,1},{1,0},{2,3},{3,2},{4,5},{5,4},{6,7},{7,6},{8,9},{9,8},{10,11... | collective-permute-start | bytes 2764808 | tf_op jit(solution)/shard_map/s_c1/ppermute | solution.py:247
  63.8 30.0 %copy-start.2 = (bf16[30,240,64]{1,2,0:T(8,128)(2,1)S(1)}, bf16[30,240,64]{1,2,0:T(8,128)(2,1)}, u32[]{:S(2)}) copy-start(bf16[30,240,64]{1,2,0:T(8,128)(2,1)} %param.5) | copy-start | bytes 2764804
  63.8 18.7 %collective-permute-start.23 = (bf16[32,32,512]{2,1,0:T(8,128)(2,1)S(1)}, bf16[32,32,512]{2,1,0:T(8,128)(2,1)S(1)}, u32[]{:S(2)}, u32[]{:S(2)}) collective-permute-start(bf16[32,32,512]{2,1,0:T(8,128)(2,1)S(1)} %collective-permute-done.15), channel_id=1, source_target_pairs={{0,32},{1,97},{2,34},{3,99},{4,36},{5,101},{6,38},{7,103},{8,40},{... | collective-permute-start | bytes 3145736 | tf_op jit(solution)/shard_map/dq2/ppermute | solution.py:247
  64.4 19.6 %collective-permute-start.19 = (bf16[30,64,240]{2,1,0:T(8,128)(2,1)S(1)}, bf16[30,64,240]{2,1,0:T(8,128)(2,1)S(1)}, u32[]{:S(2)}, u32[]{:S(2)}) collective-permute-start(bf16[30,64,240]{2,1,0:T(8,128)(2,1)S(1)} %collective-permute-done.8.p3.refs_7_), channel_id=1, source_target_pairs={{0,4},{1,13},{2,6},{3,15},{4,8},{5,1},{6,10},{7,3},{8,12},{9,5},{1... | collective-permute-start | bytes 2764808 | tf_op jit(solution)/shard_map/cq5/ppermute | solution.py:247
  73.5 10.5 %collective-permute-start.18 = (bf16[30,64,240]{2,1,0:T(8,128)(2,1)S(1)}, bf16[30,64,240]{2,1,0:T(8,128)(2,1)S(1)}, u32[]{:S(2)}, u32[]{:S(2)}) collective-permute-start(bf16[30,64,240]{2,1,0:T(8,128)(2,1)S(1)} %collective-permute-done.13.p2.refs_10_), channel_id=1, source_target_pairs={{0,1},{1,0},{2,3},{3,2},{4,5},{5,4},{6,7},{7,6},{8,9},{9,8},{10,11... | collective-permute-start | bytes 2764808 | tf_op jit(solution)/shard_map/s_cq2/ppermute | solution.py:247
  73.5 20.2 %collective-permute-start.25 = (bf16[32,32,512]{2,1,0:T(8,128)(2,1)S(1)}, bf16[32,32,512]{2,1,0:T(8,128)(2,1)S(1)}, u32[]{:S(2)}, u32[]{:S(2)}) collective-permute-start(bf16[32,32,512]{2,1,0:T(8,128)(2,1)S(1)} %collective-permute-done.17.refs_21_), channel_id=1, source_target_pairs={{0,32},{1,97},{2,34},{3,99},{4,36},{5,101},{6,38},{7,103},{8,40},{... | collective-permute-start | bytes 3145736 | tf_op jit(solution)/shard_map/dq5/ppermute | solution.py:247
  74.7 19.1 %collective-permute-start.22 = (bf16[32,32,512]{2,1,0:T(8,128)(2,1)S(1)}, bf16[32,32,512]{2,1,0:T(8,128)(2,1)S(1)}, u32[]{:S(2)}, u32[]{:S(2)}) collective-permute-start(bf16[32,32,512]{2,1,0:T(8,128)(2,1)S(1)} %collective-permute-done.9), channel_id=1, source_target_pairs={{0,1},{1,0},{2,3},{3,2},{4,5},{5,4},{6,7},{7,6},{8,9},{9,8},{10,11... | collective-permute-start | bytes 3145736 | tf_op jit(solution)/shard_map/s_d2/ppermute | solution.py:247
  82.5 11.2 %collective-permute-start.24 = (bf16[32,32,512]{2,1,0:T(8,128)(2,1)S(1)}, bf16[32,32,512]{2,1,0:T(8,128)(2,1)S(1)}, u32[]{:S(2)}, u32[]{:S(2)}) collective-permute-start(bf16[32,32,512]{2,1,0:T(8,128)(2,1)S(1)} %collective-permute-done.23), channel_id=1, source_target_pairs={{0,1},{1,0},{2,3},{3,2},{4,5},{5,4},{6,7},{7,6},{8,9},{9,8},{10,11... | collective-permute-start | bytes 3145736 | tf_op jit(solution)/shard_map/s_dq2/ppermute | solution.py:247
  84.0 9.7 %collective-permute-start.21 = (bf16[30,64,240]{2,1,0:T(8,128)(2,1)S(1)}, bf16[30,64,240]{2,1,0:T(8,128)(2,1)S(1)}, u32[]{:S(2)}, u32[]{:S(2)}) collective-permute-start(bf16[30,64,240]{2,1,0:T(8,128)(2,1)S(1)} %collective-permute-done.3.p0.refs_4_), channel_id=1, source_target_pairs={{0,1},{1,0},{2,3},{3,2},{4,5},{5,4},{6,7},{7,6},{8,9},{9,8},{10,11... | collective-permute-start | bytes 2764808 | tf_op jit(solution)/shard_map/s_c2/ppermute | solution.py:247
  84.0 9.7 %collective-permute-start.20 = (bf16[30,64,240]{2,1,0:T(8,128)(2,1)S(1)}, bf16[30,64,240]{2,1,0:T(8,128)(2,1)S(1)}, u32[]{:S(2)}, u32[]{:S(2)}) collective-permute-start(bf16[30,64,240]{2,1,0:T(8,128)(2,1)S(1)} %collective-permute-done.19.refs_13_), channel_id=1, source_target_pairs={{0,1},{1,0},{2,3},{3,2},{4,5},{5,4},{6,7},{7,6},{8,9},{9,8},{10,11... | collective-permute-start | bytes 2764808 | tf_op jit(solution)/shard_map/s_cq5/ppermute | solution.py:247

commit v4 on v3

--- a/solution.py
+++ b/solution.py
@@ -9,8 +9,7 @@
 
 BF = jnp.bfloat16
 F32 = jnp.float32
-PARAMS = pltpu.CompilerParams(vmem_limit_bytes=16 * 1024 * 1024)
-LAST_PARAMS = pltpu.CompilerParams(vmem_limit_bytes=16 * 1024 * 1024)
+PARAMS = pltpu.CompilerParams(vmem_limit_bytes=7 * 1024 * 1024)
 VMEM = pl.BlockSpec(memory_space=pltpu.VMEM)
 SMEM = pl.BlockSpec(memory_space=pltpu.SMEM)
 
@@ -115,7 +114,7 @@
         in_specs=[SMEM] * 2 + [VMEM] * 4,
         out_specs=VMEM,
         compiler_params=PARAMS,
-        cost_estimate=cost(2 * 10**9, 8 * 10**6),
+        cost_estimate=cost(1000, 1000),
         name="regroup_" + names[0],
     )(*maps, *pieces)
 
@@ -177,22 +176,33 @@
     return jnp.concatenate(tiles, axis=1)
 
 
+def early_kernel(*refs):
+    sets, b_refs, out_ref = refs[:3], refs[3:7], refs[7]
+    for k, part in enumerate(sets):
+        out_ref[pl.ds(k * 256, 256), :] = cycle_product(lambda c: part[c, :, 0:128], b_refs)
+
+
+def early_products(sets, b_early):
+    return pl.pallas_call(
+        early_kernel,
+        out_shape=jax.ShapeDtypeStruct((768, 512), F32),
+        in_specs=[VMEM] * 7,
+        out_specs=VMEM,
+        compiler_params=PARAMS,
+        cost_estimate=cost(1000, 1000),
+        name="early",
+    )(*sets, *b_early)
+
+
 def last_kernel(names, occ_ref, vir_ref, *refs):
-    refs = list(refs)
-
-    def take(n):
-        out = refs[:n]
-        del refs[:n]
-        return out
-
-    pieces, b_refs, sets, (lad_out, cyc_out, v_ref, set_ref, c_ref) = take(16), take(8), take(3), refs
+    pieces, b_refs, sets, refs = refs[:16], refs[16:24], refs[24:28], refs[28:]
+    start_ref, lad_out, cyc_out, v_ref, c_ref = refs
     row, col = here()
     ids = piece_ids(col)
-    regroup_pieces(occ_ref, vir_ref, names[12:], pieces[12:], set_ref)
-    for k, part in enumerate(sets + [set_ref]):
-        total = cycle_product(lambda c: part[c, :, 0:128], b_refs[0:4])
-        total = cycle_product(lambda c: part[c, :, 128:256], b_refs[4:8], total)
-        c_ref[pl.ds(k * 256, 256), :] = total.astype(BF)
+    for k, part in enumerate(sets):
+        at = pl.ds(k * 256, 256)
+        start = start_ref[at, :] if k < 3 else cycle_product(lambda c: part[c, :, 0:128], b_refs[0:4])
+        c_ref[at, :] = cycle_product(lambda c: part[c, :, 128:256], b_refs[4:8], start).astype(BF)
     for k in range(8):
         v_ref[k] = b_refs[k][0:8, :, 384:512]
     weights = ladder_weights(v_ref, vir_ref, row, col, [ids[n] for n in names])
@@ -220,21 +230,20 @@
         cyc_out[pl.ds(g * 256, n), :] = dot(spread[0:n], block)[:, 0:480].astype(BF)
 
 
-def last_products(names, maps, pieces, b_all, sets):
+def last_products(names, maps, pieces, b_all, sets, start):
     return pl.pallas_call(
         functools.partial(last_kernel, names),
         out_shape=(jax.ShapeDtypeStruct((30, 64, 240), BF), jax.ShapeDtypeStruct((960, 480), BF)),
-        in_specs=[SMEM] * 2 + [VMEM] * 27,
+        in_specs=[SMEM] * 2 + [VMEM] * 29,
         out_specs=(VMEM,) * 2,
         scratch_shapes=[
             pltpu.VMEM((8, 8, 32, 128), BF),
-            pltpu.VMEM((32, 256, 256), BF),
             pltpu.VMEM((1024, 512), BF),
         ],
-        compiler_params=LAST_PARAMS,
+        compiler_params=PARAMS,
         cost_estimate=cost(12 * 10**9, 38 * 10**6),
         name="last",
-    )(*maps, *pieces, *b_all, *sets)
+    )(*maps, *pieces, *b_all, *sets, start)
 
 
 def permute(value, move):
@@ -322,9 +331,10 @@
         with jax.named_scope(name):
             have[name] = permute(value, KINDS[kind])
         order.append(name)
-    ladder, cycle_out = last_products(
-        names, maps, [have[n] for n in names], [have[n] for n in B_NAMES], [sets[k] for k in range(3)]
-    )
+    sets[3] = regroup_set(SETS[3], maps, [have[n] for n in SETS[3]])
+    sets, b_all = [sets[k] for k in range(4)], [have[n] for n in B_NAMES]
+    start = early_products(sets[:3], b_all[:4])
+    ladder, cycle_out = last_products(names, maps, [have[n] for n in names], b_all, sets, start)
     ladder = jnp.transpose(ladder, (0, 2, 1))
     return ladder, cycle_out.reshape(30, 32, 480)
 

time: 112 us -> 106 us (0.946)
  waiting for transfers between devices: 51.3 us -> 43.7 us
    ppermute x26, waiting for transfers between devices: 51.3 us -> 43.7 us  [permute(): return lax.ppermute(value, ('row', 'col'), pairs)]
    pallas_call x1, Pallas kernels: 18.2 us -> 12 us  [last_products(): pl.pallas_call(functools.partial(last_kernel, names), out_shape=(jax.Shap...]
    pallas_call x3 -> x4, Pallas kernels: 11.6 us -> 15.5 us  [regroup_set(): pl.pallas_call(functools.partial(regroup_kernel, names), out_shape=jax.Sh...]
    pallas_call x0 -> x1, Pallas kernels: none -> 3.4 us  [early_products(): pl.pallas_call(early_kernel, out_shape=jax.ShapeDtypeStruct((768, 512), F...]
  transfers between devices with their start and end apart: 26 -> 26, of which waited for: 10 -> 10; matrix products, arithmetic and copies ran while one was open for 0% -> 0% of each run, Pallas kernels for 10% -> 18%
where the time goes in v4:
time: 106 us
  waiting for transfers between devices  43.7 us (41%)
  Pallas kernels  31.3 us (30%)
  starting transfers between devices  25.4 us (24%)
  local copies, waits for them, and re-layouts  4.5 us (4%)
    ppermute x26, waiting for transfers between devices, permute(): return lax.ppermute(value, ('row', 'col'), pairs)  43.7 us
    ppermute x26, starting transfers between devices, permute(): return lax.ppermute(value, ('row', 'col'), pairs)  25.4 us
    pallas_call x4, Pallas kernels, regroup_set(): pl.pallas_call(functools.partial(regroup_kernel, names), out_shape=jax.Sh...  15.5 us
    pallas_call x1, Pallas kernels, last_products(): pl.pallas_call(functools.partial(last_kernel, names), out_shape=(jax.Shap...  12 us
    unnamed x12, local copies, waits for them, and re-layouts  4.5 us
    pallas_call x1, Pallas kernels, early_products(): pl.pallas_call(early_kernel, out_shape=jax.ShapeDtypeStruct((768, 512), F...  3.4 us
  transfers between devices with their start and end apart: 26, of which 10 were waited for; matrix products, arithmetic and copies ran while one was open for 0% of the time, Pallas kernels for 18%

profile of v4, /device:TPU:0, one launch (start us, length us, event | category | flops | bytes accessed | tf_op | source)
XLA Modules:
  0.0 105.7 jit_solution(11957410182671397278)
XLA Ops:
  0.6 1.2 %copy-done = bf16[30,32,480]{2,1,0:T(8,128)(2,1)S(1)} copy-done((bf16[30,32,480]{2,1,0:T(8,128)(2,1)S(1)}, bf16[30,32,480]{2,1,0:T(8,128)(2,1)}, u32[]{:S(2)}) %copy-start) | copy-done | bytes 921624
  1.8 0.7 copy-done.5
  3.6 2.0 %collective-permute-start.1 = (bf16[30,64,240]{2,1,0:T(8,128)(2,1)}, bf16[30,64,240]{2,1,0:T(8,128)(2,1)S(1)}, u32[]{:S(2)}, u32[]{:S(2)}) collective-permute-start(bf16[30,64,240]{2,1,0:T(8,128)(2,1)} %bitcast.7), channel_id=1, source_target_pairs={{0,4},{1,13},{2,6},{3,15},{4,8},{5,1},{6,10},{7,3},{8,12},{9,5},{1... | collective-permute-start | bytes 2764808 | tf_op jit(solution)/shard_map/c1/ppermute | solution.py:256
  5.6 1.6 %collective-permute-start.2 = (bf16[30,64,240]{2,1,0:T(8,128)(2,1)}, bf16[30,64,240]{2,1,0:T(8,128)(2,1)S(1)}, u32[]{:S(2)}, u32[]{:S(2)}) collective-permute-start(bf16[30,64,240]{2,1,0:T(8,128)(2,1)} %bitcast.8), channel_id=1, source_target_pairs={{0,2},{1,3},{2,0},{3,1},{4,6},{5,7},{6,4},{7,5},{8,10},{9,11},{10,... | collective-permute-start | bytes 2764808 | tf_op jit(solution)/shard_map/aq/ppermute | solution.py:256
  7.2 1.5 %collective-permute-start.7 = (bf16[32,32,512]{2,1,0:T(8,128)(2,1)S(1)}, bf16[32,32,512]{2,1,0:T(8,128)(2,1)S(1)}, u32[]{:S(2)}, u32[]{:S(2)}) collective-permute-start(bf16[32,32,512]{2,1,0:T(8,128)(2,1)S(1)} %prepare_b.1.refs_3_.refs_16_), channel_id=1, source_target_pairs={{0,32},{1,97},{2,34},{3,99},{4,36},{5,101},{6,38},{7,103},{8,40},{... | collective-permute-start | bytes 3145736 | tf_op jit(solution)/shard_map/d1/ppermute | solution.py:256
  8.7 1.9 %collective-permute-start.3 = (bf16[30,64,240]{2,1,0:T(8,128)(2,1)S(1)}, bf16[30,64,240]{2,1,0:T(8,128)(2,1)S(1)}, u32[]{:S(2)}, u32[]{:S(2)}) collective-permute-start(bf16[30,64,240]{2,1,0:T(8,128)(2,1)S(1)} %collective-permute-done.p1.refs_1_), channel_id=1, source_target_pairs={{0,4},{1,13},{2,6},{3,15},{4,8},{5,1},{6,10},{7,3},{8,12},{9,5},{1... | collective-permute-start | bytes 2764808 | tf_op jit(solution)/shard_map/c2/ppermute | solution.py:256
  10.6 9.4 %collective-permute-done.1.p2.refs_2_ = bf16[30,64,240]{2,1,0:T(8,128)(2,1)S(1)} collective-permute-done((bf16[30,64,240]{2,1,0:T(8,128)(2,1)}, bf16[30,64,240]{2,1,0:T(8,128)(2,1)S(1)}, u32[]{:S(2)}, u32[]{:S(2)}) %collective-permute-start.1) | collective-permute-done | bytes 921632 | tf_op jit(solution)/shard_map/c1/ppermute | solution.py:256
  20.0 3.2 %collective-permute-start.14 = (bf16[32,32,512]{2,1,0:T(8,128)(2,1)S(1)}, bf16[32,32,512]{2,1,0:T(8,128)(2,1)S(1)}, u32[]{:S(2)}, u32[]{:S(2)}) collective-permute-start(bf16[32,32,512]{2,1,0:T(8,128)(2,1)S(1)} %prepare_b.1.refs_3_.refs_16_), channel_id=1, source_target_pairs={{0,16},{1,17},{2,18},{3,19},{4,20},{5,21},{6,22},{7,23},{8,24},{9,... | collective-permute-start | bytes 3145736 | tf_op jit(solution)/shard_map/bq/ppermute | solution.py:256
  23.2 6.3 %collective-permute-done.2.p3.refs_3_ = bf16[30,64,240]{2,1,0:T(8,128)(2,1)S(1)} collective-permute-done((bf16[30,64,240]{2,1,0:T(8,128)(2,1)}, bf16[30,64,240]{2,1,0:T(8,128)(2,1)S(1)}, u32[]{:S(2)}, u32[]{:S(2)}) %collective-permute-start.2) | collective-permute-done | bytes 921632 | tf_op jit(solution)/shard_map/aq/ppermute | solution.py:256
  29.5 1.5 %collective-permute-start.9 = (bf16[32,32,512]{2,1,0:T(8,128)(2,1)S(1)}, bf16[32,32,512]{2,1,0:T(8,128)(2,1)S(1)}, u32[]{:S(2)}, u32[]{:S(2)}) collective-permute-start(bf16[32,32,512]{2,1,0:T(8,128)(2,1)S(1)} %collective-permute-done.6), channel_id=1, source_target_pairs={{0,32},{1,97},{2,34},{3,99},{4,36},{5,101},{6,38},{7,103},{8,40},{... | collective-permute-start | bytes 3145736 | tf_op jit(solution)/shard_map/d2/ppermute | solution.py:256
  31.0 1.2 %copy-done.1 = bf16[30,240,64]{1,2,0:T(8,128)(2,1)S(1)} copy-done((bf16[30,240,64]{1,2,0:T(8,128)(2,1)S(1)}, bf16[30,240,64]{1,2,0:T(8,128)(2,1)}, u32[]{:S(2)}) %copy-start.1) | copy-done | bytes 921624
  32.2 0.7 copy-done.3
  33.6 3.9 %regroup_a.1.refs_0_.refs_24_ = bf16[32,256,256]{2,1,0:T(8,128)(2,1)S(1)} custom-call(s32[8,8]{1,0:T(8,128)S(1)} %copy-done.4, s32[16,16]{1,0:T(8,128)S(1)} %copy-done.3, bf16[30,64,240]{2,1,0:T(8,128)(2,1)S(1)} %bitcast.9, bf16[30,64,240]{2,1,0:T(8,128)(2,1)S(1)} %collective-permute-done.p1.refs_1_, ...), custom_call_target="tpu_custom_call" | custom-call | flops 1000 | bytes 1000 | tf_op jit(solution)/shard_map/regroup_a/pallas_call | solution.py:111
  37.4 3.1 %collective-permute-start.5 = (bf16[30,64,240]{2,1,0:T(8,128)(2,1)S(1)}, bf16[30,64,240]{2,1,0:T(8,128)(2,1)S(1)}, u32[]{:S(2)}, u32[]{:S(2)}) collective-permute-start(bf16[30,64,240]{2,1,0:T(8,128)(2,1)S(1)} %collective-permute-done.2.p3.refs_3_), channel_id=1, source_target_pairs={{0,1},{1,0},{2,3},{3,2},{4,5},{5,4},{6,7},{7,6},{8,9},{9,8},{10,11... | collective-permute-start | bytes 2764808 | tf_op jit(solution)/shard_map/s_aq/ppermute | solution.py:256
  41.1 1.5 %collective-permute-start.12 = (bf16[32,32,512]{2,1,0:T(8,128)(2,1)S(1)}, bf16[32,32,512]{2,1,0:T(8,128)(2,1)S(1)}, u32[]{:S(2)}, u32[]{:S(2)}) collective-permute-start(bf16[32,32,512]{2,1,0:T(8,128)(2,1)S(1)} %collective-permute-done.7.refs_4_.refs_17_), channel_id=1, source_target_pairs={{0,32},{1,97},{2,34},{3,99},{4,36},{5,101},{6,38},{7,103},{8,40},{... | collective-permute-start | bytes 3145736 | tf_op jit(solution)/shard_map/d5/ppermute | solution.py:256
  42.6 11.8 %collective-permute-done.14.refs_20_ = bf16[32,32,512]{2,1,0:T(8,128)(2,1)S(1)} collective-permute-done((bf16[32,32,512]{2,1,0:T(8,128)(2,1)S(1)}, bf16[32,32,512]{2,1,0:T(8,128)(2,1)S(1)}, u32[]{:S(2)}, u32[]{:S(2)}) %collective-permute-start.14) | collective-permute-done | bytes 1048608 | tf_op jit(solution)/shard_map/bq/ppermute | solution.py:256
  54.4 0.8 collective-permute-start.15
  55.2 1.6 %collective-permute-start.17 = (bf16[32,32,512]{2,1,0:T(8,128)(2,1)S(1)}, bf16[32,32,512]{2,1,0:T(8,128)(2,1)S(1)}, u32[]{:S(2)}, u32[]{:S(2)}) collective-permute-start(bf16[32,32,512]{2,1,0:T(8,128)(2,1)S(1)} %collective-permute-done.14.refs_20_), channel_id=1, source_target_pairs={{0,32},{1,97},{2,34},{3,99},{4,36},{5,101},{6,38},{7,103},{8,40},{... | collective-permute-start | bytes 3145736 | tf_op jit(solution)/shard_map/dq1/ppermute | solution.py:256
  56.7 1.1 %collective-permute-done.8.p3.refs_7_ = bf16[30,64,240]{2,1,0:T(8,128)(2,1)S(1)} collective-permute-done((bf16[30,64,240]{2,1,0:T(8,128)(2,1)S(1)}, bf16[30,64,240]{2,1,0:T(8,128)(2,1)S(1)}, u32[]{:S(2)}, u32[]{:S(2)}) %collective-permute-start.8) | collective-permute-done | bytes 921632 | tf_op jit(solution)/shard_map/cq1/ppermute | solution.py:256
  58.2 1.5 %collective-permute-start.13 = (bf16[30,64,240]{2,1,0:T(8,128)(2,1)S(1)}, bf16[30,64,240]{2,1,0:T(8,128)(2,1)S(1)}, u32[]{:S(2)}, u32[]{:S(2)}) collective-permute-start(bf16[30,64,240]{2,1,0:T(8,128)(2,1)S(1)} %collective-permute-done.5.p2.refs_6_), channel_id=1, source_target_pairs={{0,4},{1,13},{2,6},{3,15},{4,8},{5,1},{6,10},{7,3},{8,12},{9,5},{1... | collective-permute-start | bytes 2764808 | tf_op jit(solution)/shard_map/cq2/ppermute | solution.py:256
  59.7 3.9 %regroup_c2.1.refs_1_.refs_25_ = bf16[32,256,256]{2,1,0:T(8,128)(2,1)S(1)} custom-call(s32[8,8]{1,0:T(8,128)S(1)} %copy-done.4, s32[16,16]{1,0:T(8,128)S(1)} %copy-done.3, bf16[30,64,240]{2,1,0:T(8,128)(2,1)S(1)} %collective-permute-done.3.p0.refs_4_, bf16[30,64,240]{2,1,0:T(8,128)(2,1)S(1)} %collective-permute-done.4.p1.refs_5_, ...), custom_call_target="tpu_custom_call" | custom-call | flops 1000 | bytes 1000 | tf_op jit(solution)/shard_map/regroup_c2/pallas_call | solution.py:111
  64.6 1.2 %collective-permute-start.19 = (bf16[30,64,240]{2,1,0:T(8,128)(2,1)S(1)}, bf16[30,64,240]{2,1,0:T(8,128)(2,1)S(1)}, u32[]{:S(2)}, u32[]{:S(2)}) collective-permute-start(bf16[30,64,240]{2,1,0:T(8,128)(2,1)S(1)} %collective-permute-done.8.p3.refs_7_), channel_id=1, source_target_pairs={{0,4},{1,13},{2,6},{3,15},{4,8},{5,1},{6,10},{7,3},{8,12},{9,5},{1... | collective-permute-start | bytes 2764808 | tf_op jit(solution)/shard_map/cq5/ppermute | solution.py:256
  65.8 5.5 %collective-permute-done.17.refs_21_ = bf16[32,32,512]{2,1,0:T(8,128)(2,1)S(1)} collective-permute-done((bf16[32,32,512]{2,1,0:T(8,128)(2,1)S(1)}, bf16[32,32,512]{2,1,0:T(8,128)(2,1)S(1)}, u32[]{:S(2)}, u32[]{:S(2)}) %collective-permute-start.17) | collective-permute-done | bytes 1048608 | tf_op jit(solution)/shard_map/dq1/ppermute | solution.py:256
  71.3 2.2 %collective-permute-done.13.p2.refs_10_ = bf16[30,64,240]{2,1,0:T(8,128)(2,1)S(1)} collective-permute-done((bf16[30,64,240]{2,1,0:T(8,128)(2,1)S(1)}, bf16[30,64,240]{2,1,0:T(8,128)(2,1)S(1)}, u32[]{:S(2)}, u32[]{:S(2)}) %collective-permute-start.13) | collective-permute-done | bytes 921632 | tf_op jit(solution)/shard_map/cq2/ppermute | solution.py:256
  74.0 1.2 %collective-permute-start.25 = (bf16[32,32,512]{2,1,0:T(8,128)(2,1)S(1)}, bf16[32,32,512]{2,1,0:T(8,128)(2,1)S(1)}, u32[]{:S(2)}, u32[]{:S(2)}) collective-permute-start(bf16[32,32,512]{2,1,0:T(8,128)(2,1)S(1)} %collective-permute-done.17.refs_21_), channel_id=1, source_target_pairs={{0,32},{1,97},{2,34},{3,99},{4,36},{5,101},{6,38},{7,103},{8,40},{... | collective-permute-start | bytes 3145736 | tf_op jit(solution)/shard_map/dq5/ppermute | solution.py:256
  75.2 3.9 %regroup_s_c5.1.refs_2_.refs_26_ = bf16[32,256,256]{2,1,0:T(8,128)(2,1)S(1)} custom-call(s32[8,8]{1,0:T(8,128)S(1)} %copy-done.4, s32[16,16]{1,0:T(8,128)S(1)} %copy-done.3, bf16[30,64,240]{2,1,0:T(8,128)(2,1)S(1)} %collective-permute-done.10.p0.refs_8_, bf16[30,64,240]{2,1,0:T(8,128)(2,1)S(1)} %collective-permute-done.11.p1.refs_9_, ...), custom_call_target="tpu_custom_call" | custom-call | flops 1000 | bytes 1000 | tf_op jit(solution)/shard_map/regroup_s_c5/pallas_call | solution.py:111
  79.1 3.4 %collective-permute-done.23 = bf16[32,32,512]{2,1,0:T(8,128)(2,1)S(1)} collective-permute-done((bf16[32,32,512]{2,1,0:T(8,128)(2,1)S(1)}, bf16[32,32,512]{2,1,0:T(8,128)(2,1)S(1)}, u32[]{:S(2)}, u32[]{:S(2)}) %collective-permute-start.23) | collective-permute-done | bytes 1048608 | tf_op jit(solution)/shard_map/dq2/ppermute | solution.py:256
  82.5 1.5 %collective-permute-done.19.p1.refs_13_ = bf16[30,64,240]{2,1,0:T(8,128)(2,1)S(1)} collective-permute-done((bf16[30,64,240]{2,1,0:T(8,128)(2,1)S(1)}, bf16[30,64,240]{2,1,0:T(8,128)(2,1)S(1)}, u32[]{:S(2)}, u32[]{:S(2)}) %collective-permute-start.19) | collective-permute-done | bytes 921632 | tf_op jit(solution)/shard_map/cq5/ppermute | solution.py:256
  84.5 3.4 %early.1.refs_28_ = f32[768,512]{1,0:T(8,128)S(1)} custom-call(bf16[32,256,256]{2,1,0:T(8,128)(2,1)S(1)} %regroup_a.1.refs_0_.refs_24_, bf16[32,256,256]{2,1,0:T(8,128)(2,1)S(1)} %regroup_c2.1.refs_1_.refs_25_, bf16[32,256,256]{2,1,0:T(8,128)(2,1)S(1)} %regroup_s_c5.1.refs_2_.refs_26_, bf16[32,32,512]{2,1,0:T(8,128)(2,1)S(1)} %prepare_b.1.refs_3_.refs_16_, ...), custom_call_target="tpu_custom_call" | custom-call | flops 1000 | bytes 1000 | tf_op jit(solution)/shard_map/early/pallas_call | solution.py:186
  88.0 3.9 %regroup_s_cq2.1.refs_27_ = bf16[32,256,256]{2,1,0:T(8,128)(2,1)S(1)} custom-call(s32[8,8]{1,0:T(8,128)S(1)} %copy-done.4, s32[16,16]{1,0:T(8,128)S(1)} %copy-done.3, bf16[30,64,240]{2,1,0:T(8,128)(2,1)S(1)} %collective-permute-done.18.p0.refs_12_, bf16[30,64,240]{2,1,0:T(8,128)(2,1)S(1)} %collective-permute-done.19.p1.refs_13_, ...), custom_call_target="tpu_custom_call" | custom-call | flops 1000 | bytes 1000 | tf_op jit(solution)/shard_map/regroup_s_cq2/pallas_call | solution.py:111
  91.9 1.9 %collective-permute-done.25.refs_23_ = bf16[32,32,512]{2,1,0:T(8,128)(2,1)S(1)} collective-permute-done((bf16[32,32,512]{2,1,0:T(8,128)(2,1)S(1)}, bf16[32,32,512]{2,1,0:T(8,128)(2,1)S(1)}, u32[]{:S(2)}, u32[]{:S(2)}) %collective-permute-start.25) | collective-permute-done | bytes 1048608 | tf_op jit(solution)/shard_map/dq5/ppermute | solution.py:256
  93.7 12.0 %last.1 = (bf16[30,64,240]{2,1,0:T(8,128)(2,1)}, bf16[960,480]{1,0:T(8,128)(2,1)}) custom-call(s32[8,8]{1,0:T(8,128)S(1)} %copy-done.4, s32[16,16]{1,0:T(8,128)S(1)} %copy-done.3, bf16[30,64,240]{2,1,0:T(8,128)(2,1)S(1)} %bitcast.10, bf16[30,64,240]{2,1,0:T(8,128)(2,1)S(1)} %collective-permute-done.p1.refs_1_, ...), custom_call_target="tpu_custom_call" | custom-call | flops 12000000000 | bytes 38000000 | tf_op jit(solution)/shard_map/last/pallas_call | solution.py:234
  (39 shorter events, 4.7 us)
Async XLA Ops:
  0.6 1.2 %copy-start = (bf16[30,32,480]{2,1,0:T(8,128)(2,1)S(1)}, bf16[30,32,480]{2,1,0:T(8,128)(2,1)}, u32[]{:S(2)}) copy-start(bf16[30,32,480]{2,1,0:T(8,128)(2,1)} %param.7) | copy-start | bytes 2764804
  1.8 0.7 copy-start.5
  3.0 4.2 %collective-permute-start.6 = (bf16[32,32,512]{2,1,0:T(8,128)(2,1)S(1)}, bf16[32,32,512]{2,1,0:T(8,128)(2,1)S(1)}, u32[]{:S(2)}, u32[]{:S(2)}) collective-permute-start(bf16[32,32,512]{2,1,0:T(8,128)(2,1)S(1)} %prepare_b.1.refs_3_.refs_16_), channel_id=1, source_target_pairs={{0,1},{1,0},{2,3},{3,2},{4,5},{5,4},{6,7},{7,6},{8,9},{9,8},{10,11... | collective-permute-start | bytes 3145736 | tf_op jit(solution)/shard_map/s_b/ppermute | solution.py:256
  3.1 5.6 %collective-permute-start = (bf16[30,64,240]{2,1,0:T(8,128)(2,1)}, bf16[30,64,240]{2,1,0:T(8,128)(2,1)S(1)}, u32[]{:S(2)}, u32[]{:S(2)}) collective-permute-start(bf16[30,64,240]{2,1,0:T(8,128)(2,1)} %bitcast.6), channel_id=1, source_target_pairs={{0,1},{1,0},{2,3},{3,2},{4,5},{5,4},{6,7},{7,6},{8,9},{9,8},{10,11... | collective-permute-start | bytes 2764808 | tf_op jit(solution)/shard_map/s_a/ppermute | solution.py:256
  3.6 16.4 %collective-permute-start.1 = (bf16[30,64,240]{2,1,0:T(8,128)(2,1)}, bf16[30,64,240]{2,1,0:T(8,128)(2,1)S(1)}, u32[]{:S(2)}, u32[]{:S(2)}) collective-permute-start(bf16[30,64,240]{2,1,0:T(8,128)(2,1)} %bitcast.7), channel_id=1, source_target_pairs={{0,4},{1,13},{2,6},{3,15},{4,8},{5,1},{6,10},{7,3},{8,12},{9,5},{1... | collective-permute-start | bytes 2764808 | tf_op jit(solution)/shard_map/c1/ppermute | solution.py:256
  5.6 23.9 %collective-permute-start.2 = (bf16[30,64,240]{2,1,0:T(8,128)(2,1)}, bf16[30,64,240]{2,1,0:T(8,128)(2,1)S(1)}, u32[]{:S(2)}, u32[]{:S(2)}) collective-permute-start(bf16[30,64,240]{2,1,0:T(8,128)(2,1)} %bitcast.8), channel_id=1, source_target_pairs={{0,2},{1,3},{2,0},{3,1},{4,6},{5,7},{6,4},{7,5},{8,10},{9,11},{10,... | collective-permute-start | bytes 2764808 | tf_op jit(solution)/shard_map/aq/ppermute | solution.py:256
  7.2 33.9 %collective-permute-start.7 = (bf16[32,32,512]{2,1,0:T(8,128)(2,1)S(1)}, bf16[32,32,512]{2,1,0:T(8,128)(2,1)S(1)}, u32[]{:S(2)}, u32[]{:S(2)}) collective-permute-start(bf16[32,32,512]{2,1,0:T(8,128)(2,1)S(1)} %prepare_b.1.refs_3_.refs_16_), channel_id=1, source_target_pairs={{0,32},{1,97},{2,34},{3,99},{4,36},{5,101},{6,38},{7,103},{8,40},{... | collective-permute-start | bytes 3145736 | tf_op jit(solution)/shard_map/d1/ppermute | solution.py:256
  8.7 28.8 %collective-permute-start.3 = (bf16[30,64,240]{2,1,0:T(8,128)(2,1)S(1)}, bf16[30,64,240]{2,1,0:T(8,128)(2,1)S(1)}, u32[]{:S(2)}, u32[]{:S(2)}) collective-permute-start(bf16[30,64,240]{2,1,0:T(8,128)(2,1)S(1)} %collective-permute-done.p1.refs_1_), channel_id=1, source_target_pairs={{0,4},{1,13},{2,6},{3,15},{4,8},{5,1},{6,10},{7,3},{8,12},{9,5},{1... | collective-permute-start | bytes 2764808 | tf_op jit(solution)/shard_map/c2/ppermute | solution.py:256
  20.0 21.1 %collective-permute-start.4 = (bf16[30,64,240]{2,1,0:T(8,128)(2,1)S(1)}, bf16[30,64,240]{2,1,0:T(8,128)(2,1)S(1)}, u32[]{:S(2)}, u32[]{:S(2)}) collective-permute-start(bf16[30,64,240]{2,1,0:T(8,128)(2,1)S(1)} %collective-permute-done.1.p2.refs_2_), channel_id=1, source_target_pairs={{0,4},{1,13},{2,6},{3,15},{4,8},{5,1},{6,10},{7,3},{8,12},{9,5},{1... | collective-permute-start | bytes 2764808 | tf_op jit(solution)/shard_map/c5/ppermute | solution.py:256
  20.0 34.4 %collective-permute-start.14 = (bf16[32,32,512]{2,1,0:T(8,128)(2,1)S(1)}, bf16[32,32,512]{2,1,0:T(8,128)(2,1)S(1)}, u32[]{:S(2)}, u32[]{:S(2)}) collective-permute-start(bf16[32,32,512]{2,1,0:T(8,128)(2,1)S(1)} %prepare_b.1.refs_3_.refs_16_), channel_id=1, source_target_pairs={{0,16},{1,17},{2,18},{3,19},{4,20},{5,21},{6,22},{7,23},{8,24},{9,... | collective-permute-start | bytes 3145736 | tf_op jit(solution)/shard_map/bq/ppermute | solution.py:256
  29.5 25.7 %collective-permute-start.9 = (bf16[32,32,512]{2,1,0:T(8,128)(2,1)S(1)}, bf16[32,32,512]{2,1,0:T(8,128)(2,1)S(1)}, u32[]{:S(2)}, u32[]{:S(2)}) collective-permute-start(bf16[32,32,512]{2,1,0:T(8,128)(2,1)S(1)} %collective-permute-done.6), channel_id=1, source_target_pairs={{0,32},{1,97},{2,34},{3,99},{4,36},{5,101},{6,38},{7,103},{8,40},{... | collective-permute-start | bytes 3145736 | tf_op jit(solution)/shard_map/d2/ppermute | solution.py:256
  31.0 1.2 %copy-start.1 = (bf16[30,240,64]{1,2,0:T(8,128)(2,1)S(1)}, bf16[30,240,64]{1,2,0:T(8,128)(2,1)}, u32[]{:S(2)}) copy-start(bf16[30,240,64]{1,2,0:T(8,128)(2,1)} %param.5) | copy-start | bytes 2764804
  32.2 0.7 copy-start.3
  32.9 0.7 copy-start.4
  37.4 17.7 %collective-permute-start.5 = (bf16[30,64,240]{2,1,0:T(8,128)(2,1)S(1)}, bf16[30,64,240]{2,1,0:T(8,128)(2,1)S(1)}, u32[]{:S(2)}, u32[]{:S(2)}) collective-permute-start(bf16[30,64,240]{2,1,0:T(8,128)(2,1)S(1)} %collective-permute-done.2.p3.refs_3_), channel_id=1, source_target_pairs={{0,1},{1,0},{2,3},{3,2},{4,5},{5,4},{6,7},{7,6},{8,9},{9,8},{10,11... | collective-permute-start | bytes 2764808 | tf_op jit(solution)/shard_map/s_aq/ppermute | solution.py:256
  41.1 17.1 %collective-permute-start.12 = (bf16[32,32,512]{2,1,0:T(8,128)(2,1)S(1)}, bf16[32,32,512]{2,1,0:T(8,128)(2,1)S(1)}, u32[]{:S(2)}, u32[]{:S(2)}) collective-permute-start(bf16[32,32,512]{2,1,0:T(8,128)(2,1)S(1)} %collective-permute-done.7.refs_4_.refs_17_), channel_id=1, source_target_pairs={{0,32},{1,97},{2,34},{3,99},{4,36},{5,101},{6,38},{7,103},{8,40},{... | collective-permute-start | bytes 3145736 | tf_op jit(solution)/shard_map/d5/ppermute | solution.py:256
  42.6 15.3 %collective-permute-start.8 = (bf16[30,64,240]{2,1,0:T(8,128)(2,1)S(1)}, bf16[30,64,240]{2,1,0:T(8,128)(2,1)S(1)}, u32[]{:S(2)}, u32[]{:S(2)}) collective-permute-start(bf16[30,64,240]{2,1,0:T(8,128)(2,1)S(1)} %collective-permute-done.2.p3.refs_3_), channel_id=1, source_target_pairs={{0,4},{1,13},{2,6},{3,15},{4,8},{5,1},{6,10},{7,3},{8,12},{9,5},{1... | collective-permute-start | bytes 2764808 | tf_op jit(solution)/shard_map/cq1/ppermute | solution.py:256
  54.4 9.1 %collective-permute-start.15 = (bf16[32,32,512]{2,1,0:T(8,128)(2,1)S(1)}, bf16[32,32,512]{2,1,0:T(8,128)(2,1)S(1)}, u32[]{:S(2)}, u32[]{:S(2)}) collective-permute-start(bf16[32,32,512]{2,1,0:T(8,128)(2,1)S(1)} %collective-permute-done.14.refs_20_), channel_id=1, source_target_pairs={{0,1},{1,0},{2,3},{3,2},{4,5},{5,4},{6,7},{7,6},{8,9},{9,8},{10,11... | collective-permute-start | bytes 3145736 | tf_op jit(solution)/shard_map/s_bq/ppermute | solution.py:256
  55.2 8.4 %collective-permute-start.10 = (bf16[30,64,240]{2,1,0:T(8,128)(2,1)S(1)}, bf16[30,64,240]{2,1,0:T(8,128)(2,1)S(1)}, u32[]{:S(2)}, u32[]{:S(2)}) collective-permute-start(bf16[30,64,240]{2,1,0:T(8,128)(2,1)S(1)} %collective-permute-done.4.p1.refs_5_), channel_id=1, source_target_pairs={{0,1},{1,0},{2,3},{3,2},{4,5},{5,4},{6,7},{7,6},{8,9},{9,8},{10,11... | collective-permute-start | bytes 2764808 | tf_op jit(solution)/shard_map/s_c5/ppermute | solution.py:256
  55.2 16.1 %collective-permute-start.17 = (bf16[32,32,512]{2,1,0:T(8,128)(2,1)S(1)}, bf16[32,32,512]{2,1,0:T(8,128)(2,1)S(1)}, u32[]{:S(2)}, u32[]{:S(2)}) collective-permute-start(bf16[32,32,512]{2,1,0:T(8,128)(2,1)S(1)} %collective-permute-done.14.refs_20_), channel_id=1, source_target_pairs={{0,32},{1,97},{2,34},{3,99},{4,36},{5,101},{6,38},{7,103},{8,40},{... | collective-permute-start | bytes 3145736 | tf_op jit(solution)/shard_map/dq1/ppermute | solution.py:256
  57.9 6.7 %collective-permute-start.11 = (bf16[30,64,240]{2,1,0:T(8,128)(2,1)S(1)}, bf16[30,64,240]{2,1,0:T(8,128)(2,1)S(1)}, u32[]{:S(2)}, u32[]{:S(2)}) collective-permute-start(bf16[30,64,240]{2,1,0:T(8,128)(2,1)S(1)} %collective-permute-done.8.p3.refs_7_), channel_id=1, source_target_pairs={{0,1},{1,0},{2,3},{3,2},{4,5},{5,4},{6,7},{7,6},{8,9},{9,8},{10,11... | collective-permute-start | bytes 2764808 | tf_op jit(solution)/shard_map/s_cq1/ppermute | solution.py:256
  58.2 15.3 %collective-permute-start.13 = (bf16[30,64,240]{2,1,0:T(8,128)(2,1)S(1)}, bf16[30,64,240]{2,1,0:T(8,128)(2,1)S(1)}, u32[]{:S(2)}, u32[]{:S(2)}) collective-permute-start(bf16[30,64,240]{2,1,0:T(8,128)(2,1)S(1)} %collective-permute-done.5.p2.refs_6_), channel_id=1, source_target_pairs={{0,4},{1,13},{2,6},{3,15},{4,8},{5,1},{6,10},{7,3},{8,12},{9,5},{1... | collective-permute-start | bytes 2764808 | tf_op jit(solution)/shard_map/cq2/ppermute | solution.py:256
  63.6 18.9 %collective-permute-start.23 = (bf16[32,32,512]{2,1,0:T(8,128)(2,1)S(1)}, bf16[32,32,512]{2,1,0:T(8,128)(2,1)S(1)}, u32[]{:S(2)}, u32[]{:S(2)}) collective-permute-start(bf16[32,32,512]{2,1,0:T(8,128)(2,1)S(1)} %collective-permute-done.15), channel_id=1, source_target_pairs={{0,32},{1,97},{2,34},{3,99},{4,36},{5,101},{6,38},{7,103},{8,40},{... | collective-permute-start | bytes 3145736 | tf_op jit(solution)/shard_map/dq2/ppermute | solution.py:256
  63.9 9.6 %collective-permute-start.16 = (bf16[30,64,240]{2,1,0:T(8,128)(2,1)S(1)}, bf16[30,64,240]{2,1,0:T(8,128)(2,1)S(1)}, u32[]{:S(2)}, u32[]{:S(2)}) collective-permute-start(bf16[30,64,240]{2,1,0:T(8,128)(2,1)S(1)} %collective-permute-done.1.p2.refs_2_), channel_id=1, source_target_pairs={{0,1},{1,0},{2,3},{3,2},{4,5},{5,4},{6,7},{7,6},{8,9},{9,8},{10,11... | collective-permute-start | bytes 2764808 | tf_op jit(solution)/shard_map/s_c1/ppermute | solution.py:256
  64.6 19.5 %collective-permute-start.19 = (bf16[30,64,240]{2,1,0:T(8,128)(2,1)S(1)}, bf16[30,64,240]{2,1,0:T(8,128)(2,1)S(1)}, u32[]{:S(2)}, u32[]{:S(2)}) collective-permute-start(bf16[30,64,240]{2,1,0:T(8,128)(2,1)S(1)} %collective-permute-done.8.p3.refs_7_), channel_id=1, source_target_pairs={{0,4},{1,13},{2,6},{3,15},{4,8},{5,1},{6,10},{7,3},{8,12},{9,5},{1... | collective-permute-start | bytes 2764808 | tf_op jit(solution)/shard_map/cq5/ppermute | solution.py:256
  73.5 10.5 %collective-permute-start.18 = (bf16[30,64,240]{2,1,0:T(8,128)(2,1)S(1)}, bf16[30,64,240]{2,1,0:T(8,128)(2,1)S(1)}, u32[]{:S(2)}, u32[]{:S(2)}) collective-permute-start(bf16[30,64,240]{2,1,0:T(8,128)(2,1)S(1)} %collective-permute-done.13.p2.refs_10_), channel_id=1, source_target_pairs={{0,1},{1,0},{2,3},{3,2},{4,5},{5,4},{6,7},{7,6},{8,9},{9,8},{10,11... | collective-permute-start | bytes 2764808 | tf_op jit(solution)/shard_map/s_cq2/ppermute | solution.py:256
  73.5 11.0 %collective-permute-start.22 = (bf16[32,32,512]{2,1,0:T(8,128)(2,1)S(1)}, bf16[32,32,512]{2,1,0:T(8,128)(2,1)S(1)}, u32[]{:S(2)}, u32[]{:S(2)}) collective-permute-start(bf16[32,32,512]{2,1,0:T(8,128)(2,1)S(1)} %collective-permute-done.9), channel_id=1, source_target_pairs={{0,1},{1,0},{2,3},{3,2},{4,5},{5,4},{6,7},{7,6},{8,9},{9,8},{10,11... | collective-permute-start | bytes 3145736 | tf_op jit(solution)/shard_map/s_d2/ppermute | solution.py:256
  74.0 19.7 %collective-permute-start.25 = (bf16[32,32,512]{2,1,0:T(8,128)(2,1)S(1)}, bf16[32,32,512]{2,1,0:T(8,128)(2,1)S(1)}, u32[]{:S(2)}, u32[]{:S(2)}) collective-permute-start(bf16[32,32,512]{2,1,0:T(8,128)(2,1)S(1)} %collective-permute-done.17.refs_21_), channel_id=1, source_target_pairs={{0,32},{1,97},{2,34},{3,99},{4,36},{5,101},{6,38},{7,103},{8,40},{... | collective-permute-start | bytes 3145736 | tf_op jit(solution)/shard_map/dq5/ppermute | solution.py:256
  82.5 11.2 %collective-permute-start.24 = (bf16[32,32,512]{2,1,0:T(8,128)(2,1)S(1)}, bf16[32,32,512]{2,1,0:T(8,128)(2,1)S(1)}, u32[]{:S(2)}, u32[]{:S(2)}) collective-permute-start(bf16[32,32,512]{2,1,0:T(8,128)(2,1)S(1)} %collective-permute-done.23), channel_id=1, source_target_pairs={{0,1},{1,0},{2,3},{3,2},{4,5},{5,4},{6,7},{7,6},{8,9},{9,8},{10,11... | collective-permute-start | bytes 3145736 | tf_op jit(solution)/shard_map/s_dq2/ppermute | solution.py:256
  84.0 3.9 %collective-permute-start.21 = (bf16[30,64,240]{2,1,0:T(8,128)(2,1)S(1)}, bf16[30,64,240]{2,1,0:T(8,128)(2,1)S(1)}, u32[]{:S(2)}, u32[]{:S(2)}) collective-permute-start(bf16[30,64,240]{2,1,0:T(8,128)(2,1)S(1)} %collective-permute-done.3.p0.refs_4_), channel_id=1, source_target_pairs={{0,1},{1,0},{2,3},{3,2},{4,5},{5,4},{6,7},{7,6},{8,9},{9,8},{10,11... | collective-permute-start | bytes 2764808 | tf_op jit(solution)/shard_map/s_c2/ppermute | solution.py:256
  84.0 4.0 %collective-permute-start.20 = (bf16[30,64,240]{2,1,0:T(8,128)(2,1)S(1)}, bf16[30,64,240]{2,1,0:T(8,128)(2,1)S(1)}, u32[]{:S(2)}, u32[]{:S(2)}) collective-permute-start(bf16[30,64,240]{2,1,0:T(8,128)(2,1)S(1)} %collective-permute-done.19.p1.refs_13_), channel_id=1, source_target_pairs={{0,1},{1,0},{2,3},{3,2},{4,5},{5,4},{6,7},{7,6},{8,9},{9,8},{10,11... | collective-permute-start | bytes 2764808 | tf_op jit(solution)/shard_map/s_cq5/ppermute | solution.py:256
  87.9 5.8 %copy-start.2 = (bf16[30,240,64]{1,2,0:T(8,128)(2,1)S(1)}, bf16[30,240,64]{1,2,0:T(8,128)(2,1)}, u32[]{:S(2)}) copy-start(bf16[30,240,64]{1,2,0:T(8,128)(2,1)} %param.5) | copy-start | bytes 2764804

commit v5 on v4

--- a/solution.py
+++ b/solution.py
@@ -217,7 +217,7 @@
         lad_out[i] = (dot(weights, right) * keep).astype(BF)
         return 0
 
-    lax.fori_loop(0, 30, step, 0, unroll=3)
+    lax.fori_loop(0, 30, step, 0, unroll=10)
     o, s = iota((256, 256), 0), iota((256, 256), 1)
     target = jnp.zeros((256, 256), jnp.int32)
     for k, name in enumerate(names):

time: 106 us -> 105 us (level)
  no operation moved by 1% of the time
where the time goes in v5:
time: 105 us
  waiting for transfers between devices  43.7 us (42%)
  Pallas kernels  30.4 us (29%)
  starting transfers between devices  25.4 us (24%)
  local copies, waits for them, and re-layouts  4.5 us (4%)
    ppermute x26, waiting for transfers between devices, permute(): return lax.ppermute(value, ('row', 'col'), pairs)  43.7 us
    ppermute x26, starting transfers between devices, permute(): return lax.ppermute(value, ('row', 'col'), pairs)  25.4 us
    pallas_call x4, Pallas kernels, regroup_set(): pl.pallas_call(functools.partial(regroup_kernel, names), out_shape=jax.Sh...  15.5 us
    pallas_call x1, Pallas kernels, last_products(): pl.pallas_call(functools.partial(last_kernel, names), out_shape=(jax.Shap...  11.1 us
    unnamed x12, local copies, waits for them, and re-layouts  4.5 us
    pallas_call x1, Pallas kernels, early_products(): pl.pallas_call(early_kernel, out_shape=jax.ShapeDtypeStruct((768, 512), F...  3.4 us
  transfers between devices with their start and end apart: 26, of which 10 were waited for; matrix products, arithmetic and copies ran while one was open for 0% of the time, Pallas kernels for 18%

profile of v5, /device:TPU:0, one launch (start us, length us, event | category | flops | bytes accessed | tf_op | source)
XLA Modules:
  0.0 104.9 jit_solution(2949298460072995950)
XLA Ops:
  0.6 1.2 %copy-done = bf16[30,32,480]{2,1,0:T(8,128)(2,1)S(1)} copy-done((bf16[30,32,480]{2,1,0:T(8,128)(2,1)S(1)}, bf16[30,32,480]{2,1,0:T(8,128)(2,1)}, u32[]{:S(2)}) %copy-start) | copy-done | bytes 921624
  1.8 0.7 copy-done.5
  3.6 2.0 %collective-permute-start.1 = (bf16[30,64,240]{2,1,0:T(8,128)(2,1)}, bf16[30,64,240]{2,1,0:T(8,128)(2,1)S(1)}, u32[]{:S(2)}, u32[]{:S(2)}) collective-permute-start(bf16[30,64,240]{2,1,0:T(8,128)(2,1)} %bitcast.7), channel_id=1, source_target_pairs={{0,4},{1,13},{2,6},{3,15},{4,8},{5,1},{6,10},{7,3},{8,12},{9,5},{1... | collective-permute-start | bytes 2764808 | tf_op jit(solution)/shard_map/c1/ppermute | solution.py:256
  5.6 1.6 %collective-permute-start.2 = (bf16[30,64,240]{2,1,0:T(8,128)(2,1)}, bf16[30,64,240]{2,1,0:T(8,128)(2,1)S(1)}, u32[]{:S(2)}, u32[]{:S(2)}) collective-permute-start(bf16[30,64,240]{2,1,0:T(8,128)(2,1)} %bitcast.8), channel_id=1, source_target_pairs={{0,2},{1,3},{2,0},{3,1},{4,6},{5,7},{6,4},{7,5},{8,10},{9,11},{10,... | collective-permute-start | bytes 2764808 | tf_op jit(solution)/shard_map/aq/ppermute | solution.py:256
  7.2 1.5 %collective-permute-start.7 = (bf16[32,32,512]{2,1,0:T(8,128)(2,1)S(1)}, bf16[32,32,512]{2,1,0:T(8,128)(2,1)S(1)}, u32[]{:S(2)}, u32[]{:S(2)}) collective-permute-start(bf16[32,32,512]{2,1,0:T(8,128)(2,1)S(1)} %prepare_b.1.refs_3_.refs_16_), channel_id=1, source_target_pairs={{0,32},{1,97},{2,34},{3,99},{4,36},{5,101},{6,38},{7,103},{8,40},{... | collective-permute-start | bytes 3145736 | tf_op jit(solution)/shard_map/d1/ppermute | solution.py:256
  8.7 1.9 %collective-permute-start.3 = (bf16[30,64,240]{2,1,0:T(8,128)(2,1)S(1)}, bf16[30,64,240]{2,1,0:T(8,128)(2,1)S(1)}, u32[]{:S(2)}, u32[]{:S(2)}) collective-permute-start(bf16[30,64,240]{2,1,0:T(8,128)(2,1)S(1)} %collective-permute-done.p1.refs_1_), channel_id=1, source_target_pairs={{0,4},{1,13},{2,6},{3,15},{4,8},{5,1},{6,10},{7,3},{8,12},{9,5},{1... | collective-permute-start | bytes 2764808 | tf_op jit(solution)/shard_map/c2/ppermute | solution.py:256
  10.6 9.4 %collective-permute-done.1.p2.refs_2_ = bf16[30,64,240]{2,1,0:T(8,128)(2,1)S(1)} collective-permute-done((bf16[30,64,240]{2,1,0:T(8,128)(2,1)}, bf16[30,64,240]{2,1,0:T(8,128)(2,1)S(1)}, u32[]{:S(2)}, u32[]{:S(2)}) %collective-permute-start.1) | collective-permute-done | bytes 921632 | tf_op jit(solution)/shard_map/c1/ppermute | solution.py:256
  20.0 3.2 %collective-permute-start.14 = (bf16[32,32,512]{2,1,0:T(8,128)(2,1)S(1)}, bf16[32,32,512]{2,1,0:T(8,128)(2,1)S(1)}, u32[]{:S(2)}, u32[]{:S(2)}) collective-permute-start(bf16[32,32,512]{2,1,0:T(8,128)(2,1)S(1)} %prepare_b.1.refs_3_.refs_16_), channel_id=1, source_target_pairs={{0,16},{1,17},{2,18},{3,19},{4,20},{5,21},{6,22},{7,23},{8,24},{9,... | collective-permute-start | bytes 3145736 | tf_op jit(solution)/shard_map/bq/ppermute | solution.py:256
  23.2 6.3 %collective-permute-done.2.p3.refs_3_ = bf16[30,64,240]{2,1,0:T(8,128)(2,1)S(1)} collective-permute-done((bf16[30,64,240]{2,1,0:T(8,128)(2,1)}, bf16[30,64,240]{2,1,0:T(8,128)(2,1)S(1)}, u32[]{:S(2)}, u32[]{:S(2)}) %collective-permute-start.2) | collective-permute-done | bytes 921632 | tf_op jit(solution)/shard_map/aq/ppermute | solution.py:256
  29.5 1.5 %collective-permute-start.9 = (bf16[32,32,512]{2,1,0:T(8,128)(2,1)S(1)}, bf16[32,32,512]{2,1,0:T(8,128)(2,1)S(1)}, u32[]{:S(2)}, u32[]{:S(2)}) collective-permute-start(bf16[32,32,512]{2,1,0:T(8,128)(2,1)S(1)} %collective-permute-done.6), channel_id=1, source_target_pairs={{0,32},{1,97},{2,34},{3,99},{4,36},{5,101},{6,38},{7,103},{8,40},{... | collective-permute-start | bytes 3145736 | tf_op jit(solution)/shard_map/d2/ppermute | solution.py:256
  31.0 1.2 %copy-done.1 = bf16[30,240,64]{1,2,0:T(8,128)(2,1)S(1)} copy-done((bf16[30,240,64]{1,2,0:T(8,128)(2,1)S(1)}, bf16[30,240,64]{1,2,0:T(8,128)(2,1)}, u32[]{:S(2)}) %copy-start.1) | copy-done | bytes 921624
  32.2 0.7 copy-done.3
  33.6 3.9 %regroup_a.1.refs_0_.refs_24_ = bf16[32,256,256]{2,1,0:T(8,128)(2,1)S(1)} custom-call(s32[8,8]{1,0:T(8,128)S(1)} %copy-done.4, s32[16,16]{1,0:T(8,128)S(1)} %copy-done.3, bf16[30,64,240]{2,1,0:T(8,128)(2,1)S(1)} %bitcast.9, bf16[30,64,240]{2,1,0:T(8,128)(2,1)S(1)} %collective-permute-done.p1.refs_1_, ...), custom_call_target="tpu_custom_call" | custom-call | flops 1000 | bytes 1000 | tf_op jit(solution)/shard_map/regroup_a/pallas_call | solution.py:111
  37.4 3.1 %collective-permute-start.5 = (bf16[30,64,240]{2,1,0:T(8,128)(2,1)S(1)}, bf16[30,64,240]{2,1,0:T(8,128)(2,1)S(1)}, u32[]{:S(2)}, u32[]{:S(2)}) collective-permute-start(bf16[30,64,240]{2,1,0:T(8,128)(2,1)S(1)} %collective-permute-done.2.p3.refs_3_), channel_id=1, source_target_pairs={{0,1},{1,0},{2,3},{3,2},{4,5},{5,4},{6,7},{7,6},{8,9},{9,8},{10,11... | collective-permute-start | bytes 2764808 | tf_op jit(solution)/shard_map/s_aq/ppermute | solution.py:256
  41.1 1.5 %collective-permute-start.12 = (bf16[32,32,512]{2,1,0:T(8,128)(2,1)S(1)}, bf16[32,32,512]{2,1,0:T(8,128)(2,1)S(1)}, u32[]{:S(2)}, u32[]{:S(2)}) collective-permute-start(bf16[32,32,512]{2,1,0:T(8,128)(2,1)S(1)} %collective-permute-done.7.refs_4_.refs_17_), channel_id=1, source_target_pairs={{0,32},{1,97},{2,34},{3,99},{4,36},{5,101},{6,38},{7,103},{8,40},{... | collective-permute-start | bytes 3145736 | tf_op jit(solution)/shard_map/d5/ppermute | solution.py:256
  42.6 11.8 %collective-permute-done.14.refs_20_ = bf16[32,32,512]{2,1,0:T(8,128)(2,1)S(1)} collective-permute-done((bf16[32,32,512]{2,1,0:T(8,128)(2,1)S(1)}, bf16[32,32,512]{2,1,0:T(8,128)(2,1)S(1)}, u32[]{:S(2)}, u32[]{:S(2)}) %collective-permute-start.14) | collective-permute-done | bytes 1048608 | tf_op jit(solution)/shard_map/bq/ppermute | solution.py:256
  54.4 0.8 collective-permute-start.15
  55.2 1.6 %collective-permute-start.17 = (bf16[32,32,512]{2,1,0:T(8,128)(2,1)S(1)}, bf16[32,32,512]{2,1,0:T(8,128)(2,1)S(1)}, u32[]{:S(2)}, u32[]{:S(2)}) collective-permute-start(bf16[32,32,512]{2,1,0:T(8,128)(2,1)S(1)} %collective-permute-done.14.refs_20_), channel_id=1, source_target_pairs={{0,32},{1,97},{2,34},{3,99},{4,36},{5,101},{6,38},{7,103},{8,40},{... | collective-permute-start | bytes 3145736 | tf_op jit(solution)/shard_map/dq1/ppermute | solution.py:256
  56.7 1.1 %collective-permute-done.8.p3.refs_7_ = bf16[30,64,240]{2,1,0:T(8,128)(2,1)S(1)} collective-permute-done((bf16[30,64,240]{2,1,0:T(8,128)(2,1)S(1)}, bf16[30,64,240]{2,1,0:T(8,128)(2,1)S(1)}, u32[]{:S(2)}, u32[]{:S(2)}) %collective-permute-start.8) | collective-permute-done | bytes 921632 | tf_op jit(solution)/shard_map/cq1/ppermute | solution.py:256
  58.2 1.5 %collective-permute-start.13 = (bf16[30,64,240]{2,1,0:T(8,128)(2,1)S(1)}, bf16[30,64,240]{2,1,0:T(8,128)(2,1)S(1)}, u32[]{:S(2)}, u32[]{:S(2)}) collective-permute-start(bf16[30,64,240]{2,1,0:T(8,128)(2,1)S(1)} %collective-permute-done.5.p2.refs_6_), channel_id=1, source_target_pairs={{0,4},{1,13},{2,6},{3,15},{4,8},{5,1},{6,10},{7,3},{8,12},{9,5},{1... | collective-permute-start | bytes 2764808 | tf_op jit(solution)/shard_map/cq2/ppermute | solution.py:256
  59.7 3.9 %regroup_c2.1.refs_1_.refs_25_ = bf16[32,256,256]{2,1,0:T(8,128)(2,1)S(1)} custom-call(s32[8,8]{1,0:T(8,128)S(1)} %copy-done.4, s32[16,16]{1,0:T(8,128)S(1)} %copy-done.3, bf16[30,64,240]{2,1,0:T(8,128)(2,1)S(1)} %collective-permute-done.3.p0.refs_4_, bf16[30,64,240]{2,1,0:T(8,128)(2,1)S(1)} %collective-permute-done.4.p1.refs_5_, ...), custom_call_target="tpu_custom_call" | custom-call | flops 1000 | bytes 1000 | tf_op jit(solution)/shard_map/regroup_c2/pallas_call | solution.py:111
  64.6 1.2 %collective-permute-start.19 = (bf16[30,64,240]{2,1,0:T(8,128)(2,1)S(1)}, bf16[30,64,240]{2,1,0:T(8,128)(2,1)S(1)}, u32[]{:S(2)}, u32[]{:S(2)}) collective-permute-start(bf16[30,64,240]{2,1,0:T(8,128)(2,1)S(1)} %collective-permute-done.8.p3.refs_7_), channel_id=1, source_target_pairs={{0,4},{1,13},{2,6},{3,15},{4,8},{5,1},{6,10},{7,3},{8,12},{9,5},{1... | collective-permute-start | bytes 2764808 | tf_op jit(solution)/shard_map/cq5/ppermute | solution.py:256
  65.8 5.5 %collective-permute-done.17.refs_21_ = bf16[32,32,512]{2,1,0:T(8,128)(2,1)S(1)} collective-permute-done((bf16[32,32,512]{2,1,0:T(8,128)(2,1)S(1)}, bf16[32,32,512]{2,1,0:T(8,128)(2,1)S(1)}, u32[]{:S(2)}, u32[]{:S(2)}) %collective-permute-start.17) | collective-permute-done | bytes 1048608 | tf_op jit(solution)/shard_map/dq1/ppermute | solution.py:256
  71.3 2.2 %collective-permute-done.13.p2.refs_10_ = bf16[30,64,240]{2,1,0:T(8,128)(2,1)S(1)} collective-permute-done((bf16[30,64,240]{2,1,0:T(8,128)(2,1)S(1)}, bf16[30,64,240]{2,1,0:T(8,128)(2,1)S(1)}, u32[]{:S(2)}, u32[]{:S(2)}) %collective-permute-start.13) | collective-permute-done | bytes 921632 | tf_op jit(solution)/shard_map/cq2/ppermute | solution.py:256
  74.0 1.2 %collective-permute-start.25 = (bf16[32,32,512]{2,1,0:T(8,128)(2,1)S(1)}, bf16[32,32,512]{2,1,0:T(8,128)(2,1)S(1)}, u32[]{:S(2)}, u32[]{:S(2)}) collective-permute-start(bf16[32,32,512]{2,1,0:T(8,128)(2,1)S(1)} %collective-permute-done.17.refs_21_), channel_id=1, source_target_pairs={{0,32},{1,97},{2,34},{3,99},{4,36},{5,101},{6,38},{7,103},{8,40},{... | collective-permute-start | bytes 3145736 | tf_op jit(solution)/shard_map/dq5/ppermute | solution.py:256
  75.2 3.9 %regroup_s_c5.1.refs_2_.refs_26_ = bf16[32,256,256]{2,1,0:T(8,128)(2,1)S(1)} custom-call(s32[8,8]{1,0:T(8,128)S(1)} %copy-done.4, s32[16,16]{1,0:T(8,128)S(1)} %copy-done.3, bf16[30,64,240]{2,1,0:T(8,128)(2,1)S(1)} %collective-permute-done.10.p0.refs_8_, bf16[30,64,240]{2,1,0:T(8,128)(2,1)S(1)} %collective-permute-done.11.p1.refs_9_, ...), custom_call_target="tpu_custom_call" | custom-call | flops 1000 | bytes 1000 | tf_op jit(solution)/shard_map/regroup_s_c5/pallas_call | solution.py:111
  79.1 3.4 %collective-permute-done.23 = bf16[32,32,512]{2,1,0:T(8,128)(2,1)S(1)} collective-permute-done((bf16[32,32,512]{2,1,0:T(8,128)(2,1)S(1)}, bf16[32,32,512]{2,1,0:T(8,128)(2,1)S(1)}, u32[]{:S(2)}, u32[]{:S(2)}) %collective-permute-start.23) | collective-permute-done | bytes 1048608 | tf_op jit(solution)/shard_map/dq2/ppermute | solution.py:256
  82.5 1.5 %collective-permute-done.19.p1.refs_13_ = bf16[30,64,240]{2,1,0:T(8,128)(2,1)S(1)} collective-permute-done((bf16[30,64,240]{2,1,0:T(8,128)(2,1)S(1)}, bf16[30,64,240]{2,1,0:T(8,128)(2,1)S(1)}, u32[]{:S(2)}, u32[]{:S(2)}) %collective-permute-start.19) | collective-permute-done | bytes 921632 | tf_op jit(solution)/shard_map/cq5/ppermute | solution.py:256
  84.5 3.4 %early.1.refs_28_ = f32[768,512]{1,0:T(8,128)S(1)} custom-call(bf16[32,256,256]{2,1,0:T(8,128)(2,1)S(1)} %regroup_a.1.refs_0_.refs_24_, bf16[32,256,256]{2,1,0:T(8,128)(2,1)S(1)} %regroup_c2.1.refs_1_.refs_25_, bf16[32,256,256]{2,1,0:T(8,128)(2,1)S(1)} %regroup_s_c5.1.refs_2_.refs_26_, bf16[32,32,512]{2,1,0:T(8,128)(2,1)S(1)} %prepare_b.1.refs_3_.refs_16_, ...), custom_call_target="tpu_custom_call" | custom-call | flops 1000 | bytes 1000 | tf_op jit(solution)/shard_map/early/pallas_call | solution.py:186
  88.0 3.9 %regroup_s_cq2.1.refs_27_ = bf16[32,256,256]{2,1,0:T(8,128)(2,1)S(1)} custom-call(s32[8,8]{1,0:T(8,128)S(1)} %copy-done.4, s32[16,16]{1,0:T(8,128)S(1)} %copy-done.3, bf16[30,64,240]{2,1,0:T(8,128)(2,1)S(1)} %collective-permute-done.18.p0.refs_12_, bf16[30,64,240]{2,1,0:T(8,128)(2,1)S(1)} %collective-permute-done.19.p1.refs_13_, ...), custom_call_target="tpu_custom_call" | custom-call | flops 1000 | bytes 1000 | tf_op jit(solution)/shard_map/regroup_s_cq2/pallas_call | solution.py:111
  91.9 1.9 %collective-permute-done.25.refs_23_ = bf16[32,32,512]{2,1,0:T(8,128)(2,1)S(1)} collective-permute-done((bf16[32,32,512]{2,1,0:T(8,128)(2,1)S(1)}, bf16[32,32,512]{2,1,0:T(8,128)(2,1)S(1)}, u32[]{:S(2)}, u32[]{:S(2)}) %collective-permute-start.25) | collective-permute-done | bytes 1048608 | tf_op jit(solution)/shard_map/dq5/ppermute | solution.py:256
  93.7 11.1 %last.1 = (bf16[30,64,240]{2,1,0:T(8,128)(2,1)}, bf16[960,480]{1,0:T(8,128)(2,1)}) custom-call(s32[8,8]{1,0:T(8,128)S(1)} %copy-done.4, s32[16,16]{1,0:T(8,128)S(1)} %copy-done.3, bf16[30,64,240]{2,1,0:T(8,128)(2,1)S(1)} %bitcast.10, bf16[30,64,240]{2,1,0:T(8,128)(2,1)S(1)} %collective-permute-done.p1.refs_1_, ...), custom_call_target="tpu_custom_call" | custom-call | flops 12000000000 | bytes 38000000 | tf_op jit(solution)/shard_map/last/pallas_call | solution.py:234
  (39 shorter events, 4.7 us)
Async XLA Ops:
  0.6 1.2 %copy-start = (bf16[30,32,480]{2,1,0:T(8,128)(2,1)S(1)}, bf16[30,32,480]{2,1,0:T(8,128)(2,1)}, u32[]{:S(2)}) copy-start(bf16[30,32,480]{2,1,0:T(8,128)(2,1)} %param.7) | copy-start | bytes 2764804
  1.8 0.7 copy-start.5
  3.0 4.2 %collective-permute-start.6 = (bf16[32,32,512]{2,1,0:T(8,128)(2,1)S(1)}, bf16[32,32,512]{2,1,0:T(8,128)(2,1)S(1)}, u32[]{:S(2)}, u32[]{:S(2)}) collective-permute-start(bf16[32,32,512]{2,1,0:T(8,128)(2,1)S(1)} %prepare_b.1.refs_3_.refs_16_), channel_id=1, source_target_pairs={{0,1},{1,0},{2,3},{3,2},{4,5},{5,4},{6,7},{7,6},{8,9},{9,8},{10,11... | collective-permute-start | bytes 3145736 | tf_op jit(solution)/shard_map/s_b/ppermute | solution.py:256
  3.1 5.6 %collective-permute-start = (bf16[30,64,240]{2,1,0:T(8,128)(2,1)}, bf16[30,64,240]{2,1,0:T(8,128)(2,1)S(1)}, u32[]{:S(2)}, u32[]{:S(2)}) collective-permute-start(bf16[30,64,240]{2,1,0:T(8,128)(2,1)} %bitcast.6), channel_id=1, source_target_pairs={{0,1},{1,0},{2,3},{3,2},{4,5},{5,4},{6,7},{7,6},{8,9},{9,8},{10,11... | collective-permute-start | bytes 2764808 | tf_op jit(solution)/shard_map/s_a/ppermute | solution.py:256
  3.6 16.4 %collective-permute-start.1 = (bf16[30,64,240]{2,1,0:T(8,128)(2,1)}, bf16[30,64,240]{2,1,0:T(8,128)(2,1)S(1)}, u32[]{:S(2)}, u32[]{:S(2)}) collective-permute-start(bf16[30,64,240]{2,1,0:T(8,128)(2,1)} %bitcast.7), channel_id=1, source_target_pairs={{0,4},{1,13},{2,6},{3,15},{4,8},{5,1},{6,10},{7,3},{8,12},{9,5},{1... | collective-permute-start | bytes 2764808 | tf_op jit(solution)/shard_map/c1/ppermute | solution.py:256
  5.6 23.9 %collective-permute-start.2 = (bf16[30,64,240]{2,1,0:T(8,128)(2,1)}, bf16[30,64,240]{2,1,0:T(8,128)(2,1)S(1)}, u32[]{:S(2)}, u32[]{:S(2)}) collective-permute-start(bf16[30,64,240]{2,1,0:T(8,128)(2,1)} %bitcast.8), channel_id=1, source_target_pairs={{0,2},{1,3},{2,0},{3,1},{4,6},{5,7},{6,4},{7,5},{8,10},{9,11},{10,... | collective-permute-start | bytes 2764808 | tf_op jit(solution)/shard_map/aq/ppermute | solution.py:256
  7.2 33.9 %collective-permute-start.7 = (bf16[32,32,512]{2,1,0:T(8,128)(2,1)S(1)}, bf16[32,32,512]{2,1,0:T(8,128)(2,1)S(1)}, u32[]{:S(2)}, u32[]{:S(2)}) collective-permute-start(bf16[32,32,512]{2,1,0:T(8,128)(2,1)S(1)} %prepare_b.1.refs_3_.refs_16_), channel_id=1, source_target_pairs={{0,32},{1,97},{2,34},{3,99},{4,36},{5,101},{6,38},{7,103},{8,40},{... | collective-permute-start | bytes 3145736 | tf_op jit(solution)/shard_map/d1/ppermute | solution.py:256
  8.7 28.8 %collective-permute-start.3 = (bf16[30,64,240]{2,1,0:T(8,128)(2,1)S(1)}, bf16[30,64,240]{2,1,0:T(8,128)(2,1)S(1)}, u32[]{:S(2)}, u32[]{:S(2)}) collective-permute-start(bf16[30,64,240]{2,1,0:T(8,128)(2,1)S(1)} %collective-permute-done.p1.refs_1_), channel_id=1, source_target_pairs={{0,4},{1,13},{2,6},{3,15},{4,8},{5,1},{6,10},{7,3},{8,12},{9,5},{1... | collective-permute-start | bytes 2764808 | tf_op jit(solution)/shard_map/c2/ppermute | solution.py:256
  20.0 21.1 %collective-permute-start.4 = (bf16[30,64,240]{2,1,0:T(8,128)(2,1)S(1)}, bf16[30,64,240]{2,1,0:T(8,128)(2,1)S(1)}, u32[]{:S(2)}, u32[]{:S(2)}) collective-permute-start(bf16[30,64,240]{2,1,0:T(8,128)(2,1)S(1)} %collective-permute-done.1.p2.refs_2_), channel_id=1, source_target_pairs={{0,4},{1,13},{2,6},{3,15},{4,8},{5,1},{6,10},{7,3},{8,12},{9,5},{1... | collective-permute-start | bytes 2764808 | tf_op jit(solution)/shard_map/c5/ppermute | solution.py:256
  20.0 34.4 %collective-permute-start.14 = (bf16[32,32,512]{2,1,0:T(8,128)(2,1)S(1)}, bf16[32,32,512]{2,1,0:T(8,128)(2,1)S(1)}, u32[]{:S(2)}, u32[]{:S(2)}) collective-permute-start(bf16[32,32,512]{2,1,0:T(8,128)(2,1)S(1)} %prepare_b.1.refs_3_.refs_16_), channel_id=1, source_target_pairs={{0,16},{1,17},{2,18},{3,19},{4,20},{5,21},{6,22},{7,23},{8,24},{9,... | collective-permute-start | bytes 3145736 | tf_op jit(solution)/shard_map/bq/ppermute | solution.py:256
  29.5 25.7 %collective-permute-start.9 = (bf16[32,32,512]{2,1,0:T(8,128)(2,1)S(1)}, bf16[32,32,512]{2,1,0:T(8,128)(2,1)S(1)}, u32[]{:S(2)}, u32[]{:S(2)}) collective-permute-start(bf16[32,32,512]{2,1,0:T(8,128)(2,1)S(1)} %collective-permute-done.6), channel_id=1, source_target_pairs={{0,32},{1,97},{2,34},{3,99},{4,36},{5,101},{6,38},{7,103},{8,40},{... | collective-permute-start | bytes 3145736 | tf_op jit(solution)/shard_map/d2/ppermute | solution.py:256
  31.0 1.2 %copy-start.1 = (bf16[30,240,64]{1,2,0:T(8,128)(2,1)S(1)}, bf16[30,240,64]{1,2,0:T(8,128)(2,1)}, u32[]{:S(2)}) copy-start(bf16[30,240,64]{1,2,0:T(8,128)(2,1)} %param.5) | copy-start | bytes 2764804
  32.2 0.7 copy-start.3
  32.9 0.7 copy-start.4
  37.4 17.7 %collective-permute-start.5 = (bf16[30,64,240]{2,1,0:T(8,128)(2,1)S(1)}, bf16[30,64,240]{2,1,0:T(8,128)(2,1)S(1)}, u32[]{:S(2)}, u32[]{:S(2)}) collective-permute-start(bf16[30,64,240]{2,1,0:T(8,128)(2,1)S(1)} %collective-permute-done.2.p3.refs_3_), channel_id=1, source_target_pairs={{0,1},{1,0},{2,3},{3,2},{4,5},{5,4},{6,7},{7,6},{8,9},{9,8},{10,11... | collective-permute-start | bytes 2764808 | tf_op jit(solution)/shard_map/s_aq/ppermute | solution.py:256
  41.1 17.1 %collective-permute-start.12 = (bf16[32,32,512]{2,1,0:T(8,128)(2,1)S(1)}, bf16[32,32,512]{2,1,0:T(8,128)(2,1)S(1)}, u32[]{:S(2)}, u32[]{:S(2)}) collective-permute-start(bf16[32,32,512]{2,1,0:T(8,128)(2,1)S(1)} %collective-permute-done.7.refs_4_.refs_17_), channel_id=1, source_target_pairs={{0,32},{1,97},{2,34},{3,99},{4,36},{5,101},{6,38},{7,103},{8,40},{... | collective-permute-start | bytes 3145736 | tf_op jit(solution)/shard_map/d5/ppermute | solution.py:256
  42.6 15.3 %collective-permute-start.8 = (bf16[30,64,240]{2,1,0:T(8,128)(2,1)S(1)}, bf16[30,64,240]{2,1,0:T(8,128)(2,1)S(1)}, u32[]{:S(2)}, u32[]{:S(2)}) collective-permute-start(bf16[30,64,240]{2,1,0:T(8,128)(2,1)S(1)} %collective-permute-done.2.p3.refs_3_), channel_id=1, source_target_pairs={{0,4},{1,13},{2,6},{3,15},{4,8},{5,1},{6,10},{7,3},{8,12},{9,5},{1... | collective-permute-start | bytes 2764808 | tf_op jit(solution)/shard_map/cq1/ppermute | solution.py:256
  54.4 9.1 %collective-permute-start.15 = (bf16[32,32,512]{2,1,0:T(8,128)(2,1)S(1)}, bf16[32,32,512]{2,1,0:T(8,128)(2,1)S(1)}, u32[]{:S(2)}, u32[]{:S(2)}) collective-permute-start(bf16[32,32,512]{2,1,0:T(8,128)(2,1)S(1)} %collective-permute-done.14.refs_20_), channel_id=1, source_target_pairs={{0,1},{1,0},{2,3},{3,2},{4,5},{5,4},{6,7},{7,6},{8,9},{9,8},{10,11... | collective-permute-start | bytes 3145736 | tf_op jit(solution)/shard_map/s_bq/ppermute | solution.py:256
  55.2 8.4 %collective-permute-start.10 = (bf16[30,64,240]{2,1,0:T(8,128)(2,1)S(1)}, bf16[30,64,240]{2,1,0:T(8,128)(2,1)S(1)}, u32[]{:S(2)}, u32[]{:S(2)}) collective-permute-start(bf16[30,64,240]{2,1,0:T(8,128)(2,1)S(1)} %collective-permute-done.4.p1.refs_5_), channel_id=1, source_target_pairs={{0,1},{1,0},{2,3},{3,2},{4,5},{5,4},{6,7},{7,6},{8,9},{9,8},{10,11... | collective-permute-start | bytes 2764808 | tf_op jit(solution)/shard_map/s_c5/ppermute | solution.py:256
  55.2 16.1 %collective-permute-start.17 = (bf16[32,32,512]{2,1,0:T(8,128)(2,1)S(1)}, bf16[32,32,512]{2,1,0:T(8,128)(2,1)S(1)}, u32[]{:S(2)}, u32[]{:S(2)}) collective-permute-start(bf16[32,32,512]{2,1,0:T(8,128)(2,1)S(1)} %collective-permute-done.14.refs_20_), channel_id=1, source_target_pairs={{0,32},{1,97},{2,34},{3,99},{4,36},{5,101},{6,38},{7,103},{8,40},{... | collective-permute-start | bytes 3145736 | tf_op jit(solution)/shard_map/dq1/ppermute | solution.py:256
  57.9 6.7 %collective-permute-start.11 = (bf16[30,64,240]{2,1,0:T(8,128)(2,1)S(1)}, bf16[30,64,240]{2,1,0:T(8,128)(2,1)S(1)}, u32[]{:S(2)}, u32[]{:S(2)}) collective-permute-start(bf16[30,64,240]{2,1,0:T(8,128)(2,1)S(1)} %collective-permute-done.8.p3.refs_7_), channel_id=1, source_target_pairs={{0,1},{1,0},{2,3},{3,2},{4,5},{5,4},{6,7},{7,6},{8,9},{9,8},{10,11... | collective-permute-start | bytes 2764808 | tf_op jit(solution)/shard_map/s_cq1/ppermute | solution.py:256
  58.2 15.3 %collective-permute-start.13 = (bf16[30,64,240]{2,1,0:T(8,128)(2,1)S(1)}, bf16[30,64,240]{2,1,0:T(8,128)(2,1)S(1)}, u32[]{:S(2)}, u32[]{:S(2)}) collective-permute-start(bf16[30,64,240]{2,1,0:T(8,128)(2,1)S(1)} %collective-permute-done.5.p2.refs_6_), channel_id=1, source_target_pairs={{0,4},{1,13},{2,6},{3,15},{4,8},{5,1},{6,10},{7,3},{8,12},{9,5},{1... | collective-permute-start | bytes 2764808 | tf_op jit(solution)/shard_map/cq2/ppermute | solution.py:256
  63.6 18.9 %collective-permute-start.23 = (bf16[32,32,512]{2,1,0:T(8,128)(2,1)S(1)}, bf16[32,32,512]{2,1,0:T(8,128)(2,1)S(1)}, u32[]{:S(2)}, u32[]{:S(2)}) collective-permute-start(bf16[32,32,512]{2,1,0:T(8,128)(2,1)S(1)} %collective-permute-done.15), channel_id=1, source_target_pairs={{0,32},{1,97},{2,34},{3,99},{4,36},{5,101},{6,38},{7,103},{8,40},{... | collective-permute-start | bytes 3145736 | tf_op jit(solution)/shard_map/dq2/ppermute | solution.py:256
  63.9 9.6 %collective-permute-start.16 = (bf16[30,64,240]{2,1,0:T(8,128)(2,1)S(1)}, bf16[30,64,240]{2,1,0:T(8,128)(2,1)S(1)}, u32[]{:S(2)}, u32[]{:S(2)}) collective-permute-start(bf16[30,64,240]{2,1,0:T(8,128)(2,1)S(1)} %collective-permute-done.1.p2.refs_2_), channel_id=1, source_target_pairs={{0,1},{1,0},{2,3},{3,2},{4,5},{5,4},{6,7},{7,6},{8,9},{9,8},{10,11... | collective-permute-start | bytes 2764808 | tf_op jit(solution)/shard_map/s_c1/ppermute | solution.py:256
  64.6 19.5 %collective-permute-start.19 = (bf16[30,64,240]{2,1,0:T(8,128)(2,1)S(1)}, bf16[30,64,240]{2,1,0:T(8,128)(2,1)S(1)}, u32[]{:S(2)}, u32[]{:S(2)}) collective-permute-start(bf16[30,64,240]{2,1,0:T(8,128)(2,1)S(1)} %collective-permute-done.8.p3.refs_7_), channel_id=1, source_target_pairs={{0,4},{1,13},{2,6},{3,15},{4,8},{5,1},{6,10},{7,3},{8,12},{9,5},{1... | collective-permute-start | bytes 2764808 | tf_op jit(solution)/shard_map/cq5/ppermute | solution.py:256
  73.5 10.5 %collective-permute-start.18 = (bf16[30,64,240]{2,1,0:T(8,128)(2,1)S(1)}, bf16[30,64,240]{2,1,0:T(8,128)(2,1)S(1)}, u32[]{:S(2)}, u32[]{:S(2)}) collective-permute-start(bf16[30,64,240]{2,1,0:T(8,128)(2,1)S(1)} %collective-permute-done.13.p2.refs_10_), channel_id=1, source_target_pairs={{0,1},{1,0},{2,3},{3,2},{4,5},{5,4},{6,7},{7,6},{8,9},{9,8},{10,11... | collective-permute-start | bytes 2764808 | tf_op jit(solution)/shard_map/s_cq2/ppermute | solution.py:256
  73.5 11.0 %collective-permute-start.22 = (bf16[32,32,512]{2,1,0:T(8,128)(2,1)S(1)}, bf16[32,32,512]{2,1,0:T(8,128)(2,1)S(1)}, u32[]{:S(2)}, u32[]{:S(2)}) collective-permute-start(bf16[32,32,512]{2,1,0:T(8,128)(2,1)S(1)} %collective-permute-done.9), channel_id=1, source_target_pairs={{0,1},{1,0},{2,3},{3,2},{4,5},{5,4},{6,7},{7,6},{8,9},{9,8},{10,11... | collective-permute-start | bytes 3145736 | tf_op jit(solution)/shard_map/s_d2/ppermute | solution.py:256
  74.0 19.7 %collective-permute-start.25 = (bf16[32,32,512]{2,1,0:T(8,128)(2,1)S(1)}, bf16[32,32,512]{2,1,0:T(8,128)(2,1)S(1)}, u32[]{:S(2)}, u32[]{:S(2)}) collective-permute-start(bf16[32,32,512]{2,1,0:T(8,128)(2,1)S(1)} %collective-permute-done.17.refs_21_), channel_id=1, source_target_pairs={{0,32},{1,97},{2,34},{3,99},{4,36},{5,101},{6,38},{7,103},{8,40},{... | collective-permute-start | bytes 3145736 | tf_op jit(solution)/shard_map/dq5/ppermute | solution.py:256
  82.5 11.2 %collective-permute-start.24 = (bf16[32,32,512]{2,1,0:T(8,128)(2,1)S(1)}, bf16[32,32,512]{2,1,0:T(8,128)(2,1)S(1)}, u32[]{:S(2)}, u32[]{:S(2)}) collective-permute-start(bf16[32,32,512]{2,1,0:T(8,128)(2,1)S(1)} %collective-permute-done.23), channel_id=1, source_target_pairs={{0,1},{1,0},{2,3},{3,2},{4,5},{5,4},{6,7},{7,6},{8,9},{9,8},{10,11... | collective-permute-start | bytes 3145736 | tf_op jit(solution)/shard_map/s_dq2/ppermute | solution.py:256
  84.0 3.9 %collective-permute-start.21 = (bf16[30,64,240]{2,1,0:T(8,128)(2,1)S(1)}, bf16[30,64,240]{2,1,0:T(8,128)(2,1)S(1)}, u32[]{:S(2)}, u32[]{:S(2)}) collective-permute-start(bf16[30,64,240]{2,1,0:T(8,128)(2,1)S(1)} %collective-permute-done.3.p0.refs_4_), channel_id=1, source_target_pairs={{0,1},{1,0},{2,3},{3,2},{4,5},{5,4},{6,7},{7,6},{8,9},{9,8},{10,11... | collective-permute-start | bytes 2764808 | tf_op jit(solution)/shard_map/s_c2/ppermute | solution.py:256
  84.0 4.0 %collective-permute-start.20 = (bf16[30,64,240]{2,1,0:T(8,128)(2,1)S(1)}, bf16[30,64,240]{2,1,0:T(8,128)(2,1)S(1)}, u32[]{:S(2)}, u32[]{:S(2)}) collective-permute-start(bf16[30,64,240]{2,1,0:T(8,128)(2,1)S(1)} %collective-permute-done.19.p1.refs_13_), channel_id=1, source_target_pairs={{0,1},{1,0},{2,3},{3,2},{4,5},{5,4},{6,7},{7,6},{8,9},{9,8},{10,11... | collective-permute-start | bytes 2764808 | tf_op jit(solution)/shard_map/s_cq5/ppermute | solution.py:256
  87.9 5.8 %copy-start.2 = (bf16[30,240,64]{1,2,0:T(8,128)(2,1)S(1)}, bf16[30,240,64]{1,2,0:T(8,128)(2,1)}, u32[]{:S(2)}) copy-start(bf16[30,240,64]{1,2,0:T(8,128)(2,1)} %param.5) | copy-start | bytes 2764804
